TPU v7x, 32 devices: a whole 2x2x4 slice. The times are simulated.
32 devices in a mesh: row: 4 (over z), col: 8 (over y, x, core).
Axes of the slice: x: 2, y: 2, z: 4, core: 2. Of those that a mesh axis runs over, the one named last changes fastest.
Arguments:
- panel: float32 [4, 1536, 1, 8, 1536], P(None, 'row', None, 'col'), may hold values from -1 to 1, as said below
- inverse_blocks: float32 [4, 1536, 1536], P(None, 'row'), may hold values from -1 to 2, as said below
- right_side: float32 [48, 1, 8, 1536], P(None, None, 'col'), may hold values from -6 to 6
Outputs:
- solved: float32 [48, 4, 1536], P(None, None, 'row')
- updated: float32 [48, 1, 8, 1536], P(None, None, 'col', 'row')
Inputs may be any that keep to these rules, and one draw needn't show every extreme that they name: panel is zero where the row index is below the column index as defined in its meaning (the factor is lower triangular). `inverse_blocks`: each inverse block is lower triangular with a positive diagonal.
All inputs are finite; a program needn't handle non-finite values.
Results may differ from a plain program's by a relative error of at most 0.0001.
Values sent between devices are 32-bit elements; how exact they have to be, the bound alone decides.
No kernel may reach another device: no remote copies, remote signals or barrier semaphores. Data moves between devices by JAX's collectives and lax.ppermute only.
A program may use at most 64 MiB of HBM per device.

v0:
```python
import jax
import jax.numpy as jnp
from jax import lax
from jax.sharding import PartitionSpec as P


def broadcast(value, axis, source):
    kept = jnp.where(lax.axis_index(axis) == source, value, 0).astype(value.dtype)
    return lax.psum(kept, axis)


def body(panel, inverse_blocks, right_side):
    steps = panel.shape[0]
    row_index = lax.axis_index("row")
    heads = right_side[:, 0, 0, :]
    count_rhs = right_side.shape[0]
    count_rowblk = right_side.shape[1]
    block_len = right_side.shape[3]
    accum = jnp.zeros((count_rhs, count_rowblk, block_len), jnp.float32)
    solved_list = []
    for step in range(steps):
        partial_value = accum[:, 0, :]
        residue = heads - lax.psum(partial_value, "row")
        own_piece = jnp.dot(
            residue,
            inverse_blocks[step].T,
            precision=lax.Precision.HIGHEST,
            preferred_element_type=jnp.float32,
        )
        piece = broadcast(own_piece, "col", step)
        solved_list.append(piece)
        columns = panel[step, :, :, 0, :]
        accum = accum + jnp.einsum("rc,cji->rji", piece, columns, precision=lax.Precision.HIGHEST)
    totals = lax.psum_scatter(accum, "row", scatter_dimension=2, tiled=True)
    slice_len = totals.shape[2]
    mine = lax.dynamic_slice_in_dim(right_side, row_index * slice_len, slice_len, 3)[:, :, 0, :]
    updated = (mine - totals)[:, :, None, :]
    solved = jnp.stack(solved_list, axis=1)
    return (solved, updated)


def solution(mesh):
    placed = (P(None, "row", None, "col", None), P(None, "row", None), P(None, None, "col", None))
    return jax.shard_map(
        body,
        mesh=mesh,
        in_specs=placed,
        out_specs=(P(None, None, "row"), P(None, None, "col", "row")),
        check_vma=False,
    )
```

profile of v0, /device:TPU:0, one launch (start us, length us, event | category | flops | bytes accessed | tf_op | source)
XLA Modules:
  0.0 383.5 jit_solution(6443274586691453065)
XLA Ops:
  7.2 4.7 %fusion.36 = f32[48,384]{1,0:T(8,128)} fusion(f32[4,384,1536]{2,1,0:T(8,128)} %param.4, f32[48,1,1,1536]{3,2,1,0:T(1,128)} %param.5, pred[]{:T(512)S(6)} %eq.12), kind=kOutput, calls=%fused_computation.28 | convolution fusion | flops 339757056 | bytes 2727937 | tf_op jit(solution)/shard_map/dot_general | solution.py:24
  11.9 0.0 all-reduce.10.cloned.1.call-start
  12.0 10.5 %fusion.54 = (f32[1,384,1,1,1536]{4,3,2,1,0:T(1,128)S(1)}, f32[1,384,1,1,1536]{4,3,2,1,0:T(1,128)}, f32[1,384,1,1,1536]{4,3,2,1,0:T(1,128)}, f32[1,384,1,1,1536]{4,3,2,1,0:T(1,128)}) fusion(f32[4,384,1,1,1536]{4,3,2,1,0:T(1,128)} %param.3), kind=kLoop, calls=%fused_computation.44 | loop fusion | bytes 18874368 | tf_op jit(solution)/shard_map/slice | solution.py:32
  22.4 42.0 %all-reduce.8.cloned.1.call-done = f32[48,384]{1,0:T(8,128)} async-done(((f32[48,384]{1,0:T(8,128)}), f32[48,384]{1,0:T(8,128)}) %all-reduce.8.cloned.1.call-update) | async-done | bytes 73744 | tf_op jit(solution)/shard_map/psum | solution.py:9
  64.4 4.0 %fusion.9 = f32[48,1536]{1,0:T(8,128)} fusion(f32[48,384]{1,0:T(8,128)} %all-reduce.8.cloned.1.call-done, f32[1,384,1,1,1536]{4,3,2,1,0:T(1,128)} %get-tuple-element.6), kind=kOutput, calls=%fused_computation.9 | convolution fusion | flops 339738624 | bytes 2727936 | tf_op jit(solution)/shard_map/rc,cji->rji/dot_general | solution.py:33
  68.4 0.0 all-reduce.12.cloned.1.call-start
  68.4 37.2 %all-reduce.10.cloned.1.call-done = f32[48,1536]{1,0:T(8,128)} async-done(((f32[48,1536]{1,0:T(8,128)}), f32[48,1536]{1,0:T(8,128)}) %all-reduce.10.cloned.1.call-update) | async-done | bytes 294928 | tf_op jit(solution)/shard_map/psum | solution.py:23
  105.6 4.7 %fusion.39 = f32[48,384]{1,0:T(8,128)} fusion(f32[4,384,1536]{2,1,0:T(8,128)} %param.4, f32[48,1536]{1,0:T(8,128)} %all-reduce.10.cloned.1.call-done, f32[48,1,1,1536]{3,2,1,0:T(1,128)S(1)} %copy-done, pred[]{:T(512)S(6)} %eq.13), kind=kOutput, calls=%fused_computation.29 | convolution fusion | flops 339830784 | bytes 3022849 | tf_op jit(solution)/shard_map/dot_general | solution.py:24
  110.3 0.0 all-reduce.14.cloned.1.call-start
  110.3 49.4 %all-reduce.12.cloned.1.call-done = f32[48,384]{1,0:T(8,128)} async-done(((f32[48,384]{1,0:T(8,128)}), f32[48,384]{1,0:T(8,128)}) %all-reduce.12.cloned.1.call-update) | async-done | bytes 73744 | tf_op jit(solution)/shard_map/psum | solution.py:9
  159.8 4.0 %fusion.24 = f32[48,1536]{1,0:T(8,128)} fusion(f32[48,1536]{1,0:T(8,128)S(1)} %copy-done.3, f32[48,384]{1,0:T(8,128)} %all-reduce.12.cloned.1.call-done, f32[1,384,1,1,1536]{4,3,2,1,0:T(1,128)} %get-tuple-element.5), kind=kOutput, calls=%fused_computation.24 | convolution fusion | flops 339812352 | bytes 3022848 | tf_op jit(solution)/shard_map/rc,cji->rji/dot_general | solution.py:33
  163.8 37.2 %all-reduce.14.cloned.1.call-done = f32[48,1536]{1,0:T(8,128)} async-done(((f32[48,1536]{1,0:T(8,128)}), f32[48,1536]{1,0:T(8,128)}) %all-reduce.14.cloned.1.call-update) | async-done | bytes 294928 | tf_op jit(solution)/shard_map/psum | solution.py:23
  201.0 4.7 %fusion.42 = f32[48,384]{1,0:T(8,128)} fusion(f32[4,384,1536]{2,1,0:T(8,128)} %param.4, f32[48,1536]{1,0:T(8,128)} %all-reduce.14.cloned.1.call-done, f32[48,1,1,1536]{3,2,1,0:T(1,128)S(1)} %copy-done, pred[]{:T(512)S(6)} %eq.14), kind=kOutput, calls=%fused_computation.30 | convolution fusion | flops 339830784 | bytes 3022849 | tf_op jit(solution)/shard_map/dot_general | solution.py:24
  205.7 49.4 %all-reduce.16.cloned.1.call-done = f32[48,384]{1,0:T(8,128)} async-done(((f32[48,384]{1,0:T(8,128)}), f32[48,384]{1,0:T(8,128)}) %all-reduce.16.cloned.1.call-update) | async-done | bytes 73744 | tf_op jit(solution)/shard_map/psum | solution.py:9
  255.2 4.0 %fusion.27 = f32[48,1536]{1,0:T(8,128)} fusion(f32[48,1536]{1,0:T(8,128)S(1)} %copy-done.2, f32[48,384]{1,0:T(8,128)} %all-reduce.16.cloned.1.call-done, f32[1,384,1,1,1536]{4,3,2,1,0:T(1,128)} %get-tuple-element.7), kind=kOutput, calls=%fused_computation.25 | convolution fusion | flops 339812352 | bytes 3022848 | tf_op jit(solution)/shard_map/rc,cji->rji/dot_general | solution.py:33
  259.2 0.2 all-reduce.20.cloned.1.call-start
  259.4 36.9 %all-reduce.18.cloned.1.call-done = f32[48,1536]{1,0:T(8,128)} async-done(((f32[48,1536]{1,0:T(8,128)}), f32[48,1536]{1,0:T(8,128)}) %all-reduce.18.cloned.1.call-update) | async-done | bytes 294928 | tf_op jit(solution)/shard_map/psum | solution.py:23
  296.3 4.7 %fusion.45 = f32[48,384]{1,0:T(8,128)} fusion(f32[4,384,1536]{2,1,0:T(8,128)} %param.4, f32[48,1536]{1,0:T(8,128)} %all-reduce.18.cloned.1.call-done, f32[48,1,1,1536]{3,2,1,0:T(1,128)S(1)} %copy-done, pred[]{:T(512)S(6)} %eq.15), kind=kOutput, calls=%fused_computation.31 | convolution fusion | flops 339830784 | bytes 3022849 | tf_op jit(solution)/shard_map/dot_general | solution.py:24
  301.1 49.5 %all-reduce.20.cloned.1.call-done = f32[48,384]{1,0:T(8,128)} async-done(((f32[48,384]{1,0:T(8,128)}), f32[48,384]{1,0:T(8,128)}) %all-reduce.20.cloned.1.call-update) | async-done | bytes 73744 | tf_op jit(solution)/shard_map/psum | solution.py:9
  350.6 3.2 fusion.33
  353.9 0.8 copy.5
  354.8 20.3 %reduce-scatter.2.cloned.1.call-done = f32[48,1,384]{2,0,1:T(8,128)} async-done(((f32[48,1,1536]{2,0,1:T(8,128)}), f32[48,1,384]{2,0,1:T(8,128)}) %reduce-scatter.2.cloned.1.call-update) | async-done | bytes 73744 | tf_op jit(solution)/shard_map/reduce_scatter | solution.py:34
  375.1 0.9 fusion.53
  376.0 0.7 copy.6
  (30 shorter events, 0.4 us)
Async XLA Ops:
  7.2 57.2 %all-reduce.8.cloned.1.call-start = ((), (), s32[]{:S(2)}) async-start(), calls=%async_computation.1 | async-start | bytes 147456 | tf_op jit(solution)/shard_map/psum | solution.py:9
  11.9 93.7 %all-reduce.10.cloned.1.call-start = ((), (), s32[]{:S(2)}) async-start(), calls=%async_computation.2 | async-start | bytes 589824 | tf_op jit(solution)/shard_map/psum | solution.py:23
  22.4 83.2 %copy-start = (f32[48,1,1,1536]{3,2,1,0:T(1,128)S(1)}, f32[48,1,1,1536]{3,2,1,0:T(1,128)}, u32[]{:S(2)}) copy-start(f32[48,1,1,1536]{3,2,1,0:T(1,128)} %param.5) | copy-start | bytes 884740
  68.3 91.4 %copy-start.3 = (f32[48,1536]{1,0:T(8,128)S(1)}, f32[48,1536]{1,0:T(8,128)}, u32[]{:S(2)}) copy-start(f32[48,1536]{1,0:T(8,128)} %fusion.9) | copy-start | bytes 884740
  68.4 91.4 %all-reduce.12.cloned.1.call-start = ((), (), s32[]{:S(2)}) async-start(), calls=%async_computation.3 | async-start | bytes 147456 | tf_op jit(solution)/shard_map/psum | solution.py:9
  110.3 90.7 %all-reduce.14.cloned.1.call-start = ((), (), s32[]{:S(2)}) async-start(), calls=%async_computation.4 | async-start | bytes 589824 | tf_op jit(solution)/shard_map/psum | solution.py:23
  163.7 91.4 %copy-start.2 = (f32[48,1536]{1,0:T(8,128)S(1)}, f32[48,1536]{1,0:T(8,128)}, u32[]{:S(2)}) copy-start(f32[48,1536]{1,0:T(8,128)} %fusion.24) | copy-start | bytes 884740
  163.8 91.4 %all-reduce.16.cloned.1.call-start = ((), (), s32[]{:S(2)}) async-start(), calls=%async_computation.5 | async-start | bytes 147456 | tf_op jit(solution)/shard_map/psum | solution.py:9
  205.7 90.7 %all-reduce.18.cloned.1.call-start = ((), (), s32[]{:S(2)}) async-start(), calls=%async_computation.6 | async-start | bytes 589824 | tf_op jit(solution)/shard_map/psum | solution.py:23
  259.1 91.4 %copy-start.1 = (f32[48,1536]{1,0:T(8,128)S(1)}, f32[48,1536]{1,0:T(8,128)}, u32[]{:S(2)}) copy-start(f32[48,1536]{1,0:T(8,128)} %fusion.27) | copy-start | bytes 884740
  259.2 91.4 %all-reduce.20.cloned.1.call-start = ((), (), s32[]{:S(2)}) async-start(), calls=%async_computation.7 | async-start | bytes 147456 | tf_op jit(solution)/shard_map/psum | solution.py:9
  301.0 52.9 %copy-start.4 = (f32[48,384]{1,0:T(8,128)S(1)}, f32[48,384]{1,0:T(8,128)}, u32[]{:S(2)}) copy-start(f32[48,384]{1,0:T(8,128)} %all-reduce.8.cloned.1.call-done) | copy-start | bytes 221188
  301.0 52.9 %copy-start.5 = (f32[48,384]{1,0:T(8,128)S(1)}, f32[48,384]{1,0:T(8,128)}, u32[]{:S(2)}) copy-start(f32[48,384]{1,0:T(8,128)} %all-reduce.12.cloned.1.call-done) | copy-start | bytes 221188
  301.0 52.9 %copy-start.6 = (f32[48,384]{1,0:T(8,128)S(1)}, f32[48,384]{1,0:T(8,128)}, u32[]{:S(2)}) copy-start(f32[48,384]{1,0:T(8,128)} %all-reduce.16.cloned.1.call-done) | copy-start | bytes 221188
  301.0 74.0 %reduce-scatter.2.cloned.1.call-start = ((), (), s32[]{:S(2)}) async-start(), calls=%async_computation.8 | async-start | bytes 368640 | tf_op jit(solution)/shard_map/reduce_scatter | solution.py:34
  350.6 3.3 copy-start.7
Sparse Core Ops, SparseCore 0:
  12.0 52.3 all-reduce.7
  68.5 37.0 all-reduce.9
  110.4 49.3 all-reduce.11
  163.9 37.0 all-reduce.13
  205.8 49.3 all-reduce.15
  259.3 37.0 all-reduce.17
  301.1 49.3 all-reduce.19
  353.9 21.0 reduce-scatter.1
where the time goes:
time: 384 us
  waiting for transfers between devices  322 us (84%)
  matrix products  33.7 us (9%)
  between operations  14.2 us (4%)
  local copies, waits for them, and re-layouts  12.1 us (3%)
    psum x4, waiting for transfers between devices, broadcast(): return lax.psum(kept, axis)  190 us
    psum x3, waiting for transfers between devices, body(): residue = heads - lax.psum(partial_value, 'row')  111 us
    reduce_scatter x1, waiting for transfers between devices, body(): totals = lax.psum_scatter(accum, 'row', scatter_dimension=2, tiled=True)  20.3 us
    dot_general x4, matrix products, body(): jnp.dot(residue, inverse_blocks[step].T, precision=lax.Precision.HIGHEST,...  18.6 us
    dot_general x4, matrix products, body(): jnp.einsum('rc,cji->rji', piece, columns, precision=lax.Precision.HIGHEST)  15.1 us
    slice x1, local copies, waits for them, and re-layouts, body(): columns = panel[step, :, :, 0, :]  10.5 us
  transfers between devices with their start and end apart: 8, of which 8 were waited for; matrix products, arithmetic and copies ran while one was open for 3% of the time, Pallas kernels for 0%

commit v1 on v0

v1 whole, which is shorter than its diff:
```python
import functools

import jax
import jax.numpy as jnp
from jax import lax
from jax.experimental import pallas as pl
from jax.experimental.pallas import tpu as pltpu
from jax.sharding import PartitionSpec as P

LANES = 128
F32 = jnp.float32
BF16 = jnp.bfloat16
VMEM = pl.BlockSpec(memory_space=pltpu.VMEM)
SMEM = pl.BlockSpec(memory_space=pltpu.SMEM)
PARAMS = pltpu.CompilerParams(vmem_limit_bytes=16 * 2**20)


def split(value):
    head = value.astype(BF16)
    return head, (value - head.astype(F32)).astype(BF16)


def product(left, right, dims):
    count = left.shape[0]
    left_head, left_tail = split(left)
    right_head, right_tail = split(right)
    dot = functools.partial(lax.dot_general, dimension_numbers=(dims, ((), ())), preferred_element_type=F32)
    stacked = dot(jnp.concatenate([left_head, left_tail], axis=0), right_head)
    return stacked[:count] + stacked[count:] + dot(left_head, right_tail)


def tile_columns(block_ref, index, width, rows, stride):
    first = index * width // LANES
    parts = [block_ref[pl.ds(first + at, rows, stride=stride), :] for at in range(width // LANES)]
    return parts[0] if len(parts) == 1 else jnp.concatenate(parts, axis=1)


def subtract_product(solved, base_ref, block_ref, out_ref):
    rows = solved.shape[1]
    length = base_ref.shape[1]
    stride = length // LANES
    width = 2 * LANES
    for index in range(length // width):
        at = slice(index * width, (index + 1) * width)
        tile = tile_columns(block_ref, index, width, rows, stride)
        out_ref[:, at] = base_ref[:, at] - product(solved, tile, ((1,), (0,)))


def update_kernel(solved_ref, base_ref, block_ref, out_ref):
    subtract_product(solved_ref[...], base_ref, block_ref, out_ref)


def update_either_kernel(own_ref, solved_ref, base_ref, block_ref, other_ref, out_ref):
    own = own_ref[0]

    @pl.when(own == 1)
    def _():
        subtract_product(solved_ref[...], base_ref, block_ref, out_ref)

    @pl.when(own != 1)
    def _():
        subtract_product(solved_ref[...], base_ref, other_ref, out_ref)


def apply_kernel(value_ref, inverse_ref, out_ref):
    out_ref[...] = product(value_ref[...], inverse_ref[0], ((1,), (1,)))


def gather_apply_kernel(fulls, flag_ref, own_ref, *refs):
    even = flag_ref[0]
    inverse_ref, out_ref = refs[-2:]
    half_refs = refs[fulls:-2]
    value = jnp.where(even == 1, own_ref[...], 0.0)
    for ref in refs[:fulls]:
        value = value + ref[...]
    if half_refs:
        half = half_refs[0][...]
        zero = jnp.zeros_like(half)
        value = value + jnp.concatenate([jnp.where(even == 1, half, zero), jnp.where(even == 1, zero, half)], axis=1)
    out_ref[...] = product(value, inverse_ref[0], ((1,), (1,)))


def cost(count, rows, columns):
    return pl.CostEstimate(flops=6 * count * rows * columns, bytes_accessed=4 * (rows * columns + count * (rows + columns)), transcendentals=0)


def update(solved, base, block):
    count, rows = solved.shape
    return pl.pallas_call(
        update_kernel,
        out_shape=jax.ShapeDtypeStruct(base.shape, F32),
        in_specs=[VMEM] * 3,
        out_specs=VMEM,
        compiler_params=PARAMS,
        cost_estimate=cost(count, rows, base.shape[1]),
    )(solved, base, block)


def update_either(own, solved, base, block, other):
    count, rows = solved.shape
    return pl.pallas_call(
        update_either_kernel,
        out_shape=jax.ShapeDtypeStruct(base.shape, F32),
        in_specs=[SMEM] + [VMEM] * 4,
        out_specs=VMEM,
        compiler_params=PARAMS,
        cost_estimate=cost(count, rows, base.shape[1]),
    )(own, solved, base, block, other)


def inverse_spec(inverse_blocks, step):
    return pl.BlockSpec((1,) + inverse_blocks.shape[1:], lambda *_: (step, 0, 0))


def whole(array):
    return pl.BlockSpec(array.shape, lambda *_: (0,) * array.ndim)


def apply(value, inverse_blocks, step):
    count, length = value.shape
    rows = inverse_blocks.shape[1]
    return pl.pallas_call(
        apply_kernel,
        grid=(1,),
        out_shape=jax.ShapeDtypeStruct((count, rows), F32),
        in_specs=[whole(value), inverse_spec(inverse_blocks, step)],
        out_specs=pl.BlockSpec((count, rows), lambda *_: (0, 0)),
        compiler_params=PARAMS,
        cost_estimate=cost(count, rows, length),
    )(value, inverse_blocks)


def gather_apply(even, own, fulls, halves, inverse_blocks, step):
    count, length = own.shape
    rows = inverse_blocks.shape[1]
    arrays = [own] + fulls + halves
    return pl.pallas_call(
        functools.partial(gather_apply_kernel, len(fulls)),
        grid=(1,),
        out_shape=jax.ShapeDtypeStruct((count, rows), F32),
        in_specs=[SMEM] + [whole(array) for array in arrays] + [inverse_spec(inverse_blocks, step)],
        out_specs=pl.BlockSpec((count, rows), lambda *_: (0, 0)),
        compiler_params=PARAMS,
        cost_estimate=cost(count, rows, length),
    )(even, *arrays, inverse_blocks)


def body(rows, cols, panel, inverse_blocks, right_side):
    steps, depth, _, _, length = panel.shape
    count = right_side.shape[0]
    row, col = lax.axis_index("row"), lax.axis_index("col")
    parity = lax.rem(col, 2)
    is_even = parity == 0
    even = jnp.where(is_even, 1, 0).astype(jnp.int32).reshape(1)
    odd = 1 - even

    def move(value, target):
        pairs = []
        for z in range(rows):
            for q in range(cols):
                to_z, to_q = target(z, q)
                pairs.append((z * cols + q, to_z * cols + to_q))
        return lax.ppermute(value, ("row", "col"), pairs)

    def swap_core(value):
        return move(value, lambda z, q: (z, q ^ 1))

    def spread(value, source, bits):
        for bit in bits:
            moved = move(value, lambda z, q: (z, q ^ bit))
            value = jnp.where(((col ^ source) & bit) != 0, moved, value)
        return value

    bits = [1 << at for at in range(1, cols.bit_length() - 1)]
    blocks = panel.reshape(steps, depth * length // LANES, LANES)
    block = [blocks[step] for step in range(steps)]
    other = [swap_core(block[step]) for step in range(steps - 1)]
    heads = right_side.reshape(count, length)
    accum = jnp.where(row == 0, heads, 0.0)

    offsets = list(range(1, rows))
    middle = offsets.pop(len(offsets) // 2) if offsets else 0
    first, second = offsets[0::2], offsets[1::2]

    def sum_apply(total, step):
        fulls, halves = [], []
        for m_even, m_odd in zip(first, second):
            fulls.append(move(total, lambda z, q: (z ^ (m_even if q % 2 == 0 else m_odd), q)))
        if middle:
            part = lax.dynamic_slice_in_dim(total, parity * (length // 2), length // 2, 1)
            halves.append(move(part, lambda z, q: (z ^ middle, q)))
        piece = gather_apply(even, total, fulls, halves, inverse_blocks, step)
        return piece + swap_core(piece)

    own_piece = apply(heads, inverse_blocks, 0)
    piece = jnp.where(is_even, own_piece, swap_core(own_piece))
    solved = []
    for step in range(1, steps):
        hops = [bit for bit in bits if ((step - 1) ^ step) & bit]
        piece = spread(piece, step - 1, hops)
        active_even = step % 2 == 0
        base = jnp.where(is_even if active_even else ~is_even, accum, swap_core(accum))
        total = update_either(even if active_even else odd, piece, base, block[step - 1], other[step - 1])
        solved.append(spread(piece, step - 1, [bit for bit in bits if bit not in hops]))
        accum = update(solved[-1], accum, block[step - 1])
        piece = sum_apply(total, step)
    solved.append(spread(piece, steps - 1, bits))
    accum = update(solved[-1], accum, block[steps - 1])

    size = length // rows
    chunk = lambda at: lax.dynamic_slice_in_dim(accum, at * size, size, 1)
    updated = chunk(row)
    for offset in range(rows - 1, 0, -1):
        updated = updated + move(chunk(row ^ offset), lambda z, q: (z ^ offset, q))
    return jnp.stack(solved, axis=1), updated[:, None, None, :]


def solution(mesh):
    placed = (P(None, "row", None, "col", None), P(None, "row", None), P(None, None, "col", None))
    return jax.shard_map(
        functools.partial(body, mesh.shape["row"], mesh.shape["col"]),
        mesh=mesh,
        in_specs=placed,
        out_specs=(P(None, None, "row"), P(None, None, "col", "row")),
        check_vma=False,
    )
```

time: 384 us -> 114 us (0.30)
  waiting for transfers between devices: 322 us -> 43.4 us
  matrix products: 33.7 us -> 0 us
  starting transfers between devices: 0.51 us -> 30.4 us
  Pallas kernels: 0 us -> 17.7 us
  between operations: 14.2 us -> 0.91 us
  local copies, waits for them, and re-layouts: 12.1 us -> 21.5 us
    psum x7 -> x0, waiting for transfers between devices: 302 us -> none  [the longest x4 190 us: broadcast(): return lax.psum(kept, axis)]
    ppermute x0 -> x27, waiting for transfers between devices: none -> 43.4 us  [move(): return lax.ppermute(value, ('row', 'col'), pairs)]
    dot_general x8 -> x0, matrix products: 33.7 us -> none  [the longest x4 18.6 us: body(): jnp.dot(residue, inverse_blocks[step].T, precision=lax.Precision.HIGHEST,...]
    ppermute x0 -> x27, starting transfers between devices: none -> 30.4 us  [move(): return lax.ppermute(value, ('row', 'col'), pairs)]
    reduce_scatter x1 -> x0, waiting for transfers between devices: 20.3 us -> none  [body(): totals = lax.psum_scatter(accum, 'row', scatter_dimension=2, tiled=True)]
    pallas_call x0 -> x11, Pallas kernels: none -> 17.7 us  [the longest x3 8.65 us: update_either(): pl.pallas_call(update_either_kernel, out_shape=jax.ShapeDtypeStruct(base....]
    unnamed x18 -> x15, local copies, waits for them, and re-layouts: 1.57 us -> 8.94 us
  transfers between devices with their start and end apart: 8 -> 27, of which waited for: 8 -> 13; matrix products, arithmetic and copies ran while one was open for 3% -> 2% of each run, Pallas kernels for 0% -> 12%
where the time goes in v1:
time: 114 us
  waiting for transfers between devices  43.4 us (38%)
  starting transfers between devices  30.4 us (27%)
  local copies, waits for them, and re-layouts  21.5 us (19%)
  Pallas kernels  17.7 us (16%)
    ppermute x27, waiting for transfers between devices, move(): return lax.ppermute(value, ('row', 'col'), pairs)  43.4 us
    ppermute x27, starting transfers between devices, move(): return lax.ppermute(value, ('row', 'col'), pairs)  30.4 us
    slice x1, local copies, waits for them, and re-layouts, body(): block = [blocks[step] for step in range(steps)]  11.8 us
    unnamed x15, local copies, waits for them, and re-layouts  8.94 us
    pallas_call x3, Pallas kernels, update_either(): pl.pallas_call(update_either_kernel, out_shape=jax.ShapeDtypeStruct(base....  8.65 us
    pallas_call x4, Pallas kernels, update(): pl.pallas_call(update_kernel, out_shape=jax.ShapeDtypeStruct(base.shape,...  5.72 us
    pallas_call x3, Pallas kernels, gather_apply(): pl.pallas_call(functools.partial(gather_apply_kernel, len(fulls)), grid=(...  2.49 us
  transfers between devices with their start and end apart: 27, of which 13 were waited for; matrix products, arithmetic and copies ran while one was open for 2% of the time, Pallas kernels for 12%

profile of v1, /device:TPU:0, one launch (start us, length us, event | category | flops | bytes accessed | tf_op | source)
XLA Modules:
  0.0 114.1 jit_solution(7595896394342494450)
XLA Ops:
  0.7 11.8 %fusion = (f32[1,384,1,1,1536]{4,3,2,1,0:T(1,128)}, f32[1,384,1,1,1536]{4,3,2,1,0:T(1,128)}, f32[1,384,1,1,1536]{4,3,2,1,0:T(1,128)}, f32[1,384,1,1,1536]{4,3,2,1,0:T(1,128)S(1)}) fusion(f32[4,384,1,1,1536]{4,3,2,1,0:T(1,128)} %param.3), kind=kLoop, calls=%fused_computation.22 | loop fusion | bytes 18874368 | tf_op jit(solution)/shard_map/slice | solution.py:176
  15.0 2.4 %collective-permute-done = f32[48,384]{1,0:T(8,128)S(1)} collective-permute-done((f32[48,384]{1,0:T(8,128)S(1)}, f32[48,384]{1,0:T(8,128)S(1)}, u32[]{:S(2)}, u32[]{:S(2)}) %collective-permute-start) | collective-permute-done | bytes 73760 | tf_op jit(solution)/shard_map/ppermute | solution.py:163
  17.4 2.9 %collective-permute-start.1 = (f32[48,384]{1,0:T(8,128)S(1)}, f32[48,384]{1,0:T(8,128)S(1)}, u32[]{:S(2)}, u32[]{:S(2)}) collective-permute-start(f32[48,384]{1,0:T(8,128)S(1)} %broadcast_select_fusion.10.solved_ref), channel_id=1, source_target_pairs={{0,2},{1,3},{2,0},{3,1},{4,6},{5,7},{6,4},{7,5},{8,10},{9,11},{10,... | collective-permute-start | bytes 221192 | tf_op jit(solution)/shard_map/ppermute | solution.py:163
  20.4 3.0 %shard_map.51.own_ref = f32[48,1536]{1,0:T(8,128)S(1)} custom-call(s32[1]{0:T(128)S(6)} %sub.3.own_ref, f32[48,384]{1,0:T(8,128)S(1)} %broadcast_select_fusion.10.solved_ref, f32[48,1536]{1,0:T(8,128)S(1)} %broadcast_select_fusion.3.base_ref, f32[4608,128]{1,0:T(8,128)} %bitcast.2.block_ref, f32[4608,128]{1,0:T(8,128)} %collective-permute-done.4.other_ref), custom_call_target="tpu_custom_call" | custom-call | flops 169869312 | bytes 2727936 | tf_op jit(solution)/shard_map/pallas_call | solution.py:101
  23.4 1.6 %collective-permute-start.5 = (f32[48,1536]{1,0:T(8,128)S(1)}, f32[48,1536]{1,0:T(8,128)S(1)}, u32[]{:S(2)}, u32[]{:S(2)}) collective-permute-start(f32[48,1536]{1,0:T(8,128)S(1)} %shard_map.51.own_ref), channel_id=1, source_target_pairs={{0,8},{1,25},{2,10},{3,27},{4,12},{5,29},{6,14},{7,31},{8,0},{9,17... | collective-permute-start | bytes 884744 | tf_op jit(solution)/shard_map/ppermute | solution.py:163
  25.7 2.6 %collective-permute-start.6 = (f32[48,768]{1,0:T(8,128)}, f32[48,768]{1,0:T(8,128)S(1)}, u32[]{:S(2)}, u32[]{:S(2)}) collective-permute-start(f32[48,768]{1,0:T(8,128)} %constant_dynamic-slice_fusion.5), channel_id=1, source_target_pairs={{0,16},{1,17},{2,18},{3,19},{4,20},{5,21},{6,22},{7,23},{8,24},{9,... | collective-permute-start | bytes 442376 | tf_op jit(solution)/shard_map/ppermute | solution.py:163
  28.3 1.6 %collective-permute-start.2 = (f32[48,384]{1,0:T(8,128)S(1)}, f32[48,384]{1,0:T(8,128)S(1)}, u32[]{:S(2)}, u32[]{:S(2)}) collective-permute-start(f32[48,384]{1,0:T(8,128)S(1)} %broadcast_select_fusion.11), channel_id=1, source_target_pairs={{0,4},{1,5},{2,6},{3,7},{4,0},{5,1},{6,2},{7,3},{8,12},{9,13},{10,... | collective-permute-start | bytes 221192 | tf_op jit(solution)/shard_map/ppermute | solution.py:163
  29.9 8.1 %collective-permute-done.6.refs_1_ = f32[48,768]{1,0:T(8,128)S(1)} collective-permute-done((f32[48,768]{1,0:T(8,128)}, f32[48,768]{1,0:T(8,128)S(1)}, u32[]{:S(2)}, u32[]{:S(2)}) %collective-permute-start.6) | collective-permute-done | bytes 147488 | tf_op jit(solution)/shard_map/ppermute | solution.py:163
  38.0 3.7 %copy-done.1 = f32[4,384,1536]{2,1,0:T(8,128)S(1)} copy-done((f32[4,384,1536]{2,1,0:T(8,128)S(1)}, f32[4,384,1536]{2,1,0:T(8,128)}, u32[]{:S(2)}) %copy-start.1) | copy-done | bytes 9437208
  46.4 2.3 %shard_map.53.base_ref = f32[48,1536]{1,0:T(8,128)S(1)} custom-call(f32[48,384]{1,0:T(8,128)S(1)} %broadcast_select_fusion.12.solved_ref, f32[48,1536]{1,0:T(8,128)S(1)} %broadcast_select_fusion.base_ref, f32[4608,128]{1,0:T(8,128)} %bitcast.2.block_ref), custom_call_target="tpu_custom_call" | custom-call | flops 169869312 | bytes 2727936 | tf_op jit(solution)/shard_map/pallas_call | solution.py:89
  49.4 1.6 %collective-permute-start.9 = (f32[48,384]{1,0:T(8,128)S(1)}, f32[48,384]{1,0:T(8,128)S(1)}, u32[]{:S(2)}, u32[]{:S(2)}) collective-permute-start(f32[48,384]{1,0:T(8,128)S(1)} %broadcast_select_fusion.8.solved_ref), channel_id=1, source_target_pairs={{0,4},{1,5},{2,6},{3,7},{4,0},{5,1},{6,2},{7,3},{8,12},{9,13},{10,... | collective-permute-start | bytes 221192 | tf_op jit(solution)/shard_map/ppermute | solution.py:163
  51.1 3.0 %shard_map.54.own_ref = f32[48,1536]{1,0:T(8,128)S(1)} custom-call(s32[1]{0:T(128)} %bitcast.1.flag_ref.own_ref, f32[48,384]{1,0:T(8,128)S(1)} %broadcast_select_fusion.8.solved_ref, f32[48,1536]{1,0:T(8,128)S(1)} %broadcast_select_fusion.1.base_ref, f32[4608,128]{1,0:T(8,128)} %bitcast.4.block_ref, f32[4608,128]{1,0:T(8,128)} %collective-permute-done.11.other_ref), custom_call_target="tpu_custom_call" | custom-call | flops 169869312 | bytes 2727936 | tf_op jit(solution)/shard_map/pallas_call | solution.py:101
  54.2 2.3 %shard_map.56.base_ref = f32[48,1536]{1,0:T(8,128)S(1)} custom-call(f32[48,384]{1,0:T(8,128)S(1)} %broadcast_select_fusion.9.solved_ref, f32[48,1536]{1,0:T(8,128)S(1)} %shard_map.53.base_ref, f32[4608,128]{1,0:T(8,128)} %bitcast.4.block_ref), custom_call_target="tpu_custom_call" | custom-call | flops 169869312 | bytes 2727936 | tf_op jit(solution)/shard_map/pallas_call | solution.py:89
  56.5 1.7 %collective-permute-start.17 = (f32[48,1536]{1,0:T(8,128)S(1)}, f32[48,1536]{1,0:T(8,128)S(1)}, u32[]{:S(2)}, u32[]{:S(2)}) collective-permute-start(f32[48,1536]{1,0:T(8,128)S(1)} %shard_map.56.base_ref), channel_id=1, source_target_pairs={{0,1},{1,0},{2,3},{3,2},{4,5},{5,4},{6,7},{7,6},{8,9},{9,8},{10,11... | collective-permute-start | bytes 884744 | tf_op jit(solution)/shard_map/ppermute | solution.py:163
  59.6 9.7 %collective-permute-done.13.refs_1_ = f32[48,768]{1,0:T(8,128)S(1)} collective-permute-done((f32[48,768]{1,0:T(8,128)S(1)}, f32[48,768]{1,0:T(8,128)S(1)}, u32[]{:S(2)}, u32[]{:S(2)}) %collective-permute-start.13) | collective-permute-done | bytes 147488 | tf_op jit(solution)/shard_map/ppermute | solution.py:163
  69.3 3.7 %copy-done.2 = f32[4,384,1536]{2,1,0:T(8,128)S(1)} copy-done((f32[4,384,1536]{2,1,0:T(8,128)S(1)}, f32[4,384,1536]{2,1,0:T(8,128)}, u32[]{:S(2)}) %copy-start.2) | copy-done | bytes 9437208
  75.2 2.7 %shard_map.57.own_ref = f32[48,1536]{1,0:T(8,128)S(1)} custom-call(s32[1]{0:T(128)S(6)} %sub.3.own_ref, f32[48,384]{1,0:T(8,128)S(1)} %add.37.solved_ref, f32[48,1536]{1,0:T(8,128)S(1)} %broadcast_select_fusion.2.base_ref, f32[4608,128]{1,0:T(8,128)S(1)} %bitcast.19, f32[4608,128]{1,0:T(8,128)} %collective-permute-done.18.other_ref), custom_call_target="tpu_custom_call" | custom-call | flops 169869312 | bytes 2727936 | tf_op jit(solution)/shard_map/pallas_call | solution.py:101
  78.1 2.6 %collective-permute-start.20 = (f32[48,768]{1,0:T(8,128)S(1)}, f32[48,768]{1,0:T(8,128)S(1)}, u32[]{:S(2)}, u32[]{:S(2)}) collective-permute-start(f32[48,768]{1,0:T(8,128)S(1)} %constant_dynamic-slice_fusion.3), channel_id=1, source_target_pairs={{0,16},{1,17},{2,18},{3,19},{4,20},{5,21},{6,22},{7,23},{8,24},{9,... | collective-permute-start | bytes 442376 | tf_op jit(solution)/shard_map/ppermute | solution.py:163
  80.6 11.0 %collective-permute-done.20.refs_1_ = f32[48,768]{1,0:T(8,128)S(1)} collective-permute-done((f32[48,768]{1,0:T(8,128)S(1)}, f32[48,768]{1,0:T(8,128)S(1)}, u32[]{:S(2)}, u32[]{:S(2)}) %collective-permute-start.20) | collective-permute-done | bytes 147488 | tf_op jit(solution)/shard_map/ppermute | solution.py:163
  95.0 2.8 %collective-permute-done.15 = f32[48,384]{1,0:T(8,128)S(1)} collective-permute-done((f32[48,384]{1,0:T(8,128)S(1)}, f32[48,384]{1,0:T(8,128)S(1)}, u32[]{:S(2)}, u32[]{:S(2)}) %collective-permute-start.15) | collective-permute-done | bytes 73760 | tf_op jit(solution)/shard_map/ppermute | solution.py:163
  100.3 2.4 %collective-permute-done.16 = f32[48,384]{1,0:T(8,128)S(1)} collective-permute-done((f32[48,384]{1,0:T(8,128)S(1)}, f32[48,384]{1,0:T(8,128)S(1)}, u32[]{:S(2)}, u32[]{:S(2)}) %collective-permute-start.16) | collective-permute-done | bytes 73760 | tf_op jit(solution)/shard_map/ppermute | solution.py:163
  104.3 2.8 %collective-permute-start.25 = (f32[48,384]{1,0:T(8,128)S(1)}, f32[48,384]{1,0:T(8,128)S(1)}, u32[]{:S(2)}, u32[]{:S(2)}) collective-permute-start(f32[48,384]{1,0:T(8,128)S(1)} %get-tuple-element.10), channel_id=1, source_target_pairs={{0,16},{1,17},{2,18},{3,19},{4,20},{5,21},{6,22},{7,23},{8,24},{9,... | collective-permute-start | bytes 221192 | tf_op jit(solution)/shard_map/ppermute | solution.py:163
  107.1 1.6 %collective-permute-start.24 = (f32[48,384]{1,0:T(8,128)S(1)}, f32[48,384]{1,0:T(8,128)S(1)}, u32[]{:S(2)}, u32[]{:S(2)}) collective-permute-start(f32[48,384]{1,0:T(8,128)S(1)} %get-tuple-element.8), channel_id=1, source_target_pairs={{0,24},{1,25},{2,26},{3,27},{4,28},{5,29},{6,30},{7,31},{8,16},{9,... | collective-permute-start | bytes 221192 | tf_op jit(solution)/shard_map/ppermute | solution.py:163
  109.6 2.3 %collective-permute-done.25 = f32[48,384]{1,0:T(8,128)S(1)} collective-permute-done((f32[48,384]{1,0:T(8,128)S(1)}, f32[48,384]{1,0:T(8,128)S(1)}, u32[]{:S(2)}, u32[]{:S(2)}) %collective-permute-start.25) | collective-permute-done | bytes 73760 | tf_op jit(solution)/shard_map/ppermute | solution.py:163
  (79 shorter events, 23.2 us)
Async XLA Ops:
  12.5 7.9 %collective-permute-start.4 = (f32[4608,128]{1,0:T(8,128)}, f32[4608,128]{1,0:T(8,128)}, u32[]{:S(2)}, u32[]{:S(2)}) collective-permute-start(f32[4608,128]{1,0:T(8,128)} %bitcast.2.block_ref), channel_id=1, source_target_pairs={{0,1},{1,0},{2,3},{3,2},{4,5},{5,4},{6,7},{7,6},{8,9},{9,8},{10,11... | collective-permute-start | bytes 7077896 | tf_op jit(solution)/shard_map/ppermute | solution.py:163
  13.8 3.6 %collective-permute-start = (f32[48,384]{1,0:T(8,128)S(1)}, f32[48,384]{1,0:T(8,128)S(1)}, u32[]{:S(2)}, u32[]{:S(2)}) collective-permute-start(f32[48,384]{1,0:T(8,128)S(1)} %shard_map.50), channel_id=1, source_target_pairs={{0,1},{1,0},{2,3},{3,2},{4,5},{5,4},{6,7},{7,6},{8,9},{9,8},{10,11... | collective-permute-start | bytes 221192 | tf_op jit(solution)/shard_map/ppermute | solution.py:163
  13.9 37.1 %collective-permute-start.11 = (f32[4608,128]{1,0:T(8,128)}, f32[4608,128]{1,0:T(8,128)}, u32[]{:S(2)}, u32[]{:S(2)}) collective-permute-start(f32[4608,128]{1,0:T(8,128)} %bitcast.4.block_ref), channel_id=1, source_target_pairs={{0,1},{1,0},{2,3},{3,2},{4,5},{5,4},{6,7},{7,6},{8,9},{9,8},{10,11... | collective-permute-start | bytes 7077896 | tf_op jit(solution)/shard_map/ppermute | solution.py:163
  14.4 5.9 %collective-permute-start.3 = (f32[48,1536]{1,0:T(8,128)S(1)}, f32[48,1536]{1,0:T(8,128)S(1)}, u32[]{:S(2)}, u32[]{:S(2)}) collective-permute-start(f32[48,1536]{1,0:T(8,128)S(1)} %broadcast_select_fusion.base_ref), channel_id=1, source_target_pairs={{0,1},{1,0},{2,3},{3,2},{4,5},{5,4},{6,7},{7,6},{8,9},{9,8},{10,11... | collective-permute-start | bytes 884744 | tf_op jit(solution)/shard_map/ppermute | solution.py:163
  14.6 60.7 %collective-permute-start.18 = (f32[4608,128]{1,0:T(8,128)S(1)}, f32[4608,128]{1,0:T(8,128)}, u32[]{:S(2)}, u32[]{:S(2)}) collective-permute-start(f32[4608,128]{1,0:T(8,128)S(1)} %bitcast.18), channel_id=1, source_target_pairs={{0,1},{1,0},{2,3},{3,2},{4,5},{5,4},{6,7},{7,6},{8,9},{9,8},{10,11... | collective-permute-start | bytes 7077896 | tf_op jit(solution)/shard_map/ppermute | solution.py:163
  17.4 10.9 %collective-permute-start.1 = (f32[48,384]{1,0:T(8,128)S(1)}, f32[48,384]{1,0:T(8,128)S(1)}, u32[]{:S(2)}, u32[]{:S(2)}) collective-permute-start(f32[48,384]{1,0:T(8,128)S(1)} %broadcast_select_fusion.10.solved_ref), channel_id=1, source_target_pairs={{0,2},{1,3},{2,0},{3,1},{4,6},{5,7},{6,4},{7,5},{8,10},{9,11},{10,... | collective-permute-start | bytes 221192 | tf_op jit(solution)/shard_map/ppermute | solution.py:163
  23.4 14.6 %collective-permute-start.5 = (f32[48,1536]{1,0:T(8,128)S(1)}, f32[48,1536]{1,0:T(8,128)S(1)}, u32[]{:S(2)}, u32[]{:S(2)}) collective-permute-start(f32[48,1536]{1,0:T(8,128)S(1)} %shard_map.51.own_ref), channel_id=1, source_target_pairs={{0,8},{1,25},{2,10},{3,27},{4,12},{5,29},{6,14},{7,31},{8,0},{9,17... | collective-permute-start | bytes 884744 | tf_op jit(solution)/shard_map/ppermute | solution.py:163
  25.7 12.3 %collective-permute-start.6 = (f32[48,768]{1,0:T(8,128)}, f32[48,768]{1,0:T(8,128)S(1)}, u32[]{:S(2)}, u32[]{:S(2)}) collective-permute-start(f32[48,768]{1,0:T(8,128)} %constant_dynamic-slice_fusion.5), channel_id=1, source_target_pairs={{0,16},{1,17},{2,18},{3,19},{4,20},{5,21},{6,22},{7,23},{8,24},{9,... | collective-permute-start | bytes 442376 | tf_op jit(solution)/shard_map/ppermute | solution.py:163
  28.3 15.6 %collective-permute-start.2 = (f32[48,384]{1,0:T(8,128)S(1)}, f32[48,384]{1,0:T(8,128)S(1)}, u32[]{:S(2)}, u32[]{:S(2)}) collective-permute-start(f32[48,384]{1,0:T(8,128)S(1)} %broadcast_select_fusion.11), channel_id=1, source_target_pairs={{0,4},{1,5},{2,6},{3,7},{4,0},{5,1},{6,2},{7,3},{8,12},{9,13},{10,... | collective-permute-start | bytes 221192 | tf_op jit(solution)/shard_map/ppermute | solution.py:163
  44.8 4.6 %collective-permute-start.8 = (f32[48,384]{1,0:T(8,128)S(1)}, f32[48,384]{1,0:T(8,128)S(1)}, u32[]{:S(2)}, u32[]{:S(2)}) collective-permute-start(f32[48,384]{1,0:T(8,128)S(1)} %add.36), channel_id=1, source_target_pairs={{0,2},{1,3},{2,0},{3,1},{4,6},{5,7},{6,4},{7,5},{8,10},{9,11},{10,... | collective-permute-start | bytes 221192 | tf_op jit(solution)/shard_map/ppermute | solution.py:163
  48.6 2.4 %collective-permute-start.10 = (f32[48,1536]{1,0:T(8,128)S(1)}, f32[48,1536]{1,0:T(8,128)S(1)}, u32[]{:S(2)}, u32[]{:S(2)}) collective-permute-start(f32[48,1536]{1,0:T(8,128)S(1)} %shard_map.53.base_ref), channel_id=1, source_target_pairs={{0,1},{1,0},{2,3},{3,2},{4,5},{5,4},{6,7},{7,6},{8,9},{9,8},{10,11... | collective-permute-start | bytes 884744 | tf_op jit(solution)/shard_map/ppermute | solution.py:163
  49.4 4.7 %collective-permute-start.9 = (f32[48,384]{1,0:T(8,128)S(1)}, f32[48,384]{1,0:T(8,128)S(1)}, u32[]{:S(2)}, u32[]{:S(2)}) collective-permute-start(f32[48,384]{1,0:T(8,128)S(1)} %broadcast_select_fusion.8.solved_ref), channel_id=1, source_target_pairs={{0,4},{1,5},{2,6},{3,7},{4,0},{5,1},{6,2},{7,3},{8,12},{9,13},{10,... | collective-permute-start | bytes 221192 | tf_op jit(solution)/shard_map/ppermute | solution.py:163
  54.1 15.3 %collective-permute-start.12 = (f32[48,1536]{1,0:T(8,128)S(1)}, f32[48,1536]{1,0:T(8,128)S(1)}, u32[]{:S(2)}, u32[]{:S(2)}) collective-permute-start(f32[48,1536]{1,0:T(8,128)S(1)} %shard_map.54.own_ref), channel_id=1, source_target_pairs={{0,8},{1,25},{2,10},{3,27},{4,12},{5,29},{6,14},{7,31},{8,0},{9,17... | collective-permute-start | bytes 884744 | tf_op jit(solution)/shard_map/ppermute | solution.py:163
  56.5 18.7 %collective-permute-start.17 = (f32[48,1536]{1,0:T(8,128)S(1)}, f32[48,1536]{1,0:T(8,128)S(1)}, u32[]{:S(2)}, u32[]{:S(2)}) collective-permute-start(f32[48,1536]{1,0:T(8,128)S(1)} %shard_map.56.base_ref), channel_id=1, source_target_pairs={{0,1},{1,0},{2,3},{3,2},{4,5},{5,4},{6,7},{7,6},{8,9},{9,8},{10,11... | collective-permute-start | bytes 884744 | tf_op jit(solution)/shard_map/ppermute | solution.py:163
  58.2 11.1 %collective-permute-start.13 = (f32[48,768]{1,0:T(8,128)S(1)}, f32[48,768]{1,0:T(8,128)S(1)}, u32[]{:S(2)}, u32[]{:S(2)}) collective-permute-start(f32[48,768]{1,0:T(8,128)S(1)} %constant_dynamic-slice_fusion.4), channel_id=1, source_target_pairs={{0,16},{1,17},{2,18},{3,19},{4,20},{5,21},{6,22},{7,23},{8,24},{9,... | collective-permute-start | bytes 442376 | tf_op jit(solution)/shard_map/ppermute | solution.py:163
  77.9 13.7 %collective-permute-start.19 = (f32[48,1536]{1,0:T(8,128)S(1)}, f32[48,1536]{1,0:T(8,128)S(1)}, u32[]{:S(2)}, u32[]{:S(2)}) collective-permute-start(f32[48,1536]{1,0:T(8,128)S(1)} %shard_map.57.own_ref), channel_id=1, source_target_pairs={{0,8},{1,25},{2,10},{3,27},{4,12},{5,29},{6,14},{7,31},{8,0},{9,17... | collective-permute-start | bytes 884744 | tf_op jit(solution)/shard_map/ppermute | solution.py:163
  78.1 13.5 %collective-permute-start.20 = (f32[48,768]{1,0:T(8,128)S(1)}, f32[48,768]{1,0:T(8,128)S(1)}, u32[]{:S(2)}, u32[]{:S(2)}) collective-permute-start(f32[48,768]{1,0:T(8,128)S(1)} %constant_dynamic-slice_fusion.3), channel_id=1, source_target_pairs={{0,16},{1,17},{2,18},{3,19},{4,20},{5,21},{6,22},{7,23},{8,24},{9,... | collective-permute-start | bytes 442376 | tf_op jit(solution)/shard_map/ppermute | solution.py:163
  92.6 5.1 %collective-permute-start.15 = (f32[48,384]{1,0:T(8,128)S(1)}, f32[48,384]{1,0:T(8,128)S(1)}, u32[]{:S(2)}, u32[]{:S(2)}) collective-permute-start(f32[48,384]{1,0:T(8,128)S(1)} %add.37.solved_ref), channel_id=1, source_target_pairs={{0,2},{1,3},{2,0},{3,1},{4,6},{5,7},{6,4},{7,5},{8,10},{9,11},{10,... | collective-permute-start | bytes 221192 | tf_op jit(solution)/shard_map/ppermute | solution.py:163
  93.8 5.3 %collective-permute-start.22 = (f32[48,384]{1,0:T(8,128)S(1)}, f32[48,384]{1,0:T(8,128)S(1)}, u32[]{:S(2)}, u32[]{:S(2)}) collective-permute-start(f32[48,384]{1,0:T(8,128)S(1)} %add.38), channel_id=1, source_target_pairs={{0,2},{1,3},{2,0},{3,1},{4,6},{5,7},{6,4},{7,5},{8,10},{9,11},{10,... | collective-permute-start | bytes 221192 | tf_op jit(solution)/shard_map/ppermute | solution.py:163
  97.7 5.0 %collective-permute-start.16 = (f32[48,384]{1,0:T(8,128)S(1)}, f32[48,384]{1,0:T(8,128)S(1)}, u32[]{:S(2)}, u32[]{:S(2)}) collective-permute-start(f32[48,384]{1,0:T(8,128)S(1)} %broadcast_select_fusion.6), channel_id=1, source_target_pairs={{0,4},{1,5},{2,6},{3,7},{4,0},{5,1},{6,2},{7,3},{8,12},{9,13},{10,... | collective-permute-start | bytes 221192 | tf_op jit(solution)/shard_map/ppermute | solution.py:163
  99.2 4.4 %collective-permute-start.23 = (f32[48,384]{1,0:T(8,128)S(1)}, f32[48,384]{1,0:T(8,128)S(1)}, u32[]{:S(2)}, u32[]{:S(2)}) collective-permute-start(f32[48,384]{1,0:T(8,128)S(1)} %broadcast_select_fusion.4), channel_id=1, source_target_pairs={{0,4},{1,5},{2,6},{3,7},{4,0},{5,1},{6,2},{7,3},{8,12},{9,13},{10,... | collective-permute-start | bytes 221192 | tf_op jit(solution)/shard_map/ppermute | solution.py:163
  104.3 5.3 %collective-permute-start.26 = (f32[48,384]{1,0:T(8,128)S(1)}, f32[48,384]{1,0:T(8,128)S(1)}, u32[]{:S(2)}, u32[]{:S(2)}) collective-permute-start(f32[48,384]{1,0:T(8,128)S(1)} %get-tuple-element.9), channel_id=1, source_target_pairs={{0,8},{1,9},{2,10},{3,11},{4,12},{5,13},{6,14},{7,15},{8,0},{9,1},... | collective-permute-start | bytes 221192 | tf_op jit(solution)/shard_map/ppermute | solution.py:163
  104.3 7.5 %collective-permute-start.25 = (f32[48,384]{1,0:T(8,128)S(1)}, f32[48,384]{1,0:T(8,128)S(1)}, u32[]{:S(2)}, u32[]{:S(2)}) collective-permute-start(f32[48,384]{1,0:T(8,128)S(1)} %get-tuple-element.10), channel_id=1, source_target_pairs={{0,16},{1,17},{2,18},{3,19},{4,20},{5,21},{6,22},{7,23},{8,24},{9,... | collective-permute-start | bytes 221192 | tf_op jit(solution)/shard_map/ppermute | solution.py:163
  107.1 6.3 %collective-permute-start.24 = (f32[48,384]{1,0:T(8,128)S(1)}, f32[48,384]{1,0:T(8,128)S(1)}, u32[]{:S(2)}, u32[]{:S(2)}) collective-permute-start(f32[48,384]{1,0:T(8,128)S(1)} %get-tuple-element.8), channel_id=1, source_target_pairs={{0,24},{1,25},{2,26},{3,27},{4,28},{5,29},{6,30},{7,31},{8,16},{9,... | collective-permute-start | bytes 221192 | tf_op jit(solution)/shard_map/ppermute | solution.py:163
  (9 other events, 65.5 us)

commit v2 on v0

v2 whole, which is shorter than its diff:
```python
import functools

import jax
import jax.numpy as jnp
from jax import lax
from jax.experimental import pallas as pl
from jax.experimental.pallas import tpu as pltpu
from jax.sharding import PartitionSpec as P

LANES = 128
F32 = jnp.float32
BF16 = jnp.bfloat16
VMEM = pl.BlockSpec(memory_space=pltpu.VMEM)
SMEM = pl.BlockSpec(memory_space=pltpu.SMEM)
ANY = pl.BlockSpec(memory_space=pl.ANY)
HBM = pl.BlockSpec(memory_space=pltpu.HBM)
PARAMS = pltpu.CompilerParams(vmem_limit_bytes=8 * 2**20)


def split(value):
    head = value.astype(BF16)
    return head, (value - head.astype(F32)).astype(BF16)


def product(left, right, dims):
    count = left.shape[0]
    left_head, left_tail = split(left)
    right_head, right_tail = split(right)
    dot = functools.partial(lax.dot_general, dimension_numbers=(dims, ((), ())), preferred_element_type=F32)
    stacked = dot(jnp.concatenate([left_head, left_tail], axis=0), right_head)
    return stacked[:count] + stacked[count:] + dot(left_head, right_tail)


def columns(block_ref, first, width, rows):
    if block_ref.shape[0] == rows:
        return block_ref[:, first : first + width]
    stride = block_ref.shape[0] // rows
    parts = [block_ref[pl.ds(at // LANES, rows, stride=stride), :] for at in range(first, first + width, LANES)]
    return parts[0] if len(parts) == 1 else jnp.concatenate(parts, axis=1)


def subtract_products(solved, base_ref, block_refs, out_ref):
    length = base_ref.shape[1]
    width = 2 * LANES
    for first in range(0, length, width):
        at = slice(first, first + width)
        total = base_ref[:, at]
        for value, block_ref in zip(solved, block_refs):
            total = total - product(value, columns(block_ref, first, width, value.shape[1]), ((1,), (0,)))
        out_ref[:, at] = total


def call(kernel, outs, ins, in_specs, flops=0, scratch=()):
    moved = sum(4 * out.size for out in outs) if flops else 0
    return pl.pallas_call(
        kernel,
        out_shape=outs,
        in_specs=in_specs,
        out_specs=[VMEM] * len(outs),
        scratch_shapes=scratch,
        compiler_params=PARAMS,
        cost_estimate=pl.CostEstimate(flops=flops, bytes_accessed=moved, transcendentals=0),
    )(*ins)


def shape(*sizes):
    return jax.ShapeDtypeStruct(sizes, F32)


def start(copies):
    for copy in copies:
        copy.start()


def finish(copies):
    for copy in copies:
        copy.wait()


def first_step(keep, heads, inverse_blocks, count):
    rows, length = inverse_blocks.shape[1:]
    stride = heads.shape[0] // count
    pieces = 3 if rows % (3 * LANES) == 0 else 1
    size = rows // pieces

    def kernel(keep_ref, heads_ref, inverse_ref, out_ref, kept_ref, heads_here, inverse_here, sems):
        copies = [pltpu.make_async_copy(heads_ref, heads_here, sems.at[pieces])]
        for at in range(pieces):
            piece = pl.ds(at * size, size)
            copies.append(pltpu.make_async_copy(inverse_ref.at[0, piece], inverse_here.at[piece], sems.at[at]))
        start(copies)
        copies[0].wait()
        value = columns(heads_here, 0, stride * LANES, count)
        kept_ref[...] = jnp.where(keep_ref[0] == 1, value, 0.0)
        for at in range(pieces):
            piece = slice(at * size, (at + 1) * size)
            copies[at + 1].wait()
            out_ref[:, piece] = product(value, inverse_here[piece, :], ((1,), (1,)))

    return call(
        kernel,
        [shape(count, rows), shape(count, length)],
        [keep, heads, inverse_blocks],
        [SMEM, HBM, HBM],
        6 * count * rows * length,
        [pltpu.VMEM(heads.shape, F32), pltpu.VMEM((rows, length), F32), pltpu.SemaphoreType.DMA((pieces + 1,))],
    )


def after(token, value):
    def kernel(token_ref, value_ref, out_ref):
        out_ref[...] = value_ref[...]

    return call(kernel, [shape(*value.shape)], [token, value], [ANY, VMEM])[0]


def load(token, arrays):
    wanted = [(at, index) for at, (_, indices) in enumerate(arrays) for index in indices]

    def kernel(token_ref, *refs):
        ins, outs, sems = refs[: len(arrays)], refs[len(arrays) : -1], refs[-1]
        copies = [
            pltpu.make_async_copy(ins[at].at[index], out, sems.at[n]) for n, ((at, index), out) in enumerate(zip(wanted, outs))
        ]
        start(copies)
        finish(copies)

    return call(
        kernel,
        [shape(*arrays[at][0].shape[1:]) for at, _ in wanted],
        [token] + [array for array, _ in arrays],
        [ANY] + [HBM] * len(arrays),
        scratch=[pltpu.SemaphoreType.DMA((len(wanted),))],
    )


def update(solved, base, blocks, urgent=True):
    many = len(solved)

    def kernel(*refs):
        subtract_products([ref[...] for ref in refs[:many]], refs[many], refs[many + 1 : -1], refs[-1])

    flops = 6 * base.size * sum(value.shape[1] for value in solved) if urgent else 0
    ins = list(solved) + [base] + list(blocks)
    return call(kernel, [shape(*base.shape)], ins, [VMEM] * len(ins), flops)[0]


def gather_apply(odd, own, fulls, halves, inverse):
    count, length = own.shape
    rows = inverse.shape[0]

    def kernel(odd_ref, *refs):
        odd = odd_ref[0]
        own_ref, rest = refs[0], refs[1:-2]
        inverse_ref, out_ref = refs[-2:]
        value = jnp.where(odd == 1, 0.0, own_ref[...])
        for ref in rest[: len(fulls)]:
            value = value + ref[...]
        for ref in rest[len(fulls) :]:
            half = ref[...]
            zero = jnp.zeros_like(half)
            value = value + jnp.concatenate([jnp.where(odd == 1, zero, half), jnp.where(odd == 1, half, zero)], axis=1)
        out_ref[...] = product(value, inverse_ref[...], ((1,), (1,)))

    ins = [own] + fulls + halves + [inverse]
    return call(kernel, [shape(count, rows)], [odd.reshape(1)] + ins, [SMEM] + [VMEM] * len(ins), 6 * own.size * rows)[0]


def body(rows, cols, panel, inverse_blocks, right_side):
    steps, depth, _, _, length = panel.shape
    count = right_side.shape[0]
    row, col = lax.axis_index("row"), lax.axis_index("col")
    odd = lax.rem(col, 2)
    is_odd, is_right = odd == 1, lax.rem(col // 2, 2) == 1
    bits = [1 << at for at in range(1, cols.bit_length() - 1)]

    def move(value, target, senders=range(cols)):
        pairs = []
        for z in range(rows):
            for q in senders:
                to_z, to_q = target(z, q)
                pairs.append((z * cols + q, to_z * cols + to_q))
        return lax.ppermute(value, ("row", "col"), pairs)

    def swap_core(value):
        return move(value, lambda z, q: (z, q ^ 1))

    def spread(value, source, bits):
        for bit in bits:
            moved = move(value, lambda z, q: (z, q ^ bit))
            value = jnp.where(((col ^ source) & bit) != 0, moved, value)
        return value

    offsets = list(range(1, rows))
    middle = offsets.pop(len(offsets) // 2) if offsets else 0
    first, second = offsets[0::2], offsets[1::2]

    def sum_apply(total, part, inverse):
        fulls = [move(total, lambda z, q: (z ^ (b if q % 2 else a), q)) for a, b in zip(first, second)]
        halves = [move(part, lambda z, q: (z ^ middle, q))] if middle else []
        piece = gather_apply(odd, total, fulls, halves, inverse)
        return piece + swap_core(piece)

    half = length // 2
    blocks = panel.reshape(steps, depth * length // LANES, LANES)
    blocks = pltpu.with_memory_space_constraint(blocks, pltpu.HBM)
    inverse_blocks = pltpu.with_memory_space_constraint(inverse_blocks, pltpu.HBM)
    heads = pltpu.with_memory_space_constraint(right_side.reshape(count * length // LANES, LANES), pltpu.HBM)

    def to_right(value):
        return jnp.where(is_right, move(value, lambda z, q: (z, q ^ 2), (0, 1)), value)

    keep = jnp.where(row == 0, 1, 0).astype(jnp.int32).reshape(1)
    own_piece, start_value = first_step(keep, heads, inverse_blocks, count)
    x_0 = jnp.where(is_odd, swap_core(own_piece), own_piece)
    (block_0,) = load(own_piece, [(blocks, (0,))])

    def on_chip(total, step):
        total = jnp.where(is_odd == (step % 2 == 1), total, swap_core(total))
        return total, lax.dynamic_slice_in_dim(total, odd * half, half, 1)

    own_total = update([x_0], start_value, [block_0])
    total, part = on_chip(own_total, 1)
    inverse_1, block_1 = load(total, [(inverse_blocks, (1,)), (blocks, (1,))])
    x_0 = to_right(after(total, x_0))
    early = update([x_0], start_value, [block_0], False)
    x_1 = to_right(sum_apply(total, part, inverse_1))

    own_total = update([x_1], early, [block_1])
    total, part = on_chip(own_total, 2)
    inverse_2, block_2 = load(total, [(inverse_blocks, (2,)), (blocks, (2,))])
    x_2 = sum_apply(total, part, inverse_2)

    own_total = update([x_2], own_total, [block_2])
    total, part = on_chip(own_total, 3)
    inverse_3, block_3 = load(total, [(inverse_blocks, (3,)), (blocks, (3,))])
    x_2 = spread(after(total, x_2), 2, bits[:1])
    before = spread(jnp.concatenate([x_0, x_1, x_2], axis=1), 2, bits[1:])
    before = [before[:, at * depth : (at + 1) * depth] for at in range(3)]
    accum = update(before, start_value, [block_0, block_1, block_2], False)
    x_3 = spread(sum_apply(total, part, inverse_3), 2, bits)
    accum = update([x_3], accum, [block_3])

    size = length // rows
    chunk = lambda at: lax.dynamic_slice_in_dim(accum, at * size, size, 1)
    updated = chunk(row)
    for offset in range(rows - 1, 0, -1):
        updated = updated + move(chunk(row ^ offset), lambda z, q: (z ^ offset, q))
    return jnp.stack(before + [x_3], axis=1), updated[:, None, None, :]


def solution(mesh):
    placed = (P(None, "row", None, "col", None), P(None, "row", None), P(None, None, "col", None))
    return jax.shard_map(
        functools.partial(body, mesh.shape["row"], mesh.shape["col"]),
        mesh=mesh,
        in_specs=placed,
        out_specs=(P(None, None, "row"), P(None, None, "col", "row")),
        check_vma=False,
    )
```

time: 384 us -> 91.3 us (0.24)
  waiting for transfers between devices: 322 us -> 33.9 us
  matrix products: 33.7 us -> 0 us
  starting transfers between devices: 0.51 us -> 28.6 us
  Pallas kernels: 0 us -> 18.6 us
  between operations: 14.2 us -> 1.01 us
  local copies, waits for them, and re-layouts: 12.1 us -> 7.92 us
    psum x7 -> x0, waiting for transfers between devices: 302 us -> none  [the longest x4 190 us: broadcast(): return lax.psum(kept, axis)]
    ppermute x0 -> x22, waiting for transfers between devices: none -> 33.9 us  [move(): return lax.ppermute(value, ('row', 'col'), pairs)]
    dot_general x8 -> x0, matrix products: 33.7 us -> none  [the longest x4 18.6 us: body(): jnp.dot(residue, inverse_blocks[step].T, precision=lax.Precision.HIGHEST,...]
    ppermute x0 -> x22, starting transfers between devices: none -> 28.6 us  [move(): return lax.ppermute(value, ('row', 'col'), pairs)]
    reduce_scatter x1 -> x0, waiting for transfers between devices: 20.3 us -> none  [body(): totals = lax.psum_scatter(accum, 'row', scatter_dimension=2, tiled=True)]
    pallas_call x0 -> x16, Pallas kernels: none -> 18.6 us  [call(): pl.pallas_call(kernel, out_shape=outs, in_specs=in_specs, out_specs=[VMEM...]
    slice x1, local copies, waits for them, and re-layouts: 10.5 us -> 0.03 us  [body(): before = [before[:, at * depth:(at + 1) * depth] for at in range(3)]]
    unnamed x18 -> x16, local copies, waits for them, and re-layouts: 1.57 us -> 7.82 us
  transfers between devices with their start and end apart: 8 -> 22, of which waited for: 8 -> 13; matrix products, arithmetic and copies ran while one was open for 3% -> 2% of each run, Pallas kernels for 0% -> 13%
where the time goes in v2:
time: 91.3 us; the launch traced here: 91 us
  waiting for transfers between devices  33.9 us (37%)
  starting transfers between devices  28.6 us (31%)
  Pallas kernels  18.6 us (20%)
  local copies, waits for them, and re-layouts  7.92 us (9%)
  between operations  1.01 us (1%)
  other arithmetic  0.98 us (1%)
    ppermute x22, waiting for transfers between devices, move(): return lax.ppermute(value, ('row', 'col'), pairs)  33.9 us
    ppermute x22, starting transfers between devices, move(): return lax.ppermute(value, ('row', 'col'), pairs)  28.6 us
    pallas_call x16, Pallas kernels, call(): pl.pallas_call(kernel, out_shape=outs, in_specs=in_specs, out_specs=[VMEM...  18.6 us
    unnamed x16, local copies, waits for them, and re-layouts  7.82 us
  transfers between devices with their start and end apart: 22, of which 13 were waited for; matrix products, arithmetic and copies ran while one was open for 2% of the time, Pallas kernels for 13%

profile of v2, /device:TPU:0, one launch (start us, length us, event | category | flops | bytes accessed | tf_op | source)
XLA Modules:
  0.0 91.0 jit_solution(3800695541297384274)
XLA Ops:
  0.6 2.7 %shard_map.50 = (f32[48,384]{1,0:T(8,128)S(1)}, f32[48,1536]{1,0:T(8,128)S(1)}) custom-call(s32[1]{0:T(128)} %bitcast.keep_ref, f32[576,128]{1,0:T(8,128)} %bitcast.18, f32[4,384,1536]{2,1,0:T(8,128)} %refs_0_.5), custom_call_target="tpu_custom_call" | custom-call | flops 169869312 | bytes 368640 | tf_op jit(solution)/shard_map/pallas_call | solution.py:55
  3.9 1.7 %shard_map.51.refs_2_.refs_4_ = f32[4608,128]{1,0:T(8,128)S(1)} custom-call(f32[48,384]{1,0:T(8,128)S(1)} %get-tuple-element.10.token_ref, f32[4,4608,128]{2,1,0:T(8,128)} %bitcast.14), custom_call_target="tpu_custom_call" | custom-call | tf_op jit(solution)/shard_map/pallas_call | solution.py:55
  7.9 2.8 %collective-permute-start.3 = (f32[48,1536]{1,0:T(8,128)S(1)}, f32[48,1536]{1,0:T(8,128)S(1)}, u32[]{:S(2)}, u32[]{:S(2)}) collective-permute-start(f32[48,1536]{1,0:T(8,128)S(1)} %broadcast_select_fusion.2.token_ref.refs_0_), channel_id=1, source_target_pairs={{0,8},{1,25},{2,10},{3,27},{4,12},{5,29},{6,14},{7,31},{8,0},{9,17... | collective-permute-start | bytes 884744 | tf_op jit(solution)/shard_map/ppermute | solution.py:183
  10.7 2.7 %collective-permute-start.4 = (f32[48,768]{1,0:T(8,128)S(1)}, f32[48,768]{1,0:T(8,128)S(1)}, u32[]{:S(2)}, u32[]{:S(2)}) collective-permute-start(f32[48,768]{1,0:T(8,128)S(1)} %constant_dynamic-slice_fusion.5), channel_id=1, source_target_pairs={{0,16},{1,17},{2,18},{3,19},{4,20},{5,21},{6,22},{7,23},{8,24},{9,... | collective-permute-start | bytes 442376 | tf_op jit(solution)/shard_map/ppermute | solution.py:183
  13.3 2.4 %shard_map.54 = (f32[384,1536]{1,0:T(8,128)S(1)}, f32[4608,128]{1,0:T(8,128)S(1)}) custom-call(f32[48,1536]{1,0:T(8,128)S(1)} %broadcast_select_fusion.2.token_ref.refs_0_, f32[4,384,1536]{2,1,0:T(8,128)} %refs_0_.5, f32[4,4608,128]{2,1,0:T(8,128)} %bitcast.15), custom_call_target="tpu_custom_call" | custom-call | tf_op jit(solution)/shard_map/pallas_call | solution.py:55
  17.2 6.6 %collective-permute-done.4.refs_2_ = f32[48,768]{1,0:T(8,128)S(1)} collective-permute-done((f32[48,768]{1,0:T(8,128)S(1)}, f32[48,768]{1,0:T(8,128)S(1)}, u32[]{:S(2)}, u32[]{:S(2)}) %collective-permute-start.4) | collective-permute-done | bytes 147488 | tf_op jit(solution)/shard_map/ppermute | solution.py:183
  24.6 1.8 %collective-permute-start.5 = (f32[48,384]{1,0:T(8,128)S(1)}, f32[48,384]{1,0:T(8,128)S(1)}, u32[]{:S(2)}, u32[]{:S(2)}) collective-permute-start(f32[48,384]{1,0:T(8,128)S(1)} %shard_map.55), channel_id=1, source_target_pairs={{0,1},{1,0},{2,3},{3,2},{4,5},{5,4},{6,7},{7,6},{8,9},{9,8},{10,11... | collective-permute-start | bytes 221192 | tf_op jit(solution)/shard_map/ppermute | solution.py:183
  26.4 3.4 %collective-permute-start.2 = (f32[48,384]{1,0:T(8,128)S(1)}, f32[48,384]{1,0:T(8,128)S(1)}, u32[]{:S(2)}, u32[]{:S(2)}) collective-permute-start(f32[48,384]{1,0:T(8,128)S(1)} %shard_map.53), channel_id=1, source_target_pairs={{0,2},{1,3},{8,10},{9,11},{16,18},{17,19},{24,26},{25,27}} | collective-permute-start | bytes 221192 | tf_op jit(solution)/shard_map/ppermute | solution.py:183
  34.0 1.6 %collective-permute-done.7 = f32[48,1536]{1,0:T(8,128)S(1)} collective-permute-done((f32[48,1536]{1,0:T(8,128)S(1)}, f32[48,1536]{1,0:T(8,128)S(1)}, u32[]{:S(2)}, u32[]{:S(2)}) %collective-permute-start.7) | collective-permute-done | bytes 294944 | tf_op jit(solution)/shard_map/ppermute | solution.py:183
  35.7 3.1 %collective-permute-start.9 = (f32[48,768]{1,0:T(8,128)S(1)}, f32[48,768]{1,0:T(8,128)S(1)}, u32[]{:S(2)}, u32[]{:S(2)}) collective-permute-start(f32[48,768]{1,0:T(8,128)S(1)} %constant_dynamic-slice_fusion.4), channel_id=1, source_target_pairs={{0,16},{1,17},{2,18},{3,19},{4,20},{5,21},{6,22},{7,23},{8,24},{9,... | collective-permute-start | bytes 442376 | tf_op jit(solution)/shard_map/ppermute | solution.py:183
  38.8 2.4 %shard_map.58 = (f32[384,1536]{1,0:T(8,128)S(1)}, f32[4608,128]{1,0:T(8,128)S(1)}) custom-call(f32[48,1536]{1,0:T(8,128)S(1)} %broadcast_select_fusion.token_ref.refs_0_, f32[4,384,1536]{2,1,0:T(8,128)} %refs_0_.5, f32[4,4608,128]{2,1,0:T(8,128)} %bitcast.16), custom_call_target="tpu_custom_call" | custom-call | tf_op jit(solution)/shard_map/pallas_call | solution.py:55
  41.2 8.6 %collective-permute-done.9.refs_2_ = f32[48,768]{1,0:T(8,128)S(1)} collective-permute-done((f32[48,768]{1,0:T(8,128)S(1)}, f32[48,768]{1,0:T(8,128)S(1)}, u32[]{:S(2)}, u32[]{:S(2)}) %collective-permute-start.9) | collective-permute-done | bytes 147488 | tf_op jit(solution)/shard_map/ppermute | solution.py:183
  54.5 2.5 %collective-permute-start.12 = (f32[48,384]{1,0:T(8,128)S(1)}, f32[48,384]{1,0:T(8,128)S(1)}, u32[]{:S(2)}, u32[]{:S(2)}) collective-permute-start(f32[48,384]{1,0:T(8,128)S(1)} %shard_map.61), channel_id=1, source_target_pairs={{0,2},{1,3},{2,0},{3,1},{4,6},{5,7},{6,4},{7,5},{8,10},{9,11},{10,... | collective-permute-start | bytes 221192 | tf_op jit(solution)/shard_map/ppermute | solution.py:183
  57.0 2.8 %collective-permute-start.15 = (f32[48,768]{1,0:T(8,128)S(1)}, f32[48,768]{1,0:T(8,128)S(1)}, u32[]{:S(2)}, u32[]{:S(2)}) collective-permute-start(f32[48,768]{1,0:T(8,128)S(1)} %constant_dynamic-slice_fusion.3), channel_id=1, source_target_pairs={{0,16},{1,17},{2,18},{3,19},{4,20},{5,21},{6,22},{7,23},{8,24},{9,... | collective-permute-start | bytes 442376 | tf_op jit(solution)/shard_map/ppermute | solution.py:183
  60.5 2.4 %shard_map.62 = (f32[384,1536]{1,0:T(8,128)S(1)}, f32[4608,128]{1,0:T(8,128)S(1)}) custom-call(f32[48,1536]{1,0:T(8,128)S(1)} %broadcast_select_fusion.1.token_ref.refs_0_, f32[4,384,1536]{2,1,0:T(8,128)} %refs_0_.5, f32[4,4608,128]{2,1,0:T(8,128)} %bitcast.17), custom_call_target="tpu_custom_call" | custom-call | tf_op jit(solution)/shard_map/pallas_call | solution.py:55
  64.4 5.1 %collective-permute-done.15.refs_2_ = f32[48,768]{1,0:T(8,128)S(1)} collective-permute-done((f32[48,768]{1,0:T(8,128)S(1)}, f32[48,768]{1,0:T(8,128)S(1)}, u32[]{:S(2)}, u32[]{:S(2)}) %collective-permute-start.15) | collective-permute-done | bytes 147488 | tf_op jit(solution)/shard_map/ppermute | solution.py:183
  71.7 1.6 %collective-permute-start.17 = (f32[48,384]{1,0:T(8,128)S(1)}, f32[48,384]{1,0:T(8,128)S(1)}, u32[]{:S(2)}, u32[]{:S(2)}) collective-permute-start(f32[48,384]{1,0:T(8,128)S(1)} %add.39), channel_id=1, source_target_pairs={{0,2},{1,3},{2,0},{3,1},{4,6},{5,7},{6,4},{7,5},{8,10},{9,11},{10,... | collective-permute-start | bytes 221192 | tf_op jit(solution)/shard_map/ppermute | solution.py:183
  73.3 2.8 %collective-permute-done.17 = f32[48,384]{1,0:T(8,128)S(1)} collective-permute-done((f32[48,384]{1,0:T(8,128)S(1)}, f32[48,384]{1,0:T(8,128)S(1)}, u32[]{:S(2)}, u32[]{:S(2)}) %collective-permute-start.17) | collective-permute-done | bytes 73760 | tf_op jit(solution)/shard_map/ppermute | solution.py:183
  76.2 1.7 %copy-done.2 = f32[4608,128]{1,0:T(8,128)S(1)} copy-done((f32[4608,128]{1,0:T(8,128)S(1)}, f32[4608,128]{1,0:T(8,128)}, u32[]{:S(2)}) %copy-start.2) | copy-done | bytes 2359320
  77.9 1.7 %copy-done.4 = f32[4608,128]{1,0:T(8,128)S(1)} copy-done((f32[4608,128]{1,0:T(8,128)S(1)}, f32[4608,128]{1,0:T(8,128)}, u32[]{:S(2)}) %copy-start.4) | copy-done | bytes 2359320
  79.6 1.5 %shard_map.64.refs_1_ = f32[48,1536]{1,0:T(8,128)S(1)} custom-call(f32[48,384]{1,0:T(8,128)S(1)} %get-tuple-element.28.refs_0_, f32[48,384]{1,0:T(8,128)S(1)} %get-tuple-element.27.refs_1_, f32[48,384]{1,0:T(8,128)S(1)} %get-tuple-element.23.refs_2_, f32[48,1536]{1,0:T(8,128)S(1)} %get-tuple-element.11.refs_1_.refs_3_, ...), custom_call_target="tpu_custom_call" | custom-call | tf_op jit(solution)/shard_map/pallas_call | solution.py:55
  81.9 2.5 %collective-permute-start.19 = (f32[48,384]{1,0:T(8,128)S(1)}, f32[48,384]{1,0:T(8,128)S(1)}, u32[]{:S(2)}, u32[]{:S(2)}) collective-permute-start(f32[48,384]{1,0:T(8,128)S(1)} %get-tuple-element.20), channel_id=1, source_target_pairs={{0,24},{1,25},{2,26},{3,27},{4,28},{5,29},{6,30},{7,31},{8,16},{9,... | collective-permute-start | bytes 221192 | tf_op jit(solution)/shard_map/ppermute | solution.py:183
  84.4 2.0 %collective-permute-start.21 = (f32[48,384]{1,0:T(8,128)S(1)}, f32[48,384]{1,0:T(8,128)S(1)}, u32[]{:S(2)}, u32[]{:S(2)}) collective-permute-start(f32[48,384]{1,0:T(8,128)S(1)} %get-tuple-element.21), channel_id=1, source_target_pairs={{0,8},{1,9},{2,10},{3,11},{4,12},{5,13},{6,14},{7,15},{8,0},{9,1},... | collective-permute-start | bytes 221192 | tf_op jit(solution)/shard_map/ppermute | solution.py:183
  88.6 1.7 %collective-permute-done.20 = f32[48,384]{1,0:T(8,128)S(1)} collective-permute-done((f32[48,384]{1,0:T(8,128)S(1)}, f32[48,384]{1,0:T(8,128)S(1)}, u32[]{:S(2)}, u32[]{:S(2)}) %collective-permute-start.20) | collective-permute-done | bytes 73760 | tf_op jit(solution)/shard_map/ppermute | solution.py:183
  (73 shorter events, 22.1 us)
Async XLA Ops:
  3.4 2.2 %collective-permute-start = (f32[48,384]{1,0:T(8,128)S(1)}, f32[48,384]{1,0:T(8,128)S(1)}, u32[]{:S(2)}, u32[]{:S(2)}) collective-permute-start(f32[48,384]{1,0:T(8,128)S(1)} %get-tuple-element.10.token_ref), channel_id=1, source_target_pairs={{0,1},{1,0},{2,3},{3,2},{4,5},{5,4},{6,7},{7,6},{8,9},{9,8},{10,11... | collective-permute-start | bytes 221192 | tf_op jit(solution)/shard_map/ppermute | solution.py:183
  6.2 1.6 %collective-permute-start.1 = (f32[48,1536]{1,0:T(8,128)S(1)}, f32[48,1536]{1,0:T(8,128)S(1)}, u32[]{:S(2)}, u32[]{:S(2)}) collective-permute-start(f32[48,1536]{1,0:T(8,128)S(1)} %shard_map.52), channel_id=1, source_target_pairs={{0,1},{1,0},{2,3},{3,2},{4,5},{5,4},{6,7},{7,6},{8,9},{9,8},{10,11... | collective-permute-start | bytes 884744 | tf_op jit(solution)/shard_map/ppermute | solution.py:183
  7.9 15.9 %collective-permute-start.3 = (f32[48,1536]{1,0:T(8,128)S(1)}, f32[48,1536]{1,0:T(8,128)S(1)}, u32[]{:S(2)}, u32[]{:S(2)}) collective-permute-start(f32[48,1536]{1,0:T(8,128)S(1)} %broadcast_select_fusion.2.token_ref.refs_0_), channel_id=1, source_target_pairs={{0,8},{1,25},{2,10},{3,27},{4,12},{5,29},{6,14},{7,31},{8,0},{9,17... | collective-permute-start | bytes 884744 | tf_op jit(solution)/shard_map/ppermute | solution.py:183
  10.7 13.1 %collective-permute-start.4 = (f32[48,768]{1,0:T(8,128)S(1)}, f32[48,768]{1,0:T(8,128)S(1)}, u32[]{:S(2)}, u32[]{:S(2)}) collective-permute-start(f32[48,768]{1,0:T(8,128)S(1)} %constant_dynamic-slice_fusion.5), channel_id=1, source_target_pairs={{0,16},{1,17},{2,18},{3,19},{4,20},{5,21},{6,22},{7,23},{8,24},{9,... | collective-permute-start | bytes 442376 | tf_op jit(solution)/shard_map/ppermute | solution.py:183
  24.6 5.3 %collective-permute-start.5 = (f32[48,384]{1,0:T(8,128)S(1)}, f32[48,384]{1,0:T(8,128)S(1)}, u32[]{:S(2)}, u32[]{:S(2)}) collective-permute-start(f32[48,384]{1,0:T(8,128)S(1)} %shard_map.55), channel_id=1, source_target_pairs={{0,1},{1,0},{2,3},{3,2},{4,5},{5,4},{6,7},{7,6},{8,9},{9,8},{10,11... | collective-permute-start | bytes 221192 | tf_op jit(solution)/shard_map/ppermute | solution.py:183
  26.4 5.5 %collective-permute-start.2 = (f32[48,384]{1,0:T(8,128)S(1)}, f32[48,384]{1,0:T(8,128)S(1)}, u32[]{:S(2)}, u32[]{:S(2)}) collective-permute-start(f32[48,384]{1,0:T(8,128)S(1)} %shard_map.53), channel_id=1, source_target_pairs={{0,2},{1,3},{8,10},{9,11},{16,18},{17,19},{24,26},{25,27}} | collective-permute-start | bytes 221192 | tf_op jit(solution)/shard_map/ppermute | solution.py:183
  29.8 3.4 %copy-start.1 = (f32[4608,128]{1,0:T(8,128)S(1)}, f32[4608,128]{1,0:T(8,128)}, u32[]{:S(2)}) copy-start(f32[4608,128]{1,0:T(8,128)} %copy-done) | copy-start | bytes 7077892
  29.9 3.4 %collective-permute-start.6 = (f32[48,384]{1,0:T(8,128)S(1)}, f32[48,384]{1,0:T(8,128)S(1)}, u32[]{:S(2)}, u32[]{:S(2)}) collective-permute-start(f32[48,384]{1,0:T(8,128)S(1)} %add.37), channel_id=1, source_target_pairs={{0,2},{1,3},{8,10},{9,11},{16,18},{17,19},{24,26},{25,27}} | collective-permute-start | bytes 221192 | tf_op jit(solution)/shard_map/ppermute | solution.py:183
  33.9 1.6 %collective-permute-start.7 = (f32[48,1536]{1,0:T(8,128)S(1)}, f32[48,1536]{1,0:T(8,128)S(1)}, u32[]{:S(2)}, u32[]{:S(2)}) collective-permute-start(f32[48,1536]{1,0:T(8,128)S(1)} %shard_map.57.refs_1_), channel_id=1, source_target_pairs={{0,1},{1,0},{2,3},{3,2},{4,5},{5,4},{6,7},{7,6},{8,9},{9,8},{10,11... | collective-permute-start | bytes 884744 | tf_op jit(solution)/shard_map/ppermute | solution.py:183
  35.6 14.2 %collective-permute-start.8 = (f32[48,1536]{1,0:T(8,128)S(1)}, f32[48,1536]{1,0:T(8,128)S(1)}, u32[]{:S(2)}, u32[]{:S(2)}) collective-permute-start(f32[48,1536]{1,0:T(8,128)S(1)} %broadcast_select_fusion.token_ref.refs_0_), channel_id=1, source_target_pairs={{0,8},{1,25},{2,10},{3,27},{4,12},{5,29},{6,14},{7,31},{8,0},{9,17... | collective-permute-start | bytes 884744 | tf_op jit(solution)/shard_map/ppermute | solution.py:183
  35.7 14.1 %collective-permute-start.9 = (f32[48,768]{1,0:T(8,128)S(1)}, f32[48,768]{1,0:T(8,128)S(1)}, u32[]{:S(2)}, u32[]{:S(2)}) collective-permute-start(f32[48,768]{1,0:T(8,128)S(1)} %constant_dynamic-slice_fusion.4), channel_id=1, source_target_pairs={{0,16},{1,17},{2,18},{3,19},{4,20},{5,21},{6,22},{7,23},{8,24},{9,... | collective-permute-start | bytes 442376 | tf_op jit(solution)/shard_map/ppermute | solution.py:183
  41.2 11.5 %copy-start.3 = (f32[4608,128]{1,0:T(8,128)}, f32[4608,128]{1,0:T(8,128)S(1)}, u32[]{:S(2)}) copy-start(f32[4608,128]{1,0:T(8,128)S(1)} %get-tuple-element.15.refs_2_.refs_6_) | copy-start | bytes 7077892
  50.7 1.4 %collective-permute-start.10 = (f32[48,384]{1,0:T(8,128)S(1)}, f32[48,384]{1,0:T(8,128)S(1)}, u32[]{:S(2)}, u32[]{:S(2)}) collective-permute-start(f32[48,384]{1,0:T(8,128)S(1)} %shard_map.59), channel_id=1, source_target_pairs={{0,1},{1,0},{2,3},{3,2},{4,5},{5,4},{6,7},{7,6},{8,9},{9,8},{10,11... | collective-permute-start | bytes 221192 | tf_op jit(solution)/shard_map/ppermute | solution.py:183
  52.7 1.6 %collective-permute-start.11 = (f32[48,1536]{1,0:T(8,128)S(1)}, f32[48,1536]{1,0:T(8,128)S(1)}, u32[]{:S(2)}, u32[]{:S(2)}) collective-permute-start(f32[48,1536]{1,0:T(8,128)S(1)} %shard_map.60), channel_id=1, source_target_pairs={{0,1},{1,0},{2,3},{3,2},{4,5},{5,4},{6,7},{7,6},{8,9},{9,8},{10,11... | collective-permute-start | bytes 884744 | tf_op jit(solution)/shard_map/ppermute | solution.py:183
  54.4 15.1 %collective-permute-start.14 = (f32[48,1536]{1,0:T(8,128)S(1)}, f32[48,1536]{1,0:T(8,128)S(1)}, u32[]{:S(2)}, u32[]{:S(2)}) collective-permute-start(f32[48,1536]{1,0:T(8,128)S(1)} %broadcast_select_fusion.1.token_ref.refs_0_), channel_id=1, source_target_pairs={{0,8},{1,25},{2,10},{3,27},{4,12},{5,29},{6,14},{7,31},{8,0},{9,17... | collective-permute-start | bytes 884744 | tf_op jit(solution)/shard_map/ppermute | solution.py:183
  54.5 5.3 %collective-permute-start.12 = (f32[48,384]{1,0:T(8,128)S(1)}, f32[48,384]{1,0:T(8,128)S(1)}, u32[]{:S(2)}, u32[]{:S(2)}) collective-permute-start(f32[48,384]{1,0:T(8,128)S(1)} %shard_map.61), channel_id=1, source_target_pairs={{0,2},{1,3},{2,0},{3,1},{4,6},{5,7},{6,4},{7,5},{8,10},{9,11},{10,... | collective-permute-start | bytes 221192 | tf_op jit(solution)/shard_map/ppermute | solution.py:183
  57.0 12.5 %collective-permute-start.15 = (f32[48,768]{1,0:T(8,128)S(1)}, f32[48,768]{1,0:T(8,128)S(1)}, u32[]{:S(2)}, u32[]{:S(2)}) collective-permute-start(f32[48,768]{1,0:T(8,128)S(1)} %constant_dynamic-slice_fusion.3), channel_id=1, source_target_pairs={{0,16},{1,17},{2,18},{3,19},{4,20},{5,21},{6,22},{7,23},{8,24},{9,... | collective-permute-start | bytes 442376 | tf_op jit(solution)/shard_map/ppermute | solution.py:183
  60.5 12.8 %collective-permute-start.13 = (f32[48,1152]{1,0:T(8,128)}, f32[48,1152]{1,0:T(8,128)}, u32[]{:S(2)}, u32[]{:S(2)}) collective-permute-start(f32[48,1152]{1,0:T(8,128)} %pad_maximum_fusion.1), channel_id=1, source_target_pairs={{0,4},{1,5},{2,6},{3,7},{4,0},{5,1},{6,2},{7,3},{8,12},{9,13},{10,... | collective-permute-start | bytes 663560 | tf_op jit(solution)/shard_map/ppermute | solution.py:183
  70.3 1.3 %collective-permute-start.16 = (f32[48,384]{1,0:T(8,128)S(1)}, f32[48,384]{1,0:T(8,128)S(1)}, u32[]{:S(2)}, u32[]{:S(2)}) collective-permute-start(f32[48,384]{1,0:T(8,128)S(1)} %shard_map.63), channel_id=1, source_target_pairs={{0,1},{1,0},{2,3},{3,2},{4,5},{5,4},{6,7},{7,6},{8,9},{9,8},{10,11... | collective-permute-start | bytes 221192 | tf_op jit(solution)/shard_map/ppermute | solution.py:183
  71.7 4.4 %collective-permute-start.17 = (f32[48,384]{1,0:T(8,128)S(1)}, f32[48,384]{1,0:T(8,128)S(1)}, u32[]{:S(2)}, u32[]{:S(2)}) collective-permute-start(f32[48,384]{1,0:T(8,128)S(1)} %add.39), channel_id=1, source_target_pairs={{0,2},{1,3},{2,0},{3,1},{4,6},{5,7},{6,4},{7,5},{8,10},{9,11},{10,... | collective-permute-start | bytes 221192 | tf_op jit(solution)/shard_map/ppermute | solution.py:183
  76.1 5.0 %collective-permute-start.18 = (f32[48,384]{1,0:T(8,128)S(1)}, f32[48,384]{1,0:T(8,128)S(1)}, u32[]{:S(2)}, u32[]{:S(2)}) collective-permute-start(f32[48,384]{1,0:T(8,128)S(1)} %broadcast_select_fusion.5), channel_id=1, source_target_pairs={{0,4},{1,5},{2,6},{3,7},{4,0},{5,1},{6,2},{7,3},{8,12},{9,13},{10,... | collective-permute-start | bytes 221192 | tf_op jit(solution)/shard_map/ppermute | solution.py:183
  81.9 6.7 %collective-permute-start.19 = (f32[48,384]{1,0:T(8,128)S(1)}, f32[48,384]{1,0:T(8,128)S(1)}, u32[]{:S(2)}, u32[]{:S(2)}) collective-permute-start(f32[48,384]{1,0:T(8,128)S(1)} %get-tuple-element.20), channel_id=1, source_target_pairs={{0,24},{1,25},{2,26},{3,27},{4,28},{5,29},{6,30},{7,31},{8,16},{9,... | collective-permute-start | bytes 221192 | tf_op jit(solution)/shard_map/ppermute | solution.py:183
  84.3 5.9 %collective-permute-start.20 = (f32[48,384]{1,0:T(8,128)S(1)}, f32[48,384]{1,0:T(8,128)S(1)}, u32[]{:S(2)}, u32[]{:S(2)}) collective-permute-start(f32[48,384]{1,0:T(8,128)S(1)} %get-tuple-element.22), channel_id=1, source_target_pairs={{0,16},{1,17},{2,18},{3,19},{4,20},{5,21},{6,22},{7,23},{8,24},{9,... | collective-permute-start | bytes 221192 | tf_op jit(solution)/shard_map/ppermute | solution.py:183
  84.4 5.9 %collective-permute-start.21 = (f32[48,384]{1,0:T(8,128)S(1)}, f32[48,384]{1,0:T(8,128)S(1)}, u32[]{:S(2)}, u32[]{:S(2)}) collective-permute-start(f32[48,384]{1,0:T(8,128)S(1)} %get-tuple-element.21), channel_id=1, source_target_pairs={{0,8},{1,9},{2,10},{3,11},{4,12},{5,13},{6,14},{7,15},{8,0},{9,1},... | collective-permute-start | bytes 221192 | tf_op jit(solution)/shard_map/ppermute | solution.py:183
  (5 other events, 7.9 us)

commit v3 on v2

--- a/solution.py
+++ b/solution.py
@@ -14,7 +14,7 @@
 SMEM = pl.BlockSpec(memory_space=pltpu.SMEM)
 ANY = pl.BlockSpec(memory_space=pl.ANY)
 HBM = pl.BlockSpec(memory_space=pltpu.HBM)
-PARAMS = pltpu.CompilerParams(vmem_limit_bytes=8 * 2**20)
+PARAMS = pltpu.CompilerParams(vmem_limit_bytes=12 * 2**20)
 
 
 def split(value):
@@ -77,33 +77,37 @@
         copy.wait()
 
 
-def first_step(keep, heads, inverse_blocks, count):
+def first_step(keep, heads, inverse_blocks, blocks, count):
     rows, length = inverse_blocks.shape[1:]
     stride = heads.shape[0] // count
-    pieces = 3 if rows % (3 * LANES) == 0 else 1
-    size = rows // pieces
-
-    def kernel(keep_ref, heads_ref, inverse_ref, out_ref, kept_ref, heads_here, inverse_here, sems):
+    pieces = 3
+    size = length // pieces
+
+    def kernel(keep_ref, heads_ref, inverse_ref, blocks_ref, out_ref, kept_ref, block_ref, heads_here, inverse_here, sems):
         copies = [pltpu.make_async_copy(heads_ref, heads_here, sems.at[pieces])]
         for at in range(pieces):
             piece = pl.ds(at * size, size)
-            copies.append(pltpu.make_async_copy(inverse_ref.at[0, piece], inverse_here.at[piece], sems.at[at]))
-        start(copies)
+            copies.append(pltpu.make_async_copy(inverse_ref.at[0, :, piece], inverse_here.at[:, piece], sems.at[at]))
+        later = chunked(blocks_ref.at[0], block_ref, sems, pieces + 1)
+        start(copies + later)
         copies[0].wait()
         value = columns(heads_here, 0, stride * LANES, count)
         kept_ref[...] = jnp.where(keep_ref[0] == 1, value, 0.0)
+        total = jnp.zeros((count, rows), F32)
         for at in range(pieces):
             piece = slice(at * size, (at + 1) * size)
             copies[at + 1].wait()
-            out_ref[:, piece] = product(value, inverse_here[piece, :], ((1,), (1,)))
+            total = total + product(value[:, piece], inverse_here[:, piece], ((1,), (1,)))
+        out_ref[...] = total
+        finish(later)
 
     return call(
         kernel,
-        [shape(count, rows), shape(count, length)],
-        [keep, heads, inverse_blocks],
-        [SMEM, HBM, HBM],
+        [shape(count, rows), shape(count, length), shape(*blocks.shape[1:])],
+        [keep, heads, inverse_blocks, blocks],
+        [SMEM, HBM, HBM, HBM],
         6 * count * rows * length,
-        [pltpu.VMEM(heads.shape, F32), pltpu.VMEM((rows, length), F32), pltpu.SemaphoreType.DMA((pieces + 1,))],
+        [pltpu.VMEM(heads.shape, F32), pltpu.VMEM((rows, length), F32), pltpu.SemaphoreType.DMA((pieces + 5,))],
     )
 
 
@@ -114,14 +118,20 @@
     return call(kernel, [shape(*value.shape)], [token, value], [ANY, VMEM])[0]
 
 
+def chunked(source, target, sems, first, pieces=4):
+    size = target.shape[0] // pieces
+    parts = [pl.ds(at * size, size) for at in range(pieces)]
+    return [pltpu.make_async_copy(source.at[part], target.at[part], sems.at[first + at]) for at, part in enumerate(parts)]
+
+
 def load(token, arrays):
     wanted = [(at, index) for at, (_, indices) in enumerate(arrays) for index in indices]
 
     def kernel(token_ref, *refs):
         ins, outs, sems = refs[: len(arrays)], refs[len(arrays) : -1], refs[-1]
-        copies = [
-            pltpu.make_async_copy(ins[at].at[index], out, sems.at[n]) for n, ((at, index), out) in enumerate(zip(wanted, outs))
-        ]
+        copies = []
+        for (at, index), out in zip(wanted, outs):
+            copies += chunked(ins[at].at[index], out, sems, len(copies))
         start(copies)
         finish(copies)
 
@@ -130,29 +140,66 @@
         [shape(*arrays[at][0].shape[1:]) for at, _ in wanted],
         [token] + [array for array, _ in arrays],
         [ANY] + [HBM] * len(arrays),
-        scratch=[pltpu.SemaphoreType.DMA((len(wanted),))],
+        scratch=[pltpu.SemaphoreType.DMA((4 * len(wanted),))],
     )
 
 
-def update(solved, base, blocks, urgent=True):
+def update_from(token, solved, base, blocks, indices):
+    many = len(solved)
+
+    def kernel(*refs):
+        solved_refs, base_ref, blocks_ref, _, out_ref, here, sems = refs[:many], *refs[many:]
+        copies = [chunked(blocks_ref.at[index], here.at[at], sems, 4 * at) for at, index in enumerate(indices)]
+        for copy in copies:
+            start(copy)
+        for copy in copies:
+            finish(copy)
+        subtract_products([ref[...] for ref in solved_refs], base_ref, [here.at[at] for at in range(many)], out_ref)
+
+    return call(
+        kernel,
+        [shape(*base.shape)],
+        list(solved) + [base, blocks, token],
+        [VMEM] * (many + 1) + [HBM, ANY],
+        scratch=[pltpu.VMEM((many,) + blocks.shape[1:], F32), pltpu.SemaphoreType.DMA((4 * many,))],
+    )[0]
+
+
+def update(solved, base, blocks):
     many = len(solved)
 
     def kernel(*refs):
         subtract_products([ref[...] for ref in refs[:many]], refs[many], refs[many + 1 : -1], refs[-1])
 
-    flops = 6 * base.size * sum(value.shape[1] for value in solved) if urgent else 0
+    flops = 6 * base.size * sum(value.shape[1] for value in solved)
     ins = list(solved) + [base] + list(blocks)
     return call(kernel, [shape(*base.shape)], ins, [VMEM] * len(ins), flops)[0]
 
 
-def gather_apply(odd, own, fulls, halves, inverse):
+def add_rows(parts):
+    count, length = parts[0].shape
+    many = length // LANES
+    if many * LANES != length:
+        return sum(parts)
+
+    def kernel(*refs):
+        total = refs[0][...]
+        for ref in refs[1:-1]:
+            total = total + ref[...]
+        for at in range(many):
+            refs[-1][pl.ds(at, count, stride=many), :] = total[:, at * LANES : (at + 1) * LANES]
+
+    return call(kernel, [shape(count * many, LANES)], parts, [VMEM] * len(parts), parts[0].size)[0]
+
+
+def gather_apply(odd, own, fulls, halves, inverse, hold):
     count, length = own.shape
     rows = inverse.shape[0]
 
     def kernel(odd_ref, *refs):
         odd = odd_ref[0]
-        own_ref, rest = refs[0], refs[1:-2]
-        inverse_ref, out_ref = refs[-2:]
+        own_ref, rest = refs[0], refs[1 : -2 - len(hold)]
+        inverse_ref, out_ref = refs[-2 - len(hold)], refs[-1]
         value = jnp.where(odd == 1, 0.0, own_ref[...])
         for ref in rest[: len(fulls)]:
             value = value + ref[...]
@@ -163,7 +210,8 @@
         out_ref[...] = product(value, inverse_ref[...], ((1,), (1,)))
 
     ins = [own] + fulls + halves + [inverse]
-    return call(kernel, [shape(count, rows)], [odd.reshape(1)] + ins, [SMEM] + [VMEM] * len(ins), 6 * own.size * rows)[0]
+    specs = [SMEM] + [VMEM] * len(ins) + [ANY] * len(hold)
+    return call(kernel, [shape(count, rows)], [odd.reshape(1)] + ins + hold, specs, 6 * own.size * rows)[0]
 
 
 def body(rows, cols, panel, inverse_blocks, right_side):
@@ -195,11 +243,13 @@
     middle = offsets.pop(len(offsets) // 2) if offsets else 0
     first, second = offsets[0::2], offsets[1::2]
 
-    def sum_apply(total, part, inverse):
+    def sum_apply(total, part, inverse, hold):
         fulls = [move(total, lambda z, q: (z ^ (b if q % 2 else a), q)) for a, b in zip(first, second)]
         halves = [move(part, lambda z, q: (z ^ middle, q))] if middle else []
-        piece = gather_apply(odd, total, fulls, halves, inverse)
-        return piece + swap_core(piece)
+        return gather_apply(odd, total, fulls, halves, inverse, hold)
+
+    def add_cores(value):
+        return value + swap_core(value)
 
     half = length // 2
     blocks = panel.reshape(steps, depth * length // LANES, LANES)
@@ -207,46 +257,66 @@
     inverse_blocks = pltpu.with_memory_space_constraint(inverse_blocks, pltpu.HBM)
     heads = pltpu.with_memory_space_constraint(right_side.reshape(count * length // LANES, LANES), pltpu.HBM)
 
-    def to_right(value):
-        return jnp.where(is_right, move(value, lambda z, q: (z, q ^ 2), (0, 1)), value)
+    def across(value, bit):
+        return move(value, lambda z, q: (z, q ^ bit))
+
+    def from_chip(value, source):
+        kept = value
+        for bit in range(cols - 2, 0, -2):
+            moved = move(value, lambda z, q: (z, q ^ bit), (source & ~1, source | 1))
+            kept = jnp.where(((col ^ source) & ~1) == bit, moved, kept)
+        return kept
+
+    def on_right(here, moved):
+        return jnp.where(is_right, moved, here)
 
     keep = jnp.where(row == 0, 1, 0).astype(jnp.int32).reshape(1)
-    own_piece, start_value = first_step(keep, heads, inverse_blocks, count)
+    own_piece, start_value, block_0 = first_step(keep, heads, inverse_blocks, blocks, count)
     x_0 = jnp.where(is_odd, swap_core(own_piece), own_piece)
-    (block_0,) = load(own_piece, [(blocks, (0,))])
 
     def on_chip(total, step):
         total = jnp.where(is_odd == (step % 2 == 1), total, swap_core(total))
         return total, lax.dynamic_slice_in_dim(total, odd * half, half, 1)
 
-    own_total = update([x_0], start_value, [block_0])
-    total, part = on_chip(own_total, 1)
-    inverse_1, block_1 = load(total, [(inverse_blocks, (1,)), (blocks, (1,))])
-    x_0 = to_right(after(total, x_0))
-    early = update([x_0], start_value, [block_0], False)
-    x_1 = to_right(sum_apply(total, part, inverse_1))
-
-    own_total = update([x_1], early, [block_1])
+    total, part = on_chip(update([x_0], start_value, [block_0]), 1)
+    moved = across(after(total, x_0), 2)
+    (inverse,) = load(moved, [(inverse_blocks, (1,))])
+    piece = sum_apply(total, part, inverse, [moved])
+    x_0 = on_right(x_0, moved)
+    (block_1,) = load(piece, [(blocks, (1,))])
+    x_1 = add_cores(piece)
+    x_1 = on_right(x_1, across(x_1, 2))
+
+    own_total = update([x_0, x_1], start_value, [block_0, block_1])
     total, part = on_chip(own_total, 2)
-    inverse_2, block_2 = load(total, [(inverse_blocks, (2,)), (blocks, (2,))])
-    x_2 = sum_apply(total, part, inverse_2)
-
-    own_total = update([x_2], own_total, [block_2])
-    total, part = on_chip(own_total, 3)
-    inverse_3, block_3 = load(total, [(inverse_blocks, (3,)), (blocks, (3,))])
-    x_2 = spread(after(total, x_2), 2, bits[:1])
-    before = spread(jnp.concatenate([x_0, x_1, x_2], axis=1), 2, bits[1:])
-    before = [before[:, at * depth : (at + 1) * depth] for at in range(3)]
-    accum = update(before, start_value, [block_0, block_1, block_2], False)
-    x_3 = spread(sum_apply(total, part, inverse_3), 2, bits)
+    first_two = after(total, jnp.concatenate([x_0, x_1], axis=1))
+    moved = across(first_two, 4)
+    (inverse,) = load(moved, [(inverse_blocks, (2,))])
+    piece = sum_apply(total, part, inverse, [moved])
+    first_two = jnp.where((col & 4) != 0, moved, first_two)
+    first_two = spread(first_two, 0, bits[2:])
+    (block_2,) = load(piece, [(blocks, (2,))])
+    x_2 = add_cores(piece)
+
+    total, part = on_chip(update([x_2], own_total, [block_2]), 3)
+    moved = across(after(total, x_2), 2)
+    x_0, x_1 = first_two[:, :depth], first_two[:, depth:]
+    accum = update_from(total, [x_0, x_1], start_value, blocks, [0, 1])
+    (inverse,) = load(accum, [(inverse_blocks, (3,))])
+    piece = sum_apply(total, part, inverse, [moved])
+    x_2 = spread(jnp.where(is_right, x_2, moved), 2, bits[1:])
+    block_2, block_3 = load(piece, [(blocks, (2, 3))])
+    x_3 = from_chip(add_cores(piece), 3)
+    accum = update([x_2], accum, [block_2])
     accum = update([x_3], accum, [block_3])
 
     size = length // rows
     chunk = lambda at: lax.dynamic_slice_in_dim(accum, at * size, size, 1)
-    updated = chunk(row)
+    parts = [chunk(row)]
     for offset in range(rows - 1, 0, -1):
-        updated = updated + move(chunk(row ^ offset), lambda z, q: (z ^ offset, q))
-    return jnp.stack(before + [x_3], axis=1), updated[:, None, None, :]
+        parts.append(move(chunk(row ^ offset), lambda z, q: (z ^ offset, q)))
+    updated = add_rows(parts).reshape(count, 1, 1, size)
+    return jnp.stack([x_0, x_1, x_2, x_3], axis=1), updated
 
 
 def solution(mesh):

time: 91.3 us -> 88 us (0.964)
  local copies, waits for them, and re-layouts: 7.92 us -> 0.92 us
  Pallas kernels: 18.6 us -> 23.2 us
  waiting for transfers between devices: 33.9 us -> 30.7 us
  starting transfers between devices: 28.6 us -> 30.7 us
    unnamed x16 -> x1, local copies, waits for them, and re-layouts: 7.82 us -> 0.83 us
    pallas_call x16 -> x20, Pallas kernels: 18.6 us -> 23.2 us  [call(): pl.pallas_call(kernel, out_shape=outs, in_specs=in_specs, out_specs=[VMEM...]
    ppermute x22 -> x24, waiting for transfers between devices: 33.9 us -> 30.7 us  [move(): return lax.ppermute(value, ('row', 'col'), pairs)]
    ppermute x22 -> x24, starting transfers between devices: 28.6 us -> 30.7 us  [move(): return lax.ppermute(value, ('row', 'col'), pairs)]
  transfers between devices with their start and end apart: 22 -> 24, of which waited for: 13 -> 14; matrix products, arithmetic and copies ran while one was open for 2% -> 1% of each run, Pallas kernels for 13% -> 17%
where the time goes in v3:
time: 88 us; the launch traced here: 86.8 us
  starting transfers between devices  30.7 us (35%)
  waiting for transfers between devices  30.7 us (35%)
  Pallas kernels  23.2 us (26%)
  between operations  0.93 us (1%)
  local copies, waits for them, and re-layouts  0.92 us (1%)
    ppermute x24, waiting for transfers between devices, move(): return lax.ppermute(value, ('row', 'col'), pairs)  30.7 us
    ppermute x24, starting transfers between devices, move(): return lax.ppermute(value, ('row', 'col'), pairs)  30.7 us
    pallas_call x20, Pallas kernels, call(): pl.pallas_call(kernel, out_shape=outs, in_specs=in_specs, out_specs=[VMEM...  23.2 us
  transfers between devices with their start and end apart: 24, of which 14 were waited for; matrix products, arithmetic and copies ran while one was open for 1% of the time, Pallas kernels for 17%

profile of v3, /device:TPU:0, one launch (start us, length us, event | category | flops | bytes accessed | tf_op | source)
XLA Modules:
  0.0 86.8 jit_solution(11487840609284429756)
XLA Ops:
  0.6 2.5 %shard_map.50 = (f32[48,384]{1,0:T(8,128)S(1)}, f32[48,1536]{1,0:T(8,128)S(1)}, f32[4608,128]{1,0:T(8,128)S(1)}) custom-call(s32[1]{0:T(128)} %bitcast.keep_ref, f32[576,128]{1,0:T(8,128)} %bitcast.18, f32[4,384,1536]{2,1,0:T(8,128)} %refs_0_.5, f32[4,4608,128]{2,1,0:T(8,128)} %bitcast.13), custom_call_target="tpu_custom_call" | custom-call | flops 169869312 | bytes 2727936 | tf_op jit(solution)/shard_map/pallas_call | solution.py:55
  6.9 3.0 %collective-permute-start.3 = (f32[48,1536]{1,0:T(8,128)S(1)}, f32[48,1536]{1,0:T(8,128)S(1)}, u32[]{:S(2)}, u32[]{:S(2)}) collective-permute-start(f32[48,1536]{1,0:T(8,128)S(1)} %broadcast_select_fusion.1.token_ref.refs_0_), channel_id=1, source_target_pairs={{0,8},{1,25},{2,10},{3,27},{4,12},{5,29},{6,14},{7,31},{8,0},{9,17... | collective-permute-start | bytes 884744 | tf_op jit(solution)/shard_map/ppermute | solution.py:231
  9.9 2.7 %collective-permute-start.4 = (f32[48,768]{1,0:T(8,128)S(1)}, f32[48,768]{1,0:T(8,128)S(1)}, u32[]{:S(2)}, u32[]{:S(2)}) collective-permute-start(f32[48,768]{1,0:T(8,128)S(1)} %constant_dynamic-slice_fusion.6), channel_id=1, source_target_pairs={{0,16},{1,17},{2,18},{3,19},{4,20},{5,21},{6,22},{7,23},{8,24},{9,... | collective-permute-start | bytes 442376 | tf_op jit(solution)/shard_map/ppermute | solution.py:231
  12.5 1.5 %collective-permute-start.2 = (f32[48,384]{1,0:T(8,128)S(1)}, f32[48,384]{1,0:T(8,128)S(1)}, u32[]{:S(2)}, u32[]{:S(2)}) collective-permute-start(f32[48,384]{1,0:T(8,128)S(1)} %shard_map.52), channel_id=1, source_target_pairs={{0,2},{1,3},{2,0},{3,1},{4,6},{5,7},{6,4},{7,5},{8,10},{9,11},{10,... | collective-permute-start | bytes 221192 | tf_op jit(solution)/shard_map/ppermute | solution.py:231
  14.0 2.9 %collective-permute-done.2.token_ref.refs_4_ = f32[48,384]{1,0:T(8,128)S(1)} collective-permute-done((f32[48,384]{1,0:T(8,128)S(1)}, f32[48,384]{1,0:T(8,128)S(1)}, u32[]{:S(2)}, u32[]{:S(2)}) %collective-permute-start.2) | collective-permute-done | bytes 73760 | tf_op jit(solution)/shard_map/ppermute | solution.py:231
  16.9 1.6 %shard_map.53.refs_3_ = f32[384,1536]{1,0:T(8,128)S(1)} custom-call(f32[48,384]{1,0:T(8,128)S(1)} %collective-permute-done.2.token_ref.refs_4_, f32[4,384,1536]{2,1,0:T(8,128)} %refs_0_.5), custom_call_target="tpu_custom_call" | custom-call | tf_op jit(solution)/shard_map/pallas_call | solution.py:55
  18.5 4.2 %collective-permute-done.4.refs_2_ = f32[48,768]{1,0:T(8,128)S(1)} collective-permute-done((f32[48,768]{1,0:T(8,128)S(1)}, f32[48,768]{1,0:T(8,128)S(1)}, u32[]{:S(2)}, u32[]{:S(2)}) %collective-permute-start.4) | collective-permute-done | bytes 147488 | tf_op jit(solution)/shard_map/ppermute | solution.py:231
  23.6 1.8 %collective-permute-start.5 = (f32[48,384]{1,0:T(8,128)S(1)}, f32[48,384]{1,0:T(8,128)S(1)}, u32[]{:S(2)}, u32[]{:S(2)}) collective-permute-start(f32[48,384]{1,0:T(8,128)S(1)} %shard_map.54.token_ref), channel_id=1, source_target_pairs={{0,1},{1,0},{2,3},{3,2},{4,5},{5,4},{6,7},{7,6},{8,9},{9,8},{10,11... | collective-permute-start | bytes 221192 | tf_op jit(solution)/shard_map/ppermute | solution.py:231
  26.3 1.6 %collective-permute-start.6 = (f32[48,384]{1,0:T(8,128)S(1)}, f32[48,384]{1,0:T(8,128)S(1)}, u32[]{:S(2)}, u32[]{:S(2)}) collective-permute-start(f32[48,384]{1,0:T(8,128)S(1)} %add.28), channel_id=1, source_target_pairs={{0,2},{1,3},{2,0},{3,1},{4,6},{5,7},{6,4},{7,5},{8,10},{9,11},{10,... | collective-permute-start | bytes 221192 | tf_op jit(solution)/shard_map/ppermute | solution.py:231
  27.9 1.6 %shard_map.55.refs_4_ = f32[4608,128]{1,0:T(8,128)S(1)} custom-call(f32[48,384]{1,0:T(8,128)S(1)} %shard_map.54.token_ref, f32[4,4608,128]{2,1,0:T(8,128)} %bitcast.14), custom_call_target="tpu_custom_call" | custom-call | tf_op jit(solution)/shard_map/pallas_call | solution.py:55
  32.1 1.6 %collective-permute-done.7 = f32[48,1536]{1,0:T(8,128)S(1)} collective-permute-done((f32[48,1536]{1,0:T(8,128)S(1)}, f32[48,1536]{1,0:T(8,128)S(1)}, u32[]{:S(2)}, u32[]{:S(2)}) %collective-permute-start.7) | collective-permute-done | bytes 294944 | tf_op jit(solution)/shard_map/ppermute | solution.py:231
  33.9 1.6 %collective-permute-start.8 = (f32[48,768]{1,0:T(8,128)S(1)}, f32[48,768]{1,0:T(8,128)S(1)}, u32[]{:S(2)}, u32[]{:S(2)}) collective-permute-start(f32[48,768]{1,0:T(8,128)S(1)} %shard_map.57), channel_id=1, source_target_pairs={{0,4},{1,5},{2,6},{3,7},{4,0},{5,1},{6,2},{7,3},{8,12},{9,13},{10,... | collective-permute-start | bytes 442376 | tf_op jit(solution)/shard_map/ppermute | solution.py:231
  35.5 3.1 %collective-permute-start.10 = (f32[48,768]{1,0:T(8,128)S(1)}, f32[48,768]{1,0:T(8,128)S(1)}, u32[]{:S(2)}, u32[]{:S(2)}) collective-permute-start(f32[48,768]{1,0:T(8,128)S(1)} %constant_dynamic-slice_fusion.5), channel_id=1, source_target_pairs={{0,16},{1,17},{2,18},{3,19},{4,20},{5,21},{6,22},{7,23},{8,24},{9,... | collective-permute-start | bytes 442376 | tf_op jit(solution)/shard_map/ppermute | solution.py:231
  39.3 1.6 %shard_map.58.refs_3_ = f32[384,1536]{1,0:T(8,128)S(1)} custom-call(f32[48,768]{1,0:T(8,128)S(1)} %collective-permute-done.8.token_ref.refs_4_, f32[4,384,1536]{2,1,0:T(8,128)} %refs_0_.5), custom_call_target="tpu_custom_call" | custom-call | tf_op jit(solution)/shard_map/pallas_call | solution.py:55
  40.9 7.3 %collective-permute-done.10.refs_2_ = f32[48,768]{1,0:T(8,128)S(1)} collective-permute-done((f32[48,768]{1,0:T(8,128)S(1)}, f32[48,768]{1,0:T(8,128)S(1)}, u32[]{:S(2)}, u32[]{:S(2)}) %collective-permute-start.10) | collective-permute-done | bytes 147488 | tf_op jit(solution)/shard_map/ppermute | solution.py:231
  49.4 1.6 %shard_map.60.refs_2_ = f32[4608,128]{1,0:T(8,128)S(1)} custom-call(f32[48,384]{1,0:T(8,128)S(1)} %shard_map.59.token_ref, f32[4,4608,128]{2,1,0:T(8,128)} %bitcast.15), custom_call_target="tpu_custom_call" | custom-call | tf_op jit(solution)/shard_map/pallas_call | solution.py:55
  53.5 3.4 %collective-permute-start.16 = (f32[48,768]{1,0:T(8,128)S(1)}, f32[48,768]{1,0:T(8,128)S(1)}, u32[]{:S(2)}, u32[]{:S(2)}) collective-permute-start(f32[48,768]{1,0:T(8,128)S(1)} %constant_dynamic-slice_fusion.4), channel_id=1, source_target_pairs={{0,16},{1,17},{2,18},{3,19},{4,20},{5,21},{6,22},{7,23},{8,24},{9,... | collective-permute-start | bytes 442376 | tf_op jit(solution)/shard_map/ppermute | solution.py:231
  58.4 3.5 %shard_map.63.token_ref.refs_1_ = f32[48,1536]{1,0:T(8,128)S(1)} custom-call(f32[48,384]{1,0:T(8,128)S(1)} %get-tuple-element.21.refs_0_, f32[48,384]{1,0:T(8,128)S(1)} %get-tuple-element.20.refs_1_, f32[48,1536]{1,0:T(8,128)S(1)} %get-tuple-element.8.refs_1_.refs_2_, f32[4,4608,128]{2,1,0:T(8,128)} %bitcast.16, ...), custom_call_target="tpu_custom_call" | custom-call | tf_op jit(solution)/shard_map/pallas_call | solution.py:55
  61.9 1.6 %shard_map.64.refs_3_ = f32[384,1536]{1,0:T(8,128)S(1)} custom-call(f32[48,1536]{1,0:T(8,128)S(1)} %shard_map.63.token_ref.refs_1_, f32[4,384,1536]{2,1,0:T(8,128)} %refs_0_.5), custom_call_target="tpu_custom_call" | custom-call | tf_op jit(solution)/shard_map/pallas_call | solution.py:55
  63.6 4.2 %collective-permute-done.16.refs_2_ = f32[48,768]{1,0:T(8,128)S(1)} collective-permute-done((f32[48,768]{1,0:T(8,128)S(1)}, f32[48,768]{1,0:T(8,128)S(1)}, u32[]{:S(2)}, u32[]{:S(2)}) %collective-permute-start.16) | collective-permute-done | bytes 147488 | tf_op jit(solution)/shard_map/ppermute | solution.py:231
  73.7 2.4 %shard_map.66 = (f32[4608,128]{1,0:T(8,128)S(1)}, f32[4608,128]{1,0:T(8,128)S(1)}) custom-call(f32[48,384]{1,0:T(8,128)S(1)} %shard_map.65.token_ref, f32[4,4608,128]{2,1,0:T(8,128)} %bitcast.17), custom_call_target="tpu_custom_call" | custom-call | tf_op jit(solution)/shard_map/pallas_call | solution.py:55
  77.4 2.4 %collective-permute-start.21 = (f32[48,384]{1,0:T(8,128)S(1)}, f32[48,384]{1,0:T(8,128)S(1)}, u32[]{:S(2)}, u32[]{:S(2)}) collective-permute-start(f32[48,384]{1,0:T(8,128)S(1)} %get-tuple-element.16), channel_id=1, source_target_pairs={{0,24},{1,25},{2,26},{3,27},{4,28},{5,29},{6,30},{7,31},{8,16},{9,... | collective-permute-start | bytes 221192 | tf_op jit(solution)/shard_map/ppermute | solution.py:231
  79.8 2.1 %collective-permute-start.23 = (f32[48,384]{1,0:T(8,128)S(1)}, f32[48,384]{1,0:T(8,128)S(1)}, u32[]{:S(2)}, u32[]{:S(2)}) collective-permute-start(f32[48,384]{1,0:T(8,128)S(1)} %get-tuple-element.14), channel_id=1, source_target_pairs={{0,8},{1,9},{2,10},{3,11},{4,12},{5,13},{6,14},{7,15},{8,0},{9,1},... | collective-permute-start | bytes 221192 | tf_op jit(solution)/shard_map/ppermute | solution.py:231
  83.9 2.2 %collective-permute-done.22.refs_2_ = f32[48,384]{1,0:T(8,128)S(1)} collective-permute-done((f32[48,384]{1,0:T(8,128)S(1)}, f32[48,384]{1,0:T(8,128)S(1)}, u32[]{:S(2)}, u32[]{:S(2)}) %collective-permute-start.22) | collective-permute-done | bytes 73760 | tf_op jit(solution)/shard_map/ppermute | solution.py:231
  (65 shorter events, 23.9 us)
Async XLA Ops:
  3.1 1.4 %collective-permute-start = (f32[48,384]{1,0:T(8,128)S(1)}, f32[48,384]{1,0:T(8,128)S(1)}, u32[]{:S(2)}, u32[]{:S(2)}) collective-permute-start(f32[48,384]{1,0:T(8,128)S(1)} %get-tuple-element.7), channel_id=1, source_target_pairs={{0,1},{1,0},{2,3},{3,2},{4,5},{5,4},{6,7},{7,6},{8,9},{9,8},{10,11... | collective-permute-start | bytes 221192 | tf_op jit(solution)/shard_map/ppermute | solution.py:231
  5.2 1.6 %collective-permute-start.1 = (f32[48,1536]{1,0:T(8,128)S(1)}, f32[48,1536]{1,0:T(8,128)S(1)}, u32[]{:S(2)}, u32[]{:S(2)}) collective-permute-start(f32[48,1536]{1,0:T(8,128)S(1)} %shard_map.51), channel_id=1, source_target_pairs={{0,1},{1,0},{2,3},{3,2},{4,5},{5,4},{6,7},{7,6},{8,9},{9,8},{10,11... | collective-permute-start | bytes 884744 | tf_op jit(solution)/shard_map/ppermute | solution.py:231
  6.9 15.9 %collective-permute-start.3 = (f32[48,1536]{1,0:T(8,128)S(1)}, f32[48,1536]{1,0:T(8,128)S(1)}, u32[]{:S(2)}, u32[]{:S(2)}) collective-permute-start(f32[48,1536]{1,0:T(8,128)S(1)} %broadcast_select_fusion.1.token_ref.refs_0_), channel_id=1, source_target_pairs={{0,8},{1,25},{2,10},{3,27},{4,12},{5,29},{6,14},{7,31},{8,0},{9,17... | collective-permute-start | bytes 884744 | tf_op jit(solution)/shard_map/ppermute | solution.py:231
  9.9 12.9 %collective-permute-start.4 = (f32[48,768]{1,0:T(8,128)S(1)}, f32[48,768]{1,0:T(8,128)S(1)}, u32[]{:S(2)}, u32[]{:S(2)}) collective-permute-start(f32[48,768]{1,0:T(8,128)S(1)} %constant_dynamic-slice_fusion.6), channel_id=1, source_target_pairs={{0,16},{1,17},{2,18},{3,19},{4,20},{5,21},{6,22},{7,23},{8,24},{9,... | collective-permute-start | bytes 442376 | tf_op jit(solution)/shard_map/ppermute | solution.py:231
  12.5 4.4 %collective-permute-start.2 = (f32[48,384]{1,0:T(8,128)S(1)}, f32[48,384]{1,0:T(8,128)S(1)}, u32[]{:S(2)}, u32[]{:S(2)}) collective-permute-start(f32[48,384]{1,0:T(8,128)S(1)} %shard_map.52), channel_id=1, source_target_pairs={{0,2},{1,3},{2,0},{3,1},{4,6},{5,7},{6,4},{7,5},{8,10},{9,11},{10,... | collective-permute-start | bytes 221192 | tf_op jit(solution)/shard_map/ppermute | solution.py:231
  23.6 2.7 %collective-permute-start.5 = (f32[48,384]{1,0:T(8,128)S(1)}, f32[48,384]{1,0:T(8,128)S(1)}, u32[]{:S(2)}, u32[]{:S(2)}) collective-permute-start(f32[48,384]{1,0:T(8,128)S(1)} %shard_map.54.token_ref), channel_id=1, source_target_pairs={{0,1},{1,0},{2,3},{3,2},{4,5},{5,4},{6,7},{7,6},{8,9},{9,8},{10,11... | collective-permute-start | bytes 221192 | tf_op jit(solution)/shard_map/ppermute | solution.py:231
  26.3 4.6 %collective-permute-start.6 = (f32[48,384]{1,0:T(8,128)S(1)}, f32[48,384]{1,0:T(8,128)S(1)}, u32[]{:S(2)}, u32[]{:S(2)}) collective-permute-start(f32[48,384]{1,0:T(8,128)S(1)} %add.28), channel_id=1, source_target_pairs={{0,2},{1,3},{2,0},{3,1},{4,6},{5,7},{6,4},{7,5},{8,10},{9,11},{10,... | collective-permute-start | bytes 221192 | tf_op jit(solution)/shard_map/ppermute | solution.py:231
  32.1 1.6 %collective-permute-start.7 = (f32[48,1536]{1,0:T(8,128)S(1)}, f32[48,1536]{1,0:T(8,128)S(1)}, u32[]{:S(2)}, u32[]{:S(2)}) collective-permute-start(f32[48,1536]{1,0:T(8,128)S(1)} %shard_map.56.refs_1_), channel_id=1, source_target_pairs={{0,1},{1,0},{2,3},{3,2},{4,5},{5,4},{6,7},{7,6},{8,9},{9,8},{10,11... | collective-permute-start | bytes 884744 | tf_op jit(solution)/shard_map/ppermute | solution.py:231
  33.7 14.4 %collective-permute-start.9 = (f32[48,1536]{1,0:T(8,128)S(1)}, f32[48,1536]{1,0:T(8,128)S(1)}, u32[]{:S(2)}, u32[]{:S(2)}) collective-permute-start(f32[48,1536]{1,0:T(8,128)S(1)} %broadcast_select_fusion.2.token_ref.refs_0_), channel_id=1, source_target_pairs={{0,8},{1,25},{2,10},{3,27},{4,12},{5,29},{6,14},{7,31},{8,0},{9,17... | collective-permute-start | bytes 884744 | tf_op jit(solution)/shard_map/ppermute | solution.py:231
  33.9 5.4 %collective-permute-start.8 = (f32[48,768]{1,0:T(8,128)S(1)}, f32[48,768]{1,0:T(8,128)S(1)}, u32[]{:S(2)}, u32[]{:S(2)}) collective-permute-start(f32[48,768]{1,0:T(8,128)S(1)} %shard_map.57), channel_id=1, source_target_pairs={{0,4},{1,5},{2,6},{3,7},{4,0},{5,1},{6,2},{7,3},{8,12},{9,13},{10,... | collective-permute-start | bytes 442376 | tf_op jit(solution)/shard_map/ppermute | solution.py:231
  35.5 12.7 %collective-permute-start.10 = (f32[48,768]{1,0:T(8,128)S(1)}, f32[48,768]{1,0:T(8,128)S(1)}, u32[]{:S(2)}, u32[]{:S(2)}) collective-permute-start(f32[48,768]{1,0:T(8,128)S(1)} %constant_dynamic-slice_fusion.5), channel_id=1, source_target_pairs={{0,16},{1,17},{2,18},{3,19},{4,20},{5,21},{6,22},{7,23},{8,24},{9,... | collective-permute-start | bytes 442376 | tf_op jit(solution)/shard_map/ppermute | solution.py:231
  49.1 2.0 %collective-permute-start.11 = (f32[48,384]{1,0:T(8,128)S(1)}, f32[48,384]{1,0:T(8,128)S(1)}, u32[]{:S(2)}, u32[]{:S(2)}) collective-permute-start(f32[48,384]{1,0:T(8,128)S(1)} %shard_map.59.token_ref), channel_id=1, source_target_pairs={{0,1},{1,0},{2,3},{3,2},{4,5},{5,4},{6,7},{7,6},{8,9},{9,8},{10,11... | collective-permute-start | bytes 221192 | tf_op jit(solution)/shard_map/ppermute | solution.py:231
  51.7 1.6 %collective-permute-start.12 = (f32[48,1536]{1,0:T(8,128)S(1)}, f32[48,1536]{1,0:T(8,128)S(1)}, u32[]{:S(2)}, u32[]{:S(2)}) collective-permute-start(f32[48,1536]{1,0:T(8,128)S(1)} %shard_map.61), channel_id=1, source_target_pairs={{0,1},{1,0},{2,3},{3,2},{4,5},{5,4},{6,7},{7,6},{8,9},{9,8},{10,11... | collective-permute-start | bytes 884744 | tf_op jit(solution)/shard_map/ppermute | solution.py:231
  53.4 14.4 %collective-permute-start.15 = (f32[48,1536]{1,0:T(8,128)S(1)}, f32[48,1536]{1,0:T(8,128)S(1)}, u32[]{:S(2)}, u32[]{:S(2)}) collective-permute-start(f32[48,1536]{1,0:T(8,128)S(1)} %broadcast_select_fusion.token_ref.refs_4_.refs_0_), channel_id=1, source_target_pairs={{0,8},{1,25},{2,10},{3,27},{4,12},{5,29},{6,14},{7,31},{8,0},{9,17... | collective-permute-start | bytes 884744 | tf_op jit(solution)/shard_map/ppermute | solution.py:231
  53.5 14.3 %collective-permute-start.16 = (f32[48,768]{1,0:T(8,128)S(1)}, f32[48,768]{1,0:T(8,128)S(1)}, u32[]{:S(2)}, u32[]{:S(2)}) collective-permute-start(f32[48,768]{1,0:T(8,128)S(1)} %constant_dynamic-slice_fusion.4), channel_id=1, source_target_pairs={{0,16},{1,17},{2,18},{3,19},{4,20},{5,21},{6,22},{7,23},{8,24},{9,... | collective-permute-start | bytes 442376 | tf_op jit(solution)/shard_map/ppermute | solution.py:231
  56.9 6.6 %collective-permute-start.13 = (f32[48,384]{1,0:T(8,128)S(1)}, f32[48,384]{1,0:T(8,128)S(1)}, u32[]{:S(2)}, u32[]{:S(2)}) collective-permute-start(f32[48,384]{1,0:T(8,128)S(1)} %shard_map.62), channel_id=1, source_target_pairs={{0,2},{1,3},{2,0},{3,1},{4,6},{5,7},{6,4},{7,5},{8,10},{9,11},{10,... | collective-permute-start | bytes 221192 | tf_op jit(solution)/shard_map/ppermute | solution.py:231
  68.6 1.7 %collective-permute-start.17 = (f32[48,384]{1,0:T(8,128)S(1)}, f32[48,384]{1,0:T(8,128)S(1)}, u32[]{:S(2)}, u32[]{:S(2)}) collective-permute-start(f32[48,384]{1,0:T(8,128)S(1)} %shard_map.65.token_ref), channel_id=1, source_target_pairs={{0,1},{1,0},{2,3},{3,2},{4,5},{5,4},{6,7},{7,6},{8,9},{9,8},{10,11... | collective-permute-start | bytes 221192 | tf_op jit(solution)/shard_map/ppermute | solution.py:231
  69.3 4.4 %collective-permute-start.14 = (f32[48,384]{1,0:T(8,128)S(1)}, f32[48,384]{1,0:T(8,128)S(1)}, u32[]{:S(2)}, u32[]{:S(2)}) collective-permute-start(f32[48,384]{1,0:T(8,128)S(1)} %broadcast_select_fusion.6), channel_id=1, source_target_pairs={{0,4},{1,5},{2,6},{3,7},{4,0},{5,1},{6,2},{7,3},{8,12},{9,13},{10,... | collective-permute-start | bytes 221192 | tf_op jit(solution)/shard_map/ppermute | solution.py:231
  70.4 6.3 %collective-permute-start.18 = (f32[48,384]{1,0:T(8,128)S(1)}, f32[48,384]{1,0:T(8,128)S(1)}, u32[]{:S(2)}, u32[]{:S(2)}) collective-permute-start(f32[48,384]{1,0:T(8,128)S(1)} %add.30), channel_id=1, source_target_pairs={{2,0},{3,1},{10,8},{11,9},{18,16},{19,17},{26,24},{27,25}} | collective-permute-start | bytes 221192 | tf_op jit(solution)/shard_map/ppermute | solution.py:231
  71.7 5.0 %collective-permute-start.19 = (f32[48,384]{1,0:T(8,128)S(1)}, f32[48,384]{1,0:T(8,128)S(1)}, u32[]{:S(2)}, u32[]{:S(2)}) collective-permute-start(f32[48,384]{1,0:T(8,128)S(1)} %add.30), channel_id=1, source_target_pairs={{2,6},{3,7},{10,14},{11,15},{18,22},{19,23},{26,30},{27,31}} | collective-permute-start | bytes 221192 | tf_op jit(solution)/shard_map/ppermute | solution.py:231
  72.3 4.4 %collective-permute-start.20 = (f32[48,384]{1,0:T(8,128)S(1)}, f32[48,384]{1,0:T(8,128)S(1)}, u32[]{:S(2)}, u32[]{:S(2)}) collective-permute-start(f32[48,384]{1,0:T(8,128)S(1)} %add.30), channel_id=1, source_target_pairs={{2,4},{3,5},{10,12},{11,13},{18,20},{19,21},{26,28},{27,29}} | collective-permute-start | bytes 221192 | tf_op jit(solution)/shard_map/ppermute | solution.py:231
  77.4 6.5 %collective-permute-start.21 = (f32[48,384]{1,0:T(8,128)S(1)}, f32[48,384]{1,0:T(8,128)S(1)}, u32[]{:S(2)}, u32[]{:S(2)}) collective-permute-start(f32[48,384]{1,0:T(8,128)S(1)} %get-tuple-element.16), channel_id=1, source_target_pairs={{0,24},{1,25},{2,26},{3,27},{4,28},{5,29},{6,30},{7,31},{8,16},{9,... | collective-permute-start | bytes 221192 | tf_op jit(solution)/shard_map/ppermute | solution.py:231
  79.8 6.3 %collective-permute-start.22 = (f32[48,384]{1,0:T(8,128)S(1)}, f32[48,384]{1,0:T(8,128)S(1)}, u32[]{:S(2)}, u32[]{:S(2)}) collective-permute-start(f32[48,384]{1,0:T(8,128)S(1)} %get-tuple-element.15), channel_id=1, source_target_pairs={{0,16},{1,17},{2,18},{3,19},{4,20},{5,21},{6,22},{7,23},{8,24},{9,... | collective-permute-start | bytes 221192 | tf_op jit(solution)/shard_map/ppermute | solution.py:231
  79.8 6.3 %collective-permute-start.23 = (f32[48,384]{1,0:T(8,128)S(1)}, f32[48,384]{1,0:T(8,128)S(1)}, u32[]{:S(2)}, u32[]{:S(2)}) collective-permute-start(f32[48,384]{1,0:T(8,128)S(1)} %get-tuple-element.14), channel_id=1, source_target_pairs={{0,8},{1,9},{2,10},{3,11},{4,12},{5,13},{6,14},{7,15},{8,0},{9,1},... | collective-permute-start | bytes 221192 | tf_op jit(solution)/shard_map/ppermute | solution.py:231

commit v4 on v3

--- a/solution.py
+++ b/solution.py
@@ -50,8 +50,8 @@
         out_ref[:, at] = total
 
 
-def call(kernel, outs, ins, in_specs, flops=0, scratch=()):
-    moved = sum(4 * out.size for out in outs) if flops else 0
+def call(kernel, outs, ins, in_specs, flops=0, scratch=(), read=0):
+    moved = 4 * read + sum(4 * out.size for out in outs) if flops or read else 0
     return pl.pallas_call(
         kernel,
         out_shape=outs,
@@ -112,10 +112,7 @@
 
 
 def after(token, value):
-    def kernel(token_ref, value_ref, out_ref):
-        out_ref[...] = value_ref[...]
-
-    return call(kernel, [shape(*value.shape)], [token, value], [ANY, VMEM])[0]
+    return lax.optimization_barrier((token, value))[1]
 
 
 def chunked(source, target, sems, first, pieces=4):
@@ -144,24 +141,50 @@
     )
 
 
-def update_from(token, solved, base, blocks, indices):
+def update_from(token, own, solved, bases, panels, indices, read=0):
     many = len(solved)
 
-    def kernel(*refs):
-        solved_refs, base_ref, blocks_ref, _, out_ref, here, sems = refs[:many], *refs[many:]
-        copies = [chunked(blocks_ref.at[index], here.at[at], sems, 4 * at) for at, index in enumerate(indices)]
-        for copy in copies:
-            start(copy)
-        for copy in copies:
-            finish(copy)
-        subtract_products([ref[...] for ref in solved_refs], base_ref, [here.at[at] for at in range(many)], out_ref)
-
-    return call(
-        kernel,
-        [shape(*base.shape)],
-        list(solved) + [base, blocks, token],
-        [VMEM] * (many + 1) + [HBM, ANY],
-        scratch=[pltpu.VMEM((many,) + blocks.shape[1:], F32), pltpu.SemaphoreType.DMA((4 * many,))],
+    def kernel(own_ref, *refs):
+        solved_refs, base_ref, other_base_ref, panel_ref, other_panel_ref, _, out_ref, here, sems = refs[:many], *refs[many:]
+
+        def run(base_ref, panel_ref):
+            copies = [chunked(panel_ref.at[index], here.at[at], sems, 4 * at) for at, index in enumerate(indices)]
+            for copy in copies:
+                start(copy)
+            for copy in copies:
+                finish(copy)
+            subtract_products([ref[...] for ref in solved_refs], base_ref, [here.at[at] for at in range(many)], out_ref)
+
+        pl.when(own_ref[0] == 1)(lambda: run(base_ref, panel_ref))
+        pl.when(own_ref[0] != 1)(lambda: run(other_base_ref, other_panel_ref))
+
+    return call(
+        kernel,
+        [shape(*bases[0].shape)],
+        [own.reshape(1)] + list(solved) + list(bases) + list(panels) + [token],
+        [SMEM] + [VMEM] * (many + 2) + [HBM, HBM, ANY],
+        scratch=[pltpu.VMEM((many,) + panels[0].shape[1:], F32), pltpu.SemaphoreType.DMA((4 * many,))],
+        read=read,
+    )[0]
+
+
+def load_either(token, own, panels, index, read=0):
+    def kernel(token_ref, own_ref, panel_ref, other_panel_ref, out_ref, sems):
+        def run(panel_ref):
+            copies = chunked(panel_ref.at[index], out_ref, sems, 0)
+            start(copies)
+            finish(copies)
+
+        pl.when(own_ref[0] == 1)(lambda: run(panel_ref))
+        pl.when(own_ref[0] != 1)(lambda: run(other_panel_ref))
+
+    return call(
+        kernel,
+        [shape(*panels[0].shape[1:])],
+        [token, own.reshape(1)] + list(panels),
+        [ANY, SMEM, HBM, HBM],
+        scratch=[pltpu.SemaphoreType.DMA((4,))],
+        read=read,
     )[0]
 
 
@@ -174,6 +197,27 @@
     flops = 6 * base.size * sum(value.shape[1] for value in solved)
     ins = list(solved) + [base] + list(blocks)
     return call(kernel, [shape(*base.shape)], ins, [VMEM] * len(ins), flops)[0]
+
+
+def update_part(odd, choice, solved, base, block):
+    count, length = base.shape
+    half = length // 2
+
+    def kernel(odd_ref, choice_ref, *refs):
+        base_ref, block_ref, out_ref, part_ref = refs[-4:]
+        value = refs[0][...]
+        for at, ref in enumerate(refs[1:-4]):
+            value = jnp.where(choice_ref[0] == at + 1, ref[...], value)
+        subtract_products([value], base_ref, [block_ref], out_ref)
+        part_ref[...] = jnp.where(odd_ref[0] == 1, out_ref[:, half:], out_ref[:, :half])
+
+    return call(
+        kernel,
+        [shape(count, length), shape(count, half)],
+        [odd.reshape(1), choice.reshape(1), *solved, base, block],
+        [SMEM] * 2 + [VMEM] * (len(solved) + 2),
+        6 * base.size * solved[0].shape[1],
+    )
 
 
 def add_rows(parts):
@@ -218,8 +262,8 @@
     steps, depth, _, _, length = panel.shape
     count = right_side.shape[0]
     row, col = lax.axis_index("row"), lax.axis_index("col")
-    odd = lax.rem(col, 2)
-    is_odd, is_right = odd == 1, lax.rem(col // 2, 2) == 1
+    odd, side = lax.rem(col, 2), lax.rem(col // 2, 2)
+    is_odd, is_right = odd == 1, side == 1
     bits = [1 << at for at in range(1, cols.bit_length() - 1)]
 
     def move(value, target, senders=range(cols)):
@@ -278,30 +322,34 @@
         total = jnp.where(is_odd == (step % 2 == 1), total, swap_core(total))
         return total, lax.dynamic_slice_in_dim(total, odd * half, half, 1)
 
+    even = 1 - odd
+
+    starts = [start_value, swap_core(after(x_0, start_value))]
+    even = 1 - odd
     total, part = on_chip(update([x_0], start_value, [block_0]), 1)
+    panels = [blocks, pltpu.with_memory_space_constraint(swap_core(after(total, panel.reshape(blocks.shape))), pltpu.HBM)]
     moved = across(after(total, x_0), 2)
     (inverse,) = load(moved, [(inverse_blocks, (1,))])
     piece = sum_apply(total, part, inverse, [moved])
     x_0 = on_right(x_0, moved)
-    (block_1,) = load(piece, [(blocks, (1,))])
+    block = load_either(piece, even, panels, 1, blocks.size)
+    base = update_from(piece, even, [x_0], starts, panels, [0], blocks.size)
     x_1 = add_cores(piece)
-    x_1 = on_right(x_1, across(x_1, 2))
-
-    own_total = update([x_0, x_1], start_value, [block_0, block_1])
-    total, part = on_chip(own_total, 2)
-    first_two = after(total, jnp.concatenate([x_0, x_1], axis=1))
-    moved = across(first_two, 4)
-    (inverse,) = load(moved, [(inverse_blocks, (2,))])
-    piece = sum_apply(total, part, inverse, [moved])
-    first_two = jnp.where((col & 4) != 0, moved, first_two)
-    first_two = spread(first_two, 0, bits[2:])
-    (block_2,) = load(piece, [(blocks, (2,))])
+    moved = across(x_1, 2)
+
+    total, part = update_part(odd, side, [x_1, moved], base, block)
+    x_1 = on_right(x_1, moved)
+    base = update_from(total, odd, [x_0, x_1], starts, panels, [0, 1])
+    moved = [across(after(total, x), 4) for x in (x_0, x_1)]
+    (inverse,) = load(moved[1], [(inverse_blocks, (2,))])
+    piece = sum_apply(total, part, inverse, [base] + moved)
+    block = load_either(piece, odd, panels, 2, blocks.size)
+    x_0, x_1 = [spread(jnp.where((col & 4) != 0, far, x), 0, bits[2:]) for x, far in zip((x_0, x_1), moved)]
     x_2 = add_cores(piece)
 
-    total, part = on_chip(update([x_2], own_total, [block_2]), 3)
+    total, part = update_part(odd, side, [x_2], base, block)
     moved = across(after(total, x_2), 2)
-    x_0, x_1 = first_two[:, :depth], first_two[:, depth:]
-    accum = update_from(total, [x_0, x_1], start_value, blocks, [0, 1])
+    accum = update_from(total, jnp.ones_like(odd), [x_0, x_1], starts, panels, [0, 1])
     (inverse,) = load(accum, [(inverse_blocks, (3,))])
     piece = sum_apply(total, part, inverse, [moved])
     x_2 = spread(jnp.where(is_right, x_2, moved), 2, bits[1:])

time: 88 us -> 84.9 us (0.965)
  waiting for transfers between devices: 30.7 us -> 23.8 us
  Pallas kernels: 23.2 us -> 28.3 us
  starting transfers between devices: 30.7 us -> 29.6 us
    ppermute x24 -> x25, waiting for transfers between devices: 30.7 us -> 23.8 us  [move(): return lax.ppermute(value, ('row', 'col'), pairs)]
    pallas_call x20 -> x19, Pallas kernels: 23.2 us -> 28.3 us  [call(): pl.pallas_call(kernel, out_shape=outs, in_specs=in_specs, out_specs=[VMEM...]
    ppermute x24 -> x25, starting transfers between devices: 30.7 us -> 29.6 us  [move(): return lax.ppermute(value, ('row', 'col'), pairs)]
  transfers between devices with their start and end apart: 24 -> 25, of which waited for: 14 -> 11; matrix products, arithmetic and copies ran while one was open for 1% -> 1% of each run, Pallas kernels for 17% -> 25%
where the time goes in v4:
time: 84.9 us; the launch traced here: 83.6 us
  starting transfers between devices  29.6 us (35%)
  Pallas kernels  28.3 us (33%)
  waiting for transfers between devices  23.8 us (28%)
  between operations  0.94 us (1%)
  local copies, waits for them, and re-layouts  0.88 us (1%)
    ppermute x25, starting transfers between devices, move(): return lax.ppermute(value, ('row', 'col'), pairs)  29.6 us
    pallas_call x19, Pallas kernels, call(): pl.pallas_call(kernel, out_shape=outs, in_specs=in_specs, out_specs=[VMEM...  28.3 us
    ppermute x25, waiting for transfers between devices, move(): return lax.ppermute(value, ('row', 'col'), pairs)  23.8 us
  transfers between devices with their start and end apart: 25, of which 11 were waited for; matrix products, arithmetic and copies ran while one was open for 1% of the time, Pallas kernels for 25%

profile of v4, /device:TPU:0, one launch (start us, length us, event | category | flops | bytes accessed | tf_op | source)
XLA Modules:
  0.0 83.6 jit_solution(11905297131543878380)
XLA Ops:
  0.6 2.5 %shard_map.50 = (f32[48,384]{1,0:T(8,128)S(1)}, f32[48,1536]{1,0:T(8,128)S(1)}, f32[4608,128]{1,0:T(8,128)S(1)}) custom-call(s32[1]{0:T(128)} %bitcast.2.keep_ref, f32[576,128]{1,0:T(8,128)} %bitcast.23, f32[4,384,1536]{2,1,0:T(8,128)} %refs_0_.5, f32[4,4608,128]{2,1,0:T(8,128)} %bitcast.15), custom_call_target="tpu_custom_call" | custom-call | flops 169869312 | bytes 2727936 | tf_op jit(solution)/shard_map/pallas_call | solution.py:55
  7.3 2.7 %collective-permute-start.2 = (f32[48,1536]{1,0:T(8,128)S(1)}, f32[48,1536]{1,0:T(8,128)S(1)}, u32[]{:S(2)}, u32[]{:S(2)}) collective-permute-start(f32[48,1536]{1,0:T(8,128)S(1)} %broadcast_select_fusion.refs_0_), channel_id=1, source_target_pairs={{0,8},{1,25},{2,10},{3,27},{4,12},{5,29},{6,14},{7,31},{8,0},{9,17... | collective-permute-start | bytes 884744 | tf_op jit(solution)/shard_map/ppermute | solution.py:275
  10.0 2.7 %collective-permute-start.3 = (f32[48,768]{1,0:T(8,128)S(1)}, f32[48,768]{1,0:T(8,128)S(1)}, u32[]{:S(2)}, u32[]{:S(2)}) collective-permute-start(f32[48,768]{1,0:T(8,128)S(1)} %constant_dynamic-slice_fusion.4), channel_id=1, source_target_pairs={{0,16},{1,17},{2,18},{3,19},{4,20},{5,21},{6,22},{7,23},{8,24},{9,... | collective-permute-start | bytes 442376 | tf_op jit(solution)/shard_map/ppermute | solution.py:275
  14.2 2.9 %collective-permute-done.4.token_ref.refs_4_ = f32[48,384]{1,0:T(8,128)S(1)} collective-permute-done((f32[48,384]{1,0:T(8,128)S(1)}, f32[48,384]{1,0:T(8,128)S(1)}, u32[]{:S(2)}, u32[]{:S(2)}) %collective-permute-start.4) | collective-permute-done | bytes 73760 | tf_op jit(solution)/shard_map/ppermute | solution.py:275
  17.0 1.6 %shard_map.52.refs_3_ = f32[384,1536]{1,0:T(8,128)S(1)} custom-call(f32[48,384]{1,0:T(8,128)S(1)} %collective-permute-done.4.token_ref.refs_4_, f32[4,384,1536]{2,1,0:T(8,128)} %refs_0_.5), custom_call_target="tpu_custom_call" | custom-call | tf_op jit(solution)/shard_map/pallas_call | solution.py:55
  18.7 4.4 %collective-permute-done.3.refs_2_ = f32[48,768]{1,0:T(8,128)S(1)} collective-permute-done((f32[48,768]{1,0:T(8,128)S(1)}, f32[48,768]{1,0:T(8,128)S(1)}, u32[]{:S(2)}, u32[]{:S(2)}) %collective-permute-start.3) | collective-permute-done | bytes 147488 | tf_op jit(solution)/shard_map/ppermute | solution.py:275
  23.9 1.8 %collective-permute-start.5 = (f32[48,384]{1,0:T(8,128)S(1)}, f32[48,384]{1,0:T(8,128)S(1)}, u32[]{:S(2)}, u32[]{:S(2)}) collective-permute-start(f32[48,384]{1,0:T(8,128)S(1)} %shard_map.53.refs_5_.token_ref), channel_id=1, source_target_pairs={{0,1},{1,0},{2,3},{3,2},{4,5},{5,4},{6,7},{7,6},{8,9},{9,8},{10,11... | collective-permute-start | bytes 221192 | tf_op jit(solution)/shard_map/ppermute | solution.py:275
  28.2 1.6 %shard_map.55.refs_3_ = f32[4608,128]{1,0:T(8,128)S(1)} custom-call(f32[48,384]{1,0:T(8,128)S(1)} %shard_map.53.refs_5_.token_ref, s32[1]{0:T(128)} %bitcast.5.own_ref, f32[4,4608,128]{2,1,0:T(8,128)} %bitcast.17, f32[4,4608,128]{2,1,0:T(8,128)} %collective-permute-done.8.refs_4_.other_panel_ref.refs_5_), custom_call_target="tpu_custom_call" | custom-call | bytes 11796480 | tf_op jit(solution)/shard_map/pallas_call | solution.py:55
  29.9 2.2 %shard_map.54.refs_2_ = f32[48,1536]{1,0:T(8,128)S(1)} custom-call(s32[1]{0:T(128)} %bitcast.5.own_ref, f32[48,384]{1,0:T(8,128)S(1)} %broadcast_select_fusion.4.refs_0_, f32[48,1536]{1,0:T(8,128)S(1)} %get-tuple-element.21.refs_1_.refs_2_, f32[48,1536]{1,0:T(8,128)S(1)} %collective-permute-done.7.refs_2_.refs_3_, f32[4,4608,128]{2,1,0:T(8,128)} %bitcast.18, ...), custom_call_target="tpu_custom_call" | custom-call | bytes 9732096 | tf_op jit(solution)/shard_map/pallas_call | solution.py:55
  32.8 3.0 %collective-permute-start.12 = (f32[48,768]{1,0:T(8,128)S(1)}, f32[48,768]{1,0:T(8,128)S(1)}, u32[]{:S(2)}, u32[]{:S(2)}) collective-permute-start(f32[48,768]{1,0:T(8,128)S(1)} %get-tuple-element.26), channel_id=1, source_target_pairs={{0,16},{1,17},{2,18},{3,19},{4,20},{5,21},{6,22},{7,23},{8,24},{9,... | collective-permute-start | bytes 442376 | tf_op jit(solution)/shard_map/ppermute | solution.py:275
  37.9 3.5 %shard_map.58.refs_4_.refs_1_ = f32[48,1536]{1,0:T(8,128)S(1)} custom-call(s32[1]{0:T(128)} %bitcast.odd_ref.own_ref, f32[48,384]{1,0:T(8,128)S(1)} %broadcast_select_fusion.4.refs_0_, f32[48,384]{1,0:T(8,128)S(1)} %broadcast_select_fusion.3.refs_1_, f32[48,1536]{1,0:T(8,128)S(1)} %get-tuple-element.21.refs_1_.refs_2_, ...), custom_call_target="tpu_custom_call" | custom-call | tf_op jit(solution)/shard_map/pallas_call | solution.py:55
  41.4 1.6 %shard_map.57.refs_3_ = f32[384,1536]{1,0:T(8,128)S(1)} custom-call(f32[48,384]{1,0:T(8,128)S(1)} %collective-permute-done.10.token_ref.refs_6_, f32[4,384,1536]{2,1,0:T(8,128)} %refs_0_.5), custom_call_target="tpu_custom_call" | custom-call | tf_op jit(solution)/shard_map/pallas_call | solution.py:55
  43.1 3.8 %collective-permute-done.12.refs_2_ = f32[48,768]{1,0:T(8,128)S(1)} collective-permute-done((f32[48,768]{1,0:T(8,128)S(1)}, f32[48,768]{1,0:T(8,128)S(1)}, u32[]{:S(2)}, u32[]{:S(2)}) %collective-permute-start.12) | collective-permute-done | bytes 147488 | tf_op jit(solution)/shard_map/ppermute | solution.py:275
  48.2 1.6 %shard_map.60.refs_2_ = f32[4608,128]{1,0:T(8,128)S(1)} custom-call(f32[48,384]{1,0:T(8,128)S(1)} %shard_map.59.token_ref, s32[1]{0:T(128)} %bitcast.odd_ref.own_ref, f32[4,4608,128]{2,1,0:T(8,128)} %bitcast.20, f32[4,4608,128]{2,1,0:T(8,128)} %collective-permute-done.8.refs_4_.other_panel_ref.refs_5_), custom_call_target="tpu_custom_call" | custom-call | bytes 11796480 | tf_op jit(solution)/shard_map/pallas_call | solution.py:55
  50.6 2.7 %collective-permute-start.17 = (f32[48,768]{1,0:T(8,128)S(1)}, f32[48,768]{1,0:T(8,128)S(1)}, u32[]{:S(2)}, u32[]{:S(2)}) collective-permute-start(f32[48,768]{1,0:T(8,128)S(1)} %get-tuple-element.29), channel_id=1, source_target_pairs={{0,16},{1,17},{2,18},{3,19},{4,20},{5,21},{6,22},{7,23},{8,24},{9,... | collective-permute-start | bytes 442376 | tf_op jit(solution)/shard_map/ppermute | solution.py:275
  53.9 3.5 %shard_map.62.token_ref.refs_1_ = f32[48,1536]{1,0:T(8,128)S(1)} custom-call(s32[1]{0:T(128)} %constant.40.clone.1.own_ref, f32[48,384]{1,0:T(8,128)S(1)} %broadcast_select_fusion.7.refs_0_, f32[48,384]{1,0:T(8,128)S(1)} %broadcast_select_fusion.6.refs_1_, f32[48,1536]{1,0:T(8,128)S(1)} %get-tuple-element.21.refs_1_.refs_2_, ...), custom_call_target="tpu_custom_call" | custom-call | tf_op jit(solution)/shard_map/pallas_call | solution.py:55
  57.4 1.6 %shard_map.63.refs_3_ = f32[384,1536]{1,0:T(8,128)S(1)} custom-call(f32[48,1536]{1,0:T(8,128)S(1)} %shard_map.62.token_ref.refs_1_, f32[4,384,1536]{2,1,0:T(8,128)} %refs_0_.5), custom_call_target="tpu_custom_call" | custom-call | tf_op jit(solution)/shard_map/pallas_call | solution.py:55
  59.0 5.6 %collective-permute-done.17.refs_2_ = f32[48,768]{1,0:T(8,128)S(1)} collective-permute-done((f32[48,768]{1,0:T(8,128)S(1)}, f32[48,768]{1,0:T(8,128)S(1)}, u32[]{:S(2)}, u32[]{:S(2)}) %collective-permute-start.17) | collective-permute-done | bytes 147488 | tf_op jit(solution)/shard_map/ppermute | solution.py:275
  65.6 1.6 %collective-permute-start.15 = (f32[48,384]{1,0:T(8,128)S(1)}, f32[48,384]{1,0:T(8,128)S(1)}, u32[]{:S(2)}, u32[]{:S(2)}) collective-permute-start(f32[48,384]{1,0:T(8,128)S(1)} %broadcast_select_fusion.2), channel_id=1, source_target_pairs={{0,4},{1,5},{2,6},{3,7},{4,0},{5,1},{6,2},{7,3},{8,12},{9,13},{10,... | collective-permute-start | bytes 221192 | tf_op jit(solution)/shard_map/ppermute | solution.py:275
  70.3 2.4 %shard_map.65 = (f32[4608,128]{1,0:T(8,128)S(1)}, f32[4608,128]{1,0:T(8,128)S(1)}) custom-call(f32[48,384]{1,0:T(8,128)S(1)} %shard_map.64.token_ref, f32[4,4608,128]{2,1,0:T(8,128)} %bitcast.22), custom_call_target="tpu_custom_call" | custom-call | tf_op jit(solution)/shard_map/pallas_call | solution.py:55
  74.2 1.8 %collective-permute-start.22 = (f32[48,384]{1,0:T(8,128)S(1)}, f32[48,384]{1,0:T(8,128)S(1)}, u32[]{:S(2)}, u32[]{:S(2)}) collective-permute-start(f32[48,384]{1,0:T(8,128)S(1)} %get-tuple-element.36), channel_id=1, source_target_pairs={{0,24},{1,25},{2,26},{3,27},{4,28},{5,29},{6,30},{7,31},{8,16},{9,... | collective-permute-start | bytes 221192 | tf_op jit(solution)/shard_map/ppermute | solution.py:275
  76.0 2.6 %collective-permute-start.24 = (f32[48,384]{1,0:T(8,128)S(1)}, f32[48,384]{1,0:T(8,128)S(1)}, u32[]{:S(2)}, u32[]{:S(2)}) collective-permute-start(f32[48,384]{1,0:T(8,128)S(1)} %get-tuple-element.34), channel_id=1, source_target_pairs={{0,8},{1,9},{2,10},{3,11},{4,12},{5,13},{6,14},{7,15},{8,0},{9,1},... | collective-permute-start | bytes 221192 | tf_op jit(solution)/shard_map/ppermute | solution.py:275
  79.5 1.8 %collective-permute-done.22.refs_1_ = f32[48,384]{1,0:T(8,128)S(1)} collective-permute-done((f32[48,384]{1,0:T(8,128)S(1)}, f32[48,384]{1,0:T(8,128)S(1)}, u32[]{:S(2)}, u32[]{:S(2)}) %collective-permute-start.22) | collective-permute-done | bytes 73760 | tf_op jit(solution)/shard_map/ppermute | solution.py:275
  81.3 1.7 %collective-permute-done.23.refs_2_ = f32[48,384]{1,0:T(8,128)S(1)} collective-permute-done((f32[48,384]{1,0:T(8,128)S(1)}, f32[48,384]{1,0:T(8,128)S(1)}, u32[]{:S(2)}, u32[]{:S(2)}) %collective-permute-start.23) | collective-permute-done | bytes 73760 | tf_op jit(solution)/shard_map/ppermute | solution.py:275
  (61 shorter events, 21.3 us)
Async XLA Ops:
  5.2 1.6 %collective-permute-start.1 = (f32[48,1536]{1,0:T(8,128)S(1)}, f32[48,1536]{1,0:T(8,128)S(1)}, u32[]{:S(2)}, u32[]{:S(2)}) collective-permute-start(f32[48,1536]{1,0:T(8,128)S(1)} %shard_map.51), channel_id=1, source_target_pairs={{0,1},{1,0},{2,3},{3,2},{4,5},{5,4},{6,7},{7,6},{8,9},{9,8},{10,11... | collective-permute-start | bytes 884744 | tf_op jit(solution)/shard_map/ppermute | solution.py:275
  6.9 21.4 %collective-permute-start.8 = (f32[4,4608,128]{2,1,0:T(8,128)}, f32[4,4608,128]{2,1,0:T(8,128)}, u32[]{:S(2)}, u32[]{:S(2)}) collective-permute-start(f32[4,4608,128]{2,1,0:T(8,128)} %bitcast.16), channel_id=1, source_target_pairs={{0,1},{1,0},{2,3},{3,2},{4,5},{5,4},{6,7},{7,6},{8,9},{9,8},{10,11... | collective-permute-start | bytes 28311560 | tf_op jit(solution)/shard_map/ppermute | solution.py:275
  7.3 15.8 %collective-permute-start.2 = (f32[48,1536]{1,0:T(8,128)S(1)}, f32[48,1536]{1,0:T(8,128)S(1)}, u32[]{:S(2)}, u32[]{:S(2)}) collective-permute-start(f32[48,1536]{1,0:T(8,128)S(1)} %broadcast_select_fusion.refs_0_), channel_id=1, source_target_pairs={{0,8},{1,25},{2,10},{3,27},{4,12},{5,29},{6,14},{7,31},{8,0},{9,17... | collective-permute-start | bytes 884744 | tf_op jit(solution)/shard_map/ppermute | solution.py:275
  10.0 13.0 %collective-permute-start.3 = (f32[48,768]{1,0:T(8,128)S(1)}, f32[48,768]{1,0:T(8,128)S(1)}, u32[]{:S(2)}, u32[]{:S(2)}) collective-permute-start(f32[48,768]{1,0:T(8,128)S(1)} %constant_dynamic-slice_fusion.4), channel_id=1, source_target_pairs={{0,16},{1,17},{2,18},{3,19},{4,20},{5,21},{6,22},{7,23},{8,24},{9,... | collective-permute-start | bytes 442376 | tf_op jit(solution)/shard_map/ppermute | solution.py:275
  12.7 4.4 %collective-permute-start.4 = (f32[48,384]{1,0:T(8,128)S(1)}, f32[48,384]{1,0:T(8,128)S(1)}, u32[]{:S(2)}, u32[]{:S(2)}) collective-permute-start(f32[48,384]{1,0:T(8,128)S(1)} %broadcast_select_fusion.5.refs_0_), channel_id=1, source_target_pairs={{0,2},{1,3},{2,0},{3,1},{4,6},{5,7},{6,4},{7,5},{8,10},{9,11},{10,... | collective-permute-start | bytes 221192 | tf_op jit(solution)/shard_map/ppermute | solution.py:275
  23.9 2.8 %collective-permute-start.5 = (f32[48,384]{1,0:T(8,128)S(1)}, f32[48,384]{1,0:T(8,128)S(1)}, u32[]{:S(2)}, u32[]{:S(2)}) collective-permute-start(f32[48,384]{1,0:T(8,128)S(1)} %shard_map.53.refs_5_.token_ref), channel_id=1, source_target_pairs={{0,1},{1,0},{2,3},{3,2},{4,5},{5,4},{6,7},{7,6},{8,9},{9,8},{10,11... | collective-permute-start | bytes 221192 | tf_op jit(solution)/shard_map/ppermute | solution.py:275
  25.7 4.2 %collective-permute-start.7 = (f32[48,1536]{1,0:T(8,128)S(1)}, f32[48,1536]{1,0:T(8,128)S(1)}, u32[]{:S(2)}, u32[]{:S(2)}) collective-permute-start(f32[48,1536]{1,0:T(8,128)S(1)} %get-tuple-element.21.refs_1_.refs_2_), channel_id=1, source_target_pairs={{0,1},{1,0},{2,3},{3,2},{4,5},{5,4},{6,7},{7,6},{8,9},{9,8},{10,11... | collective-permute-start | bytes 884744 | tf_op jit(solution)/shard_map/ppermute | solution.py:275
  26.6 5.5 %collective-permute-start.6 = (f32[48,384]{1,0:T(8,128)S(1)}, f32[48,384]{1,0:T(8,128)S(1)}, u32[]{:S(2)}, u32[]{:S(2)}) collective-permute-start(f32[48,384]{1,0:T(8,128)S(1)} %add.26.refs_0_), channel_id=1, source_target_pairs={{0,2},{1,3},{2,0},{3,1},{4,6},{5,7},{6,4},{7,5},{8,10},{9,11},{10,... | collective-permute-start | bytes 221192 | tf_op jit(solution)/shard_map/ppermute | solution.py:275
  32.7 14.2 %collective-permute-start.11 = (f32[48,1536]{1,0:T(8,128)S(1)}, f32[48,1536]{1,0:T(8,128)S(1)}, u32[]{:S(2)}, u32[]{:S(2)}) collective-permute-start(f32[48,1536]{1,0:T(8,128)S(1)} %get-tuple-element.23.refs_6_.refs_0_), channel_id=1, source_target_pairs={{0,8},{1,25},{2,10},{3,27},{4,12},{5,29},{6,14},{7,31},{8,0},{9,17... | collective-permute-start | bytes 884744 | tf_op jit(solution)/shard_map/ppermute | solution.py:275
  32.8 14.1 %collective-permute-start.12 = (f32[48,768]{1,0:T(8,128)S(1)}, f32[48,768]{1,0:T(8,128)S(1)}, u32[]{:S(2)}, u32[]{:S(2)}) collective-permute-start(f32[48,768]{1,0:T(8,128)S(1)} %get-tuple-element.26), channel_id=1, source_target_pairs={{0,16},{1,17},{2,18},{3,19},{4,20},{5,21},{6,22},{7,23},{8,24},{9,... | collective-permute-start | bytes 442376 | tf_op jit(solution)/shard_map/ppermute | solution.py:275
  35.9 5.6 %collective-permute-start.10 = (f32[48,384]{1,0:T(8,128)S(1)}, f32[48,384]{1,0:T(8,128)S(1)}, u32[]{:S(2)}, u32[]{:S(2)}) collective-permute-start(f32[48,384]{1,0:T(8,128)S(1)} %broadcast_select_fusion.3.refs_1_), channel_id=1, source_target_pairs={{0,4},{1,5},{2,6},{3,7},{4,0},{5,1},{6,2},{7,3},{8,12},{9,13},{10,... | collective-permute-start | bytes 221192 | tf_op jit(solution)/shard_map/ppermute | solution.py:275
  37.4 5.6 %collective-permute-start.9 = (f32[48,384]{1,0:T(8,128)S(1)}, f32[48,384]{1,0:T(8,128)S(1)}, u32[]{:S(2)}, u32[]{:S(2)}) collective-permute-start(f32[48,384]{1,0:T(8,128)S(1)} %broadcast_select_fusion.4.refs_0_), channel_id=1, source_target_pairs={{0,4},{1,5},{2,6},{3,7},{4,0},{5,1},{6,2},{7,3},{8,12},{9,13},{10,... | collective-permute-start | bytes 221192 | tf_op jit(solution)/shard_map/ppermute | solution.py:275
  47.7 2.1 %collective-permute-start.13 = (f32[48,384]{1,0:T(8,128)S(1)}, f32[48,384]{1,0:T(8,128)S(1)}, u32[]{:S(2)}, u32[]{:S(2)}) collective-permute-start(f32[48,384]{1,0:T(8,128)S(1)} %shard_map.59.token_ref), channel_id=1, source_target_pairs={{0,1},{1,0},{2,3},{3,2},{4,5},{5,4},{6,7},{7,6},{8,9},{9,8},{10,11... | collective-permute-start | bytes 221192 | tf_op jit(solution)/shard_map/ppermute | solution.py:275
  50.5 14.1 %collective-permute-start.16 = (f32[48,1536]{1,0:T(8,128)S(1)}, f32[48,1536]{1,0:T(8,128)S(1)}, u32[]{:S(2)}, u32[]{:S(2)}) collective-permute-start(f32[48,1536]{1,0:T(8,128)S(1)} %get-tuple-element.27.refs_6_.refs_0_), channel_id=1, source_target_pairs={{0,8},{1,25},{2,10},{3,27},{4,12},{5,29},{6,14},{7,31},{8,0},{9,17... | collective-permute-start | bytes 884744 | tf_op jit(solution)/shard_map/ppermute | solution.py:275
  50.6 14.0 %collective-permute-start.17 = (f32[48,768]{1,0:T(8,128)S(1)}, f32[48,768]{1,0:T(8,128)S(1)}, u32[]{:S(2)}, u32[]{:S(2)}) collective-permute-start(f32[48,768]{1,0:T(8,128)S(1)} %get-tuple-element.29), channel_id=1, source_target_pairs={{0,16},{1,17},{2,18},{3,19},{4,20},{5,21},{6,22},{7,23},{8,24},{9,... | collective-permute-start | bytes 442376 | tf_op jit(solution)/shard_map/ppermute | solution.py:275
  53.3 5.8 %collective-permute-start.14 = (f32[48,384]{1,0:T(8,128)S(1)}, f32[48,384]{1,0:T(8,128)S(1)}, u32[]{:S(2)}, u32[]{:S(2)}) collective-permute-start(f32[48,384]{1,0:T(8,128)S(1)} %add.27.refs_0_), channel_id=1, source_target_pairs={{0,2},{1,3},{2,0},{3,1},{4,6},{5,7},{6,4},{7,5},{8,10},{9,11},{10,... | collective-permute-start | bytes 221192 | tf_op jit(solution)/shard_map/ppermute | solution.py:275
  65.4 1.8 %collective-permute-start.18 = (f32[48,384]{1,0:T(8,128)S(1)}, f32[48,384]{1,0:T(8,128)S(1)}, u32[]{:S(2)}, u32[]{:S(2)}) collective-permute-start(f32[48,384]{1,0:T(8,128)S(1)} %shard_map.64.token_ref), channel_id=1, source_target_pairs={{0,1},{1,0},{2,3},{3,2},{4,5},{5,4},{6,7},{7,6},{8,9},{9,8},{10,11... | collective-permute-start | bytes 221192 | tf_op jit(solution)/shard_map/ppermute | solution.py:275
  65.6 4.7 %collective-permute-start.15 = (f32[48,384]{1,0:T(8,128)S(1)}, f32[48,384]{1,0:T(8,128)S(1)}, u32[]{:S(2)}, u32[]{:S(2)}) collective-permute-start(f32[48,384]{1,0:T(8,128)S(1)} %broadcast_select_fusion.2), channel_id=1, source_target_pairs={{0,4},{1,5},{2,6},{3,7},{4,0},{5,1},{6,2},{7,3},{8,12},{9,13},{10,... | collective-permute-start | bytes 221192 | tf_op jit(solution)/shard_map/ppermute | solution.py:275
  67.3 6.2 %collective-permute-start.19 = (f32[48,384]{1,0:T(8,128)S(1)}, f32[48,384]{1,0:T(8,128)S(1)}, u32[]{:S(2)}, u32[]{:S(2)}) collective-permute-start(f32[48,384]{1,0:T(8,128)S(1)} %add.28), channel_id=1, source_target_pairs={{2,0},{3,1},{10,8},{11,9},{18,16},{19,17},{26,24},{27,25}} | collective-permute-start | bytes 221192 | tf_op jit(solution)/shard_map/ppermute | solution.py:275
  68.6 5.0 %collective-permute-start.20 = (f32[48,384]{1,0:T(8,128)S(1)}, f32[48,384]{1,0:T(8,128)S(1)}, u32[]{:S(2)}, u32[]{:S(2)}) collective-permute-start(f32[48,384]{1,0:T(8,128)S(1)} %add.28), channel_id=1, source_target_pairs={{2,6},{3,7},{10,14},{11,15},{18,22},{19,23},{26,30},{27,31}} | collective-permute-start | bytes 221192 | tf_op jit(solution)/shard_map/ppermute | solution.py:275
  69.2 4.3 %collective-permute-start.21 = (f32[48,384]{1,0:T(8,128)S(1)}, f32[48,384]{1,0:T(8,128)S(1)}, u32[]{:S(2)}, u32[]{:S(2)}) collective-permute-start(f32[48,384]{1,0:T(8,128)S(1)} %add.28), channel_id=1, source_target_pairs={{2,4},{3,5},{10,12},{11,13},{18,20},{19,21},{26,28},{27,29}} | collective-permute-start | bytes 221192 | tf_op jit(solution)/shard_map/ppermute | solution.py:275
  74.2 7.1 %collective-permute-start.22 = (f32[48,384]{1,0:T(8,128)S(1)}, f32[48,384]{1,0:T(8,128)S(1)}, u32[]{:S(2)}, u32[]{:S(2)}) collective-permute-start(f32[48,384]{1,0:T(8,128)S(1)} %get-tuple-element.36), channel_id=1, source_target_pairs={{0,24},{1,25},{2,26},{3,27},{4,28},{5,29},{6,30},{7,31},{8,16},{9,... | collective-permute-start | bytes 221192 | tf_op jit(solution)/shard_map/ppermute | solution.py:275
  76.0 7.0 %collective-permute-start.23 = (f32[48,384]{1,0:T(8,128)S(1)}, f32[48,384]{1,0:T(8,128)S(1)}, u32[]{:S(2)}, u32[]{:S(2)}) collective-permute-start(f32[48,384]{1,0:T(8,128)S(1)} %get-tuple-element.35), channel_id=1, source_target_pairs={{0,16},{1,17},{2,18},{3,19},{4,20},{5,21},{6,22},{7,23},{8,24},{9,... | collective-permute-start | bytes 221192 | tf_op jit(solution)/shard_map/ppermute | solution.py:275
  76.0 7.0 %collective-permute-start.24 = (f32[48,384]{1,0:T(8,128)S(1)}, f32[48,384]{1,0:T(8,128)S(1)}, u32[]{:S(2)}, u32[]{:S(2)}) collective-permute-start(f32[48,384]{1,0:T(8,128)S(1)} %get-tuple-element.34), channel_id=1, source_target_pairs={{0,8},{1,9},{2,10},{3,11},{4,12},{5,13},{6,14},{7,15},{8,0},{9,1},... | collective-permute-start | bytes 221192 | tf_op jit(solution)/shard_map/ppermute | solution.py:275
  (1 other events, 1.4 us)

commit v5 on v4

--- a/solution.py
+++ b/solution.py
@@ -22,13 +22,16 @@
     return head, (value - head.astype(F32)).astype(BF16)
 
 
-def product(left, right, dims):
+def product_split(left, right_head, right_tail, dims):
     count = left.shape[0]
     left_head, left_tail = split(left)
-    right_head, right_tail = split(right)
     dot = functools.partial(lax.dot_general, dimension_numbers=(dims, ((), ())), preferred_element_type=F32)
     stacked = dot(jnp.concatenate([left_head, left_tail], axis=0), right_head)
     return stacked[:count] + stacked[count:] + dot(left_head, right_tail)
+
+
+def product(left, right, dims):
+    return product_split(left, *split(right), dims)
 
 
 def columns(block_ref, first, width, rows):
@@ -121,6 +124,28 @@
     return [pltpu.make_async_copy(source.at[part], target.at[part], sems.at[first + at]) for at, part in enumerate(parts)]
 
 
+def load_inverse(token, inverse_blocks, index):
+    rows, length = inverse_blocks.shape[1:]
+    pieces = rows // LANES if rows % LANES == 0 else 1
+    size = rows // pieces
+
+    def kernel(token_ref, inverse_ref, head_ref, tail_ref, here, sems):
+        copies = chunked(inverse_ref.at[index], here, sems, 0, pieces)
+        start(copies)
+        for at, copy in enumerate(copies):
+            copy.wait()
+            part = slice(at * size, (at + 1) * size)
+            head_ref[:, part], tail_ref[:, part] = split(here[part, :].T)
+
+    return call(
+        kernel,
+        [jax.ShapeDtypeStruct((length, rows), BF16)] * 2,
+        [token, inverse_blocks],
+        [ANY, HBM],
+        scratch=[pltpu.VMEM((rows, length), F32), pltpu.SemaphoreType.DMA((pieces,))],
+    )
+
+
 def load(token, arrays):
     wanted = [(at, index) for at, (_, indices) in enumerate(arrays) for index in indices]
 
@@ -155,8 +180,12 @@
                 finish(copy)
             subtract_products([ref[...] for ref in solved_refs], base_ref, [here.at[at] for at in range(many)], out_ref)
 
+        def skip():
+            out_ref[...] = jnp.zeros_like(out_ref)
+
         pl.when(own_ref[0] == 1)(lambda: run(base_ref, panel_ref))
-        pl.when(own_ref[0] != 1)(lambda: run(other_base_ref, other_panel_ref))
+        pl.when(own_ref[0] == 0)(lambda: run(other_base_ref, other_panel_ref))
+        pl.when(own_ref[0] > 1)(skip)
 
     return call(
         kernel,
@@ -175,8 +204,12 @@
             start(copies)
             finish(copies)
 
+        def skip():
+            out_ref[...] = jnp.zeros_like(out_ref)
+
         pl.when(own_ref[0] == 1)(lambda: run(panel_ref))
-        pl.when(own_ref[0] != 1)(lambda: run(other_panel_ref))
+        pl.when(own_ref[0] == 0)(lambda: run(other_panel_ref))
+        pl.when(own_ref[0] > 1)(skip)
 
     return call(
         kernel,
@@ -238,12 +271,13 @@
 
 def gather_apply(odd, own, fulls, halves, inverse, hold):
     count, length = own.shape
-    rows = inverse.shape[0]
+    rows = inverse[0].shape[1]
 
     def kernel(odd_ref, *refs):
         odd = odd_ref[0]
-        own_ref, rest = refs[0], refs[1 : -2 - len(hold)]
-        inverse_ref, out_ref = refs[-2 - len(hold)], refs[-1]
+        own_ref, rest = refs[0], refs[1 : -3 - len(hold)]
+        head_ref, tail_ref = refs[-3 - len(hold)], refs[-2 - len(hold)]
+        out_ref = refs[-1]
         value = jnp.where(odd == 1, 0.0, own_ref[...])
         for ref in rest[: len(fulls)]:
             value = value + ref[...]
@@ -251,9 +285,9 @@
             half = ref[...]
             zero = jnp.zeros_like(half)
             value = value + jnp.concatenate([jnp.where(odd == 1, zero, half), jnp.where(odd == 1, half, zero)], axis=1)
-        out_ref[...] = product(value, inverse_ref[...], ((1,), (1,)))
-
-    ins = [own] + fulls + halves + [inverse]
+        out_ref[...] = product_split(value, head_ref[...], tail_ref[...], ((1,), (0,)))
+
+    ins = [own] + fulls + halves + list(inverse)
     specs = [SMEM] + [VMEM] * len(ins) + [ANY] * len(hold)
     return call(kernel, [shape(count, rows)], [odd.reshape(1)] + ins + hold, specs, 6 * own.size * rows)[0]
 
@@ -322,35 +356,35 @@
         total = jnp.where(is_odd == (step % 2 == 1), total, swap_core(total))
         return total, lax.dynamic_slice_in_dim(total, odd * half, half, 1)
 
-    even = 1 - odd
+    even_2, odd_2 = [jnp.where(col // 2 == 1, value, 2) for value in (1 - odd, odd)]
 
     starts = [start_value, swap_core(after(x_0, start_value))]
-    even = 1 - odd
+    even_2, odd_2 = [jnp.where(col // 2 == 1, value, 2) for value in (1 - odd, odd)]
     total, part = on_chip(update([x_0], start_value, [block_0]), 1)
     panels = [blocks, pltpu.with_memory_space_constraint(swap_core(after(total, panel.reshape(blocks.shape))), pltpu.HBM)]
     moved = across(after(total, x_0), 2)
-    (inverse,) = load(moved, [(inverse_blocks, (1,))])
+    inverse = load_inverse(moved, inverse_blocks, 1)
     piece = sum_apply(total, part, inverse, [moved])
     x_0 = on_right(x_0, moved)
-    block = load_either(piece, even, panels, 1, blocks.size)
-    base = update_from(piece, even, [x_0], starts, panels, [0], blocks.size)
+    block = load_either(piece, even_2, panels, 1, blocks.size)
+    base = update_from(piece, even_2, [x_0], starts, panels, [0], blocks.size)
     x_1 = add_cores(piece)
     moved = across(x_1, 2)
 
     total, part = update_part(odd, side, [x_1, moved], base, block)
     x_1 = on_right(x_1, moved)
-    base = update_from(total, odd, [x_0, x_1], starts, panels, [0, 1])
+    base = update_from(total, odd_2, [x_0, x_1], starts, panels, [0, 1])
     moved = [across(after(total, x), 4) for x in (x_0, x_1)]
-    (inverse,) = load(moved[1], [(inverse_blocks, (2,))])
+    inverse = load_inverse(moved[1], inverse_blocks, 2)
     piece = sum_apply(total, part, inverse, [base] + moved)
-    block = load_either(piece, odd, panels, 2, blocks.size)
+    block = load_either(piece, odd_2, panels, 2, blocks.size)
     x_0, x_1 = [spread(jnp.where((col & 4) != 0, far, x), 0, bits[2:]) for x, far in zip((x_0, x_1), moved)]
     x_2 = add_cores(piece)
 
     total, part = update_part(odd, side, [x_2], base, block)
     moved = across(after(total, x_2), 2)
     accum = update_from(total, jnp.ones_like(odd), [x_0, x_1], starts, panels, [0, 1])
-    (inverse,) = load(accum, [(inverse_blocks, (3,))])
+    inverse = load_inverse(accum, inverse_blocks, 3)
     piece = sum_apply(total, part, inverse, [moved])
     x_2 = spread(jnp.where(is_right, x_2, moved), 2, bits[1:])
     block_2, block_3 = load(piece, [(blocks, (2, 3))])

time: 84.9 us -> 82.4 us (0.971)
  Pallas kernels: 28.3 us -> 20.2 us
  waiting for transfers between devices: 23.8 us -> 26.8 us
  starting transfers between devices: 29.6 us -> 31.9 us
    pallas_call x19, Pallas kernels: 28.3 us -> 20.2 us  [call(): pl.pallas_call(kernel, out_shape=outs, in_specs=in_specs, out_specs=[VMEM...]
    ppermute x25, waiting for transfers between devices: 23.8 us -> 26.8 us  [move(): return lax.ppermute(value, ('row', 'col'), pairs)]
    ppermute x25, starting transfers between devices: 29.6 us -> 31.9 us  [move(): return lax.ppermute(value, ('row', 'col'), pairs)]
  transfers between devices with their start and end apart: 25 -> 25, of which waited for: 11 -> 14; matrix products, arithmetic and copies ran while one was open for 1% -> 1% of each run, Pallas kernels for 25% -> 17%
where the time goes in v5:
time: 82.4 us; the launch traced here: 80.9 us
  starting transfers between devices  31.9 us (39%)
  waiting for transfers between devices  26.8 us (33%)
  Pallas kernels  20.2 us (25%)
  between operations  0.9 us (1%)
  local copies, waits for them, and re-layouts  0.88 us (1%)
    ppermute x25, starting transfers between devices, move(): return lax.ppermute(value, ('row', 'col'), pairs)  31.9 us
    ppermute x25, waiting for transfers between devices, move(): return lax.ppermute(value, ('row', 'col'), pairs)  26.8 us
    pallas_call x19, Pallas kernels, call(): pl.pallas_call(kernel, out_shape=outs, in_specs=in_specs, out_specs=[VMEM...  20.2 us
  transfers between devices with their start and end apart: 25, of which 14 were waited for; matrix products, arithmetic and copies ran while one was open for 1% of the time, Pallas kernels for 17%

profile of v5, /device:TPU:0, one launch (start us, length us, event | category | flops | bytes accessed | tf_op | source)
XLA Modules:
  0.0 80.9 jit_solution(6030116448541640993)
XLA Ops:
  0.6 2.5 %shard_map.50 = (f32[48,384]{1,0:T(8,128)S(1)}, f32[48,1536]{1,0:T(8,128)S(1)}, f32[4608,128]{1,0:T(8,128)S(1)}) custom-call(s32[1]{0:T(128)} %bitcast.2.keep_ref, f32[576,128]{1,0:T(8,128)} %bitcast.24, f32[4,384,1536]{2,1,0:T(8,128)} %inverse_ref.7, f32[4,4608,128]{2,1,0:T(8,128)} %bitcast.16), custom_call_target="tpu_custom_call" | custom-call | flops 169869312 | bytes 2727936 | tf_op jit(solution)/shard_map/pallas_call | solution.py:58
  7.3 2.7 %collective-permute-start.2 = (f32[48,1536]{1,0:T(8,128)S(1)}, f32[48,1536]{1,0:T(8,128)S(1)}, u32[]{:S(2)}, u32[]{:S(2)}) collective-permute-start(f32[48,1536]{1,0:T(8,128)S(1)} %broadcast_select_fusion.refs_0_), channel_id=1, source_target_pairs={{0,8},{1,25},{2,10},{3,27},{4,12},{5,29},{6,14},{7,31},{8,0},{9,17... | collective-permute-start | bytes 884744 | tf_op jit(solution)/shard_map/ppermute | solution.py:309
  10.0 2.7 %collective-permute-start.3 = (f32[48,768]{1,0:T(8,128)S(1)}, f32[48,768]{1,0:T(8,128)S(1)}, u32[]{:S(2)}, u32[]{:S(2)}) collective-permute-start(f32[48,768]{1,0:T(8,128)S(1)} %constant_dynamic-slice_fusion.4), channel_id=1, source_target_pairs={{0,16},{1,17},{2,18},{3,19},{4,20},{5,21},{6,22},{7,23},{8,24},{9,... | collective-permute-start | bytes 442376 | tf_op jit(solution)/shard_map/ppermute | solution.py:309
  12.7 1.5 %collective-permute-start.4 = (f32[48,384]{1,0:T(8,128)S(1)}, f32[48,384]{1,0:T(8,128)S(1)}, u32[]{:S(2)}, u32[]{:S(2)}) collective-permute-start(f32[48,384]{1,0:T(8,128)S(1)} %broadcast_select_fusion.5.refs_0_), channel_id=1, source_target_pairs={{0,2},{1,3},{2,0},{3,1},{4,6},{5,7},{6,4},{7,5},{8,10},{9,11},{10,... | collective-permute-start | bytes 221192 | tf_op jit(solution)/shard_map/ppermute | solution.py:309
  14.2 2.9 %collective-permute-done.4.token_ref.refs_5_ = f32[48,384]{1,0:T(8,128)S(1)} collective-permute-done((f32[48,384]{1,0:T(8,128)S(1)}, f32[48,384]{1,0:T(8,128)S(1)}, u32[]{:S(2)}, u32[]{:S(2)}) %collective-permute-start.4) | collective-permute-done | bytes 73760 | tf_op jit(solution)/shard_map/ppermute | solution.py:309
  17.0 2.0 %shard_map.52 = (bf16[1536,384]{1,0:T(8,128)(2,1)S(1)}, bf16[1536,384]{1,0:T(8,128)(2,1)S(1)}) custom-call(f32[48,384]{1,0:T(8,128)S(1)} %collective-permute-done.4.token_ref.refs_5_, f32[4,384,1536]{2,1,0:T(8,128)} %inverse_ref.7), custom_call_target="tpu_custom_call" | custom-call | tf_op jit(solution)/shard_map/pallas_call | solution.py:58
  19.0 4.0 %collective-permute-done.3.refs_2_ = f32[48,768]{1,0:T(8,128)S(1)} collective-permute-done((f32[48,768]{1,0:T(8,128)S(1)}, f32[48,768]{1,0:T(8,128)S(1)}, u32[]{:S(2)}, u32[]{:S(2)}) %collective-permute-start.3) | collective-permute-done | bytes 147488 | tf_op jit(solution)/shard_map/ppermute | solution.py:309
  23.6 1.9 %collective-permute-start.5 = (f32[48,384]{1,0:T(8,128)S(1)}, f32[48,384]{1,0:T(8,128)S(1)}, u32[]{:S(2)}, u32[]{:S(2)}) collective-permute-start(f32[48,384]{1,0:T(8,128)S(1)} %shard_map.53.refs_5_.token_ref), channel_id=1, source_target_pairs={{0,1},{1,0},{2,3},{3,2},{4,5},{5,4},{6,7},{7,6},{8,9},{9,8},{10,11... | collective-permute-start | bytes 221192 | tf_op jit(solution)/shard_map/ppermute | solution.py:309
  26.4 1.6 %collective-permute-start.6 = (f32[48,384]{1,0:T(8,128)S(1)}, f32[48,384]{1,0:T(8,128)S(1)}, u32[]{:S(2)}, u32[]{:S(2)}) collective-permute-start(f32[48,384]{1,0:T(8,128)S(1)} %add.26.refs_0_), channel_id=1, source_target_pairs={{0,2},{1,3},{2,0},{3,1},{4,6},{5,7},{6,4},{7,5},{8,10},{9,11},{10,... | collective-permute-start | bytes 221192 | tf_op jit(solution)/shard_map/ppermute | solution.py:309
  28.2 2.7 %collective-permute-done.6.refs_1_ = f32[48,384]{1,0:T(8,128)S(1)} collective-permute-done((f32[48,384]{1,0:T(8,128)S(1)}, f32[48,384]{1,0:T(8,128)S(1)}, u32[]{:S(2)}, u32[]{:S(2)}) %collective-permute-start.6) | collective-permute-done | bytes 73760 | tf_op jit(solution)/shard_map/ppermute | solution.py:309
  31.6 3.0 %collective-permute-start.12 = (f32[48,768]{1,0:T(8,128)S(1)}, f32[48,768]{1,0:T(8,128)S(1)}, u32[]{:S(2)}, u32[]{:S(2)}) collective-permute-start(f32[48,768]{1,0:T(8,128)S(1)} %get-tuple-element.34), channel_id=1, source_target_pairs={{0,16},{1,17},{2,18},{3,19},{4,20},{5,21},{6,22},{7,23},{8,24},{9,... | collective-permute-start | bytes 442376 | tf_op jit(solution)/shard_map/ppermute | solution.py:309
  34.7 1.6 %collective-permute-start.10 = (f32[48,384]{1,0:T(8,128)S(1)}, f32[48,384]{1,0:T(8,128)S(1)}, u32[]{:S(2)}, u32[]{:S(2)}) collective-permute-start(f32[48,384]{1,0:T(8,128)S(1)} %broadcast_select_fusion.3.refs_1_), channel_id=1, source_target_pairs={{0,4},{1,5},{2,6},{3,7},{4,0},{5,1},{6,2},{7,3},{8,12},{9,13},{10,... | collective-permute-start | bytes 221192 | tf_op jit(solution)/shard_map/ppermute | solution.py:309
  36.9 2.2 %collective-permute-done.10.token_ref.refs_7_ = f32[48,384]{1,0:T(8,128)S(1)} collective-permute-done((f32[48,384]{1,0:T(8,128)S(1)}, f32[48,384]{1,0:T(8,128)S(1)}, u32[]{:S(2)}, u32[]{:S(2)}) %collective-permute-start.10) | collective-permute-done | bytes 73760 | tf_op jit(solution)/shard_map/ppermute | solution.py:309
  39.1 2.0 %shard_map.57 = (bf16[1536,384]{1,0:T(8,128)(2,1)S(1)}, bf16[1536,384]{1,0:T(8,128)(2,1)S(1)}) custom-call(f32[48,384]{1,0:T(8,128)S(1)} %collective-permute-done.10.token_ref.refs_7_, f32[4,384,1536]{2,1,0:T(8,128)} %inverse_ref.7), custom_call_target="tpu_custom_call" | custom-call | tf_op jit(solution)/shard_map/pallas_call | solution.py:58
  41.1 4.3 %collective-permute-done.12.refs_2_ = f32[48,768]{1,0:T(8,128)S(1)} collective-permute-done((f32[48,768]{1,0:T(8,128)S(1)}, f32[48,768]{1,0:T(8,128)S(1)}, u32[]{:S(2)}, u32[]{:S(2)}) %collective-permute-start.12) | collective-permute-done | bytes 147488 | tf_op jit(solution)/shard_map/ppermute | solution.py:309
  48.1 2.7 %collective-permute-start.17 = (f32[48,768]{1,0:T(8,128)S(1)}, f32[48,768]{1,0:T(8,128)S(1)}, u32[]{:S(2)}, u32[]{:S(2)}) collective-permute-start(f32[48,768]{1,0:T(8,128)S(1)} %get-tuple-element.39), channel_id=1, source_target_pairs={{0,16},{1,17},{2,18},{3,19},{4,20},{5,21},{6,22},{7,23},{8,24},{9,... | collective-permute-start | bytes 442376 | tf_op jit(solution)/shard_map/ppermute | solution.py:309
  50.8 2.5 %collective-permute-start.14 = (f32[48,384]{1,0:T(8,128)S(1)}, f32[48,384]{1,0:T(8,128)S(1)}, u32[]{:S(2)}, u32[]{:S(2)}) collective-permute-start(f32[48,384]{1,0:T(8,128)S(1)} %add.27.refs_0_), channel_id=1, source_target_pairs={{0,2},{1,3},{2,0},{3,1},{4,6},{5,7},{6,4},{7,5},{8,10},{9,11},{10,... | collective-permute-start | bytes 221192 | tf_op jit(solution)/shard_map/ppermute | solution.py:309
  53.3 3.7 %shard_map.62.token_ref.refs_1_ = f32[48,1536]{1,0:T(8,128)S(1)} custom-call(s32[1]{0:T(128)} %constant.44.clone.1.own_ref, f32[48,384]{1,0:T(8,128)S(1)} %broadcast_select_fusion.7.refs_0_, f32[48,384]{1,0:T(8,128)S(1)} %broadcast_select_fusion.6.refs_1_, f32[48,1536]{1,0:T(8,128)S(1)} %get-tuple-element.29.refs_1_.refs_2_, ...), custom_call_target="tpu_custom_call" | custom-call | tf_op jit(solution)/shard_map/pallas_call | solution.py:58
  57.0 2.0 %shard_map.63 = (bf16[1536,384]{1,0:T(8,128)(2,1)S(1)}, bf16[1536,384]{1,0:T(8,128)(2,1)S(1)}) custom-call(f32[48,1536]{1,0:T(8,128)S(1)} %shard_map.62.token_ref.refs_1_, f32[4,384,1536]{2,1,0:T(8,128)} %inverse_ref.7), custom_call_target="tpu_custom_call" | custom-call | tf_op jit(solution)/shard_map/pallas_call | solution.py:58
  59.0 3.2 %collective-permute-done.17.refs_2_ = f32[48,768]{1,0:T(8,128)S(1)} collective-permute-done((f32[48,768]{1,0:T(8,128)S(1)}, f32[48,768]{1,0:T(8,128)S(1)}, u32[]{:S(2)}, u32[]{:S(2)}) %collective-permute-start.17) | collective-permute-done | bytes 147488 | tf_op jit(solution)/shard_map/ppermute | solution.py:309
  63.4 1.6 %collective-permute-start.15 = (f32[48,384]{1,0:T(8,128)S(1)}, f32[48,384]{1,0:T(8,128)S(1)}, u32[]{:S(2)}, u32[]{:S(2)}) collective-permute-start(f32[48,384]{1,0:T(8,128)S(1)} %broadcast_select_fusion.2), channel_id=1, source_target_pairs={{0,4},{1,5},{2,6},{3,7},{4,0},{5,1},{6,2},{7,3},{8,12},{9,13},{10,... | collective-permute-start | bytes 221192 | tf_op jit(solution)/shard_map/ppermute | solution.py:309
  67.8 2.4 %shard_map.65 = (f32[4608,128]{1,0:T(8,128)S(1)}, f32[4608,128]{1,0:T(8,128)S(1)}) custom-call(f32[48,384]{1,0:T(8,128)S(1)} %shard_map.64.token_ref, f32[4,4608,128]{2,1,0:T(8,128)} %bitcast.23), custom_call_target="tpu_custom_call" | custom-call | tf_op jit(solution)/shard_map/pallas_call | solution.py:58
  73.3 3.1 %collective-permute-start.24 = (f32[48,384]{1,0:T(8,128)S(1)}, f32[48,384]{1,0:T(8,128)S(1)}, u32[]{:S(2)}, u32[]{:S(2)}) collective-permute-start(f32[48,384]{1,0:T(8,128)S(1)} %get-tuple-element.46), channel_id=1, source_target_pairs={{0,8},{1,9},{2,10},{3,11},{4,12},{5,13},{6,14},{7,15},{8,0},{9,1},... | collective-permute-start | bytes 221192 | tf_op jit(solution)/shard_map/ppermute | solution.py:309
  77.2 1.7 %collective-permute-done.22.refs_1_ = f32[48,384]{1,0:T(8,128)S(1)} collective-permute-done((f32[48,384]{1,0:T(8,128)S(1)}, f32[48,384]{1,0:T(8,128)S(1)}, u32[]{:S(2)}, u32[]{:S(2)}) %collective-permute-start.22) | collective-permute-done | bytes 73760 | tf_op jit(solution)/shard_map/ppermute | solution.py:309
  (61 shorter events, 19.8 us)
Async XLA Ops:
  3.1 1.4 %collective-permute-start = (f32[48,384]{1,0:T(8,128)S(1)}, f32[48,384]{1,0:T(8,128)S(1)}, u32[]{:S(2)}, u32[]{:S(2)}) collective-permute-start(f32[48,384]{1,0:T(8,128)S(1)} %get-tuple-element.23), channel_id=1, source_target_pairs={{0,1},{1,0},{2,3},{3,2},{4,5},{5,4},{6,7},{7,6},{8,9},{9,8},{10,11... | collective-permute-start | bytes 221192 | tf_op jit(solution)/shard_map/ppermute | solution.py:309
  5.2 1.6 %collective-permute-start.1 = (f32[48,1536]{1,0:T(8,128)S(1)}, f32[48,1536]{1,0:T(8,128)S(1)}, u32[]{:S(2)}, u32[]{:S(2)}) collective-permute-start(f32[48,1536]{1,0:T(8,128)S(1)} %shard_map.51), channel_id=1, source_target_pairs={{0,1},{1,0},{2,3},{3,2},{4,5},{5,4},{6,7},{7,6},{8,9},{9,8},{10,11... | collective-permute-start | bytes 884744 | tf_op jit(solution)/shard_map/ppermute | solution.py:309
  6.9 21.1 %collective-permute-start.8 = (f32[4,4608,128]{2,1,0:T(8,128)}, f32[4,4608,128]{2,1,0:T(8,128)}, u32[]{:S(2)}, u32[]{:S(2)}) collective-permute-start(f32[4,4608,128]{2,1,0:T(8,128)} %bitcast.17), channel_id=1, source_target_pairs={{0,1},{1,0},{2,3},{3,2},{4,5},{5,4},{6,7},{7,6},{8,9},{9,8},{10,11... | collective-permute-start | bytes 28311560 | tf_op jit(solution)/shard_map/ppermute | solution.py:309
  7.3 15.8 %collective-permute-start.2 = (f32[48,1536]{1,0:T(8,128)S(1)}, f32[48,1536]{1,0:T(8,128)S(1)}, u32[]{:S(2)}, u32[]{:S(2)}) collective-permute-start(f32[48,1536]{1,0:T(8,128)S(1)} %broadcast_select_fusion.refs_0_), channel_id=1, source_target_pairs={{0,8},{1,25},{2,10},{3,27},{4,12},{5,29},{6,14},{7,31},{8,0},{9,17... | collective-permute-start | bytes 884744 | tf_op jit(solution)/shard_map/ppermute | solution.py:309
  10.0 13.0 %collective-permute-start.3 = (f32[48,768]{1,0:T(8,128)S(1)}, f32[48,768]{1,0:T(8,128)S(1)}, u32[]{:S(2)}, u32[]{:S(2)}) collective-permute-start(f32[48,768]{1,0:T(8,128)S(1)} %constant_dynamic-slice_fusion.4), channel_id=1, source_target_pairs={{0,16},{1,17},{2,18},{3,19},{4,20},{5,21},{6,22},{7,23},{8,24},{9,... | collective-permute-start | bytes 442376 | tf_op jit(solution)/shard_map/ppermute | solution.py:309
  12.7 4.4 %collective-permute-start.4 = (f32[48,384]{1,0:T(8,128)S(1)}, f32[48,384]{1,0:T(8,128)S(1)}, u32[]{:S(2)}, u32[]{:S(2)}) collective-permute-start(f32[48,384]{1,0:T(8,128)S(1)} %broadcast_select_fusion.5.refs_0_), channel_id=1, source_target_pairs={{0,2},{1,3},{2,0},{3,1},{4,6},{5,7},{6,4},{7,5},{8,10},{9,11},{10,... | collective-permute-start | bytes 221192 | tf_op jit(solution)/shard_map/ppermute | solution.py:309
  23.6 2.8 %collective-permute-start.5 = (f32[48,384]{1,0:T(8,128)S(1)}, f32[48,384]{1,0:T(8,128)S(1)}, u32[]{:S(2)}, u32[]{:S(2)}) collective-permute-start(f32[48,384]{1,0:T(8,128)S(1)} %shard_map.53.refs_5_.token_ref), channel_id=1, source_target_pairs={{0,1},{1,0},{2,3},{3,2},{4,5},{5,4},{6,7},{7,6},{8,9},{9,8},{10,11... | collective-permute-start | bytes 221192 | tf_op jit(solution)/shard_map/ppermute | solution.py:309
  25.4 2.7 %collective-permute-start.7 = (f32[48,1536]{1,0:T(8,128)S(1)}, f32[48,1536]{1,0:T(8,128)S(1)}, u32[]{:S(2)}, u32[]{:S(2)}) collective-permute-start(f32[48,1536]{1,0:T(8,128)S(1)} %get-tuple-element.29.refs_1_.refs_2_), channel_id=1, source_target_pairs={{0,1},{1,0},{2,3},{3,2},{4,5},{5,4},{6,7},{7,6},{8,9},{9,8},{10,11... | collective-permute-start | bytes 884744 | tf_op jit(solution)/shard_map/ppermute | solution.py:309
  26.4 4.6 %collective-permute-start.6 = (f32[48,384]{1,0:T(8,128)S(1)}, f32[48,384]{1,0:T(8,128)S(1)}, u32[]{:S(2)}, u32[]{:S(2)}) collective-permute-start(f32[48,384]{1,0:T(8,128)S(1)} %add.26.refs_0_), channel_id=1, source_target_pairs={{0,2},{1,3},{2,0},{3,1},{4,6},{5,7},{6,4},{7,5},{8,10},{9,11},{10,... | collective-permute-start | bytes 221192 | tf_op jit(solution)/shard_map/ppermute | solution.py:309
  31.5 13.8 %collective-permute-start.11 = (f32[48,1536]{1,0:T(8,128)S(1)}, f32[48,1536]{1,0:T(8,128)S(1)}, u32[]{:S(2)}, u32[]{:S(2)}) collective-permute-start(f32[48,1536]{1,0:T(8,128)S(1)} %get-tuple-element.31.refs_6_.refs_0_), channel_id=1, source_target_pairs={{0,8},{1,25},{2,10},{3,27},{4,12},{5,29},{6,14},{7,31},{8,0},{9,17... | collective-permute-start | bytes 884744 | tf_op jit(solution)/shard_map/ppermute | solution.py:309
  31.6 13.8 %collective-permute-start.12 = (f32[48,768]{1,0:T(8,128)S(1)}, f32[48,768]{1,0:T(8,128)S(1)}, u32[]{:S(2)}, u32[]{:S(2)}) collective-permute-start(f32[48,768]{1,0:T(8,128)S(1)} %get-tuple-element.34), channel_id=1, source_target_pairs={{0,16},{1,17},{2,18},{3,19},{4,20},{5,21},{6,22},{7,23},{8,24},{9,... | collective-permute-start | bytes 442376 | tf_op jit(solution)/shard_map/ppermute | solution.py:309
  34.7 4.4 %collective-permute-start.10 = (f32[48,384]{1,0:T(8,128)S(1)}, f32[48,384]{1,0:T(8,128)S(1)}, u32[]{:S(2)}, u32[]{:S(2)}) collective-permute-start(f32[48,384]{1,0:T(8,128)S(1)} %broadcast_select_fusion.3.refs_1_), channel_id=1, source_target_pairs={{0,4},{1,5},{2,6},{3,7},{4,0},{5,1},{6,2},{7,3},{8,12},{9,13},{10,... | collective-permute-start | bytes 221192 | tf_op jit(solution)/shard_map/ppermute | solution.py:309
  36.3 4.8 %collective-permute-start.9 = (f32[48,384]{1,0:T(8,128)S(1)}, f32[48,384]{1,0:T(8,128)S(1)}, u32[]{:S(2)}, u32[]{:S(2)}) collective-permute-start(f32[48,384]{1,0:T(8,128)S(1)} %broadcast_select_fusion.4.refs_0_), channel_id=1, source_target_pairs={{0,4},{1,5},{2,6},{3,7},{4,0},{5,1},{6,2},{7,3},{8,12},{9,13},{10,... | collective-permute-start | bytes 221192 | tf_op jit(solution)/shard_map/ppermute | solution.py:309
  47.8 14.3 %collective-permute-start.16 = (f32[48,1536]{1,0:T(8,128)S(1)}, f32[48,1536]{1,0:T(8,128)S(1)}, u32[]{:S(2)}, u32[]{:S(2)}) collective-permute-start(f32[48,1536]{1,0:T(8,128)S(1)} %get-tuple-element.37.refs_6_.refs_0_), channel_id=1, source_target_pairs={{0,8},{1,25},{2,10},{3,27},{4,12},{5,29},{6,14},{7,31},{8,0},{9,17... | collective-permute-start | bytes 884744 | tf_op jit(solution)/shard_map/ppermute | solution.py:309
  48.1 14.0 %collective-permute-start.17 = (f32[48,768]{1,0:T(8,128)S(1)}, f32[48,768]{1,0:T(8,128)S(1)}, u32[]{:S(2)}, u32[]{:S(2)}) collective-permute-start(f32[48,768]{1,0:T(8,128)S(1)} %get-tuple-element.39), channel_id=1, source_target_pairs={{0,16},{1,17},{2,18},{3,19},{4,20},{5,21},{6,22},{7,23},{8,24},{9,... | collective-permute-start | bytes 442376 | tf_op jit(solution)/shard_map/ppermute | solution.py:309
  50.8 8.1 %collective-permute-start.14 = (f32[48,384]{1,0:T(8,128)S(1)}, f32[48,384]{1,0:T(8,128)S(1)}, u32[]{:S(2)}, u32[]{:S(2)}) collective-permute-start(f32[48,384]{1,0:T(8,128)S(1)} %add.27.refs_0_), channel_id=1, source_target_pairs={{0,2},{1,3},{2,0},{3,1},{4,6},{5,7},{6,4},{7,5},{8,10},{9,11},{10,... | collective-permute-start | bytes 221192 | tf_op jit(solution)/shard_map/ppermute | solution.py:309
  62.7 2.3 %collective-permute-start.18 = (f32[48,384]{1,0:T(8,128)S(1)}, f32[48,384]{1,0:T(8,128)S(1)}, u32[]{:S(2)}, u32[]{:S(2)}) collective-permute-start(f32[48,384]{1,0:T(8,128)S(1)} %shard_map.64.token_ref), channel_id=1, source_target_pairs={{0,1},{1,0},{2,3},{3,2},{4,5},{5,4},{6,7},{7,6},{8,9},{9,8},{10,11... | collective-permute-start | bytes 221192 | tf_op jit(solution)/shard_map/ppermute | solution.py:309
  63.4 4.4 %collective-permute-start.15 = (f32[48,384]{1,0:T(8,128)S(1)}, f32[48,384]{1,0:T(8,128)S(1)}, u32[]{:S(2)}, u32[]{:S(2)}) collective-permute-start(f32[48,384]{1,0:T(8,128)S(1)} %broadcast_select_fusion.2), channel_id=1, source_target_pairs={{0,4},{1,5},{2,6},{3,7},{4,0},{5,1},{6,2},{7,3},{8,12},{9,13},{10,... | collective-permute-start | bytes 221192 | tf_op jit(solution)/shard_map/ppermute | solution.py:309
  65.0 6.2 %collective-permute-start.19 = (f32[48,384]{1,0:T(8,128)S(1)}, f32[48,384]{1,0:T(8,128)S(1)}, u32[]{:S(2)}, u32[]{:S(2)}) collective-permute-start(f32[48,384]{1,0:T(8,128)S(1)} %add.28), channel_id=1, source_target_pairs={{2,0},{3,1},{10,8},{11,9},{18,16},{19,17},{26,24},{27,25}} | collective-permute-start | bytes 221192 | tf_op jit(solution)/shard_map/ppermute | solution.py:309
  66.3 5.0 %collective-permute-start.20 = (f32[48,384]{1,0:T(8,128)S(1)}, f32[48,384]{1,0:T(8,128)S(1)}, u32[]{:S(2)}, u32[]{:S(2)}) collective-permute-start(f32[48,384]{1,0:T(8,128)S(1)} %add.28), channel_id=1, source_target_pairs={{2,6},{3,7},{10,14},{11,15},{18,22},{19,23},{26,30},{27,31}} | collective-permute-start | bytes 221192 | tf_op jit(solution)/shard_map/ppermute | solution.py:309
  66.9 4.3 %collective-permute-start.21 = (f32[48,384]{1,0:T(8,128)S(1)}, f32[48,384]{1,0:T(8,128)S(1)}, u32[]{:S(2)}, u32[]{:S(2)}) collective-permute-start(f32[48,384]{1,0:T(8,128)S(1)} %add.28), channel_id=1, source_target_pairs={{2,4},{3,5},{10,12},{11,13},{18,20},{19,21},{26,28},{27,29}} | collective-permute-start | bytes 221192 | tf_op jit(solution)/shard_map/ppermute | solution.py:309
  71.9 7.0 %collective-permute-start.22 = (f32[48,384]{1,0:T(8,128)S(1)}, f32[48,384]{1,0:T(8,128)S(1)}, u32[]{:S(2)}, u32[]{:S(2)}) collective-permute-start(f32[48,384]{1,0:T(8,128)S(1)} %get-tuple-element.48), channel_id=1, source_target_pairs={{0,24},{1,25},{2,26},{3,27},{4,28},{5,29},{6,30},{7,31},{8,16},{9,... | collective-permute-start | bytes 221192 | tf_op jit(solution)/shard_map/ppermute | solution.py:309
  73.3 7.0 %collective-permute-start.23 = (f32[48,384]{1,0:T(8,128)S(1)}, f32[48,384]{1,0:T(8,128)S(1)}, u32[]{:S(2)}, u32[]{:S(2)}) collective-permute-start(f32[48,384]{1,0:T(8,128)S(1)} %get-tuple-element.47), channel_id=1, source_target_pairs={{0,16},{1,17},{2,18},{3,19},{4,20},{5,21},{6,22},{7,23},{8,24},{9,... | collective-permute-start | bytes 221192 | tf_op jit(solution)/shard_map/ppermute | solution.py:309
  73.3 7.0 %collective-permute-start.24 = (f32[48,384]{1,0:T(8,128)S(1)}, f32[48,384]{1,0:T(8,128)S(1)}, u32[]{:S(2)}, u32[]{:S(2)}) collective-permute-start(f32[48,384]{1,0:T(8,128)S(1)} %get-tuple-element.46), channel_id=1, source_target_pairs={{0,8},{1,9},{2,10},{3,11},{4,12},{5,13},{6,14},{7,15},{8,0},{9,1},... | collective-permute-start | bytes 221192 | tf_op jit(solution)/shard_map/ppermute | solution.py:309
  (1 other events, 1.3 us)

commit v6 on v5

--- a/solution.py
+++ b/solution.py
@@ -181,7 +181,7 @@
             subtract_products([ref[...] for ref in solved_refs], base_ref, [here.at[at] for at in range(many)], out_ref)
 
         def skip():
-            out_ref[...] = jnp.zeros_like(out_ref)
+            out_ref[...] = base_ref[...]
 
         pl.when(own_ref[0] == 1)(lambda: run(base_ref, panel_ref))
         pl.when(own_ref[0] == 0)(lambda: run(other_base_ref, other_panel_ref))
@@ -383,13 +383,16 @@
 
     total, part = update_part(odd, side, [x_2], base, block)
     moved = across(after(total, x_2), 2)
-    accum = update_from(total, jnp.ones_like(odd), [x_0, x_1], starts, panels, [0, 1])
+    x_2 = jnp.where(is_right, x_2, moved)
+    near = col // 4 == 0
+    known = [x_0, x_1, jnp.where(near, x_2, 0.0)]
+    accum = update_from(moved, jnp.ones_like(odd), known, starts, panels, [0, 1, 2])
     inverse = load_inverse(accum, inverse_blocks, 3)
     piece = sum_apply(total, part, inverse, [moved])
-    x_2 = spread(jnp.where(is_right, x_2, moved), 2, bits[1:])
-    block_2, block_3 = load(piece, [(blocks, (2, 3))])
+    x_2 = spread(x_2, 2, bits[1:])
+    (block_3,) = load(piece, [(blocks, (3,))])
     x_3 = from_chip(add_cores(piece), 3)
-    accum = update([x_2], accum, [block_2])
+    accum = update_from(block_3, jnp.where(near, 2, 1), [x_2], [accum, accum], panels, [2])
     accum = update([x_3], accum, [block_3])
 
     size = length // rows

time: 82.4 us -> 82.3 us (level)
  no operation moved by 1% of the time
where the time goes in v6:
time: 82.3 us; the launch traced here: 80.9 us
  starting transfers between devices  31.3 us (38%)
  waiting for transfers between devices  27.5 us (33%)
  Pallas kernels  20.1 us (24%)
  between operations  0.9 us (1%)
  local copies, waits for them, and re-layouts  0.88 us (1%)
    ppermute x25, starting transfers between devices, move(): return lax.ppermute(value, ('row', 'col'), pairs)  31.3 us
    ppermute x25, waiting for transfers between devices, move(): return lax.ppermute(value, ('row', 'col'), pairs)  27.5 us
    pallas_call x19, Pallas kernels, call(): pl.pallas_call(kernel, out_shape=outs, in_specs=in_specs, out_specs=[VMEM...  20.1 us
  transfers between devices with their start and end apart: 25, of which 14 were waited for; matrix products, arithmetic and copies ran while one was open for 1% of the time, Pallas kernels for 17%

profile of v6, /device:TPU:0, one launch (start us, length us, event | category | flops | bytes accessed | tf_op | source)
XLA Modules:
  0.0 80.9 jit_solution(6497102994191126623)
XLA Ops:
  0.6 2.5 %shard_map.50 = (f32[48,384]{1,0:T(8,128)S(1)}, f32[48,1536]{1,0:T(8,128)S(1)}, f32[4608,128]{1,0:T(8,128)S(1)}) custom-call(s32[1]{0:T(128)} %bitcast.2.keep_ref, f32[576,128]{1,0:T(8,128)} %bitcast.26, f32[4,384,1536]{2,1,0:T(8,128)} %inverse_ref.7, f32[4,4608,128]{2,1,0:T(8,128)} %bitcast.17), custom_call_target="tpu_custom_call" | custom-call | flops 169869312 | bytes 2727936 | tf_op jit(solution)/shard_map/pallas_call | solution.py:58
  7.3 2.7 %collective-permute-start.2 = (f32[48,1536]{1,0:T(8,128)S(1)}, f32[48,1536]{1,0:T(8,128)S(1)}, u32[]{:S(2)}, u32[]{:S(2)}) collective-permute-start(f32[48,1536]{1,0:T(8,128)S(1)} %broadcast_select_fusion.refs_0_), channel_id=1, source_target_pairs={{0,8},{1,25},{2,10},{3,27},{4,12},{5,29},{6,14},{7,31},{8,0},{9,17... | collective-permute-start | bytes 884744 | tf_op jit(solution)/shard_map/ppermute | solution.py:309
  10.0 2.7 %collective-permute-start.3 = (f32[48,768]{1,0:T(8,128)S(1)}, f32[48,768]{1,0:T(8,128)S(1)}, u32[]{:S(2)}, u32[]{:S(2)}) collective-permute-start(f32[48,768]{1,0:T(8,128)S(1)} %constant_dynamic-slice_fusion.4), channel_id=1, source_target_pairs={{0,16},{1,17},{2,18},{3,19},{4,20},{5,21},{6,22},{7,23},{8,24},{9,... | collective-permute-start | bytes 442376 | tf_op jit(solution)/shard_map/ppermute | solution.py:309
  12.7 1.5 %collective-permute-start.4 = (f32[48,384]{1,0:T(8,128)S(1)}, f32[48,384]{1,0:T(8,128)S(1)}, u32[]{:S(2)}, u32[]{:S(2)}) collective-permute-start(f32[48,384]{1,0:T(8,128)S(1)} %broadcast_select_fusion.6.refs_0_), channel_id=1, source_target_pairs={{0,2},{1,3},{2,0},{3,1},{4,6},{5,7},{6,4},{7,5},{8,10},{9,11},{10,... | collective-permute-start | bytes 221192 | tf_op jit(solution)/shard_map/ppermute | solution.py:309
  14.2 2.9 %collective-permute-done.4.token_ref.refs_5_ = f32[48,384]{1,0:T(8,128)S(1)} collective-permute-done((f32[48,384]{1,0:T(8,128)S(1)}, f32[48,384]{1,0:T(8,128)S(1)}, u32[]{:S(2)}, u32[]{:S(2)}) %collective-permute-start.4) | collective-permute-done | bytes 73760 | tf_op jit(solution)/shard_map/ppermute | solution.py:309
  17.0 2.0 %shard_map.52 = (bf16[1536,384]{1,0:T(8,128)(2,1)S(1)}, bf16[1536,384]{1,0:T(8,128)(2,1)S(1)}) custom-call(f32[48,384]{1,0:T(8,128)S(1)} %collective-permute-done.4.token_ref.refs_5_, f32[4,384,1536]{2,1,0:T(8,128)} %inverse_ref.7), custom_call_target="tpu_custom_call" | custom-call | tf_op jit(solution)/shard_map/pallas_call | solution.py:58
  19.0 4.0 %collective-permute-done.3.refs_2_ = f32[48,768]{1,0:T(8,128)S(1)} collective-permute-done((f32[48,768]{1,0:T(8,128)S(1)}, f32[48,768]{1,0:T(8,128)S(1)}, u32[]{:S(2)}, u32[]{:S(2)}) %collective-permute-start.3) | collective-permute-done | bytes 147488 | tf_op jit(solution)/shard_map/ppermute | solution.py:309
  23.6 1.9 %collective-permute-start.5 = (f32[48,384]{1,0:T(8,128)S(1)}, f32[48,384]{1,0:T(8,128)S(1)}, u32[]{:S(2)}, u32[]{:S(2)}) collective-permute-start(f32[48,384]{1,0:T(8,128)S(1)} %shard_map.53.refs_5_.token_ref), channel_id=1, source_target_pairs={{0,1},{1,0},{2,3},{3,2},{4,5},{5,4},{6,7},{7,6},{8,9},{9,8},{10,11... | collective-permute-start | bytes 221192 | tf_op jit(solution)/shard_map/ppermute | solution.py:309
  26.4 1.6 %collective-permute-start.6 = (f32[48,384]{1,0:T(8,128)S(1)}, f32[48,384]{1,0:T(8,128)S(1)}, u32[]{:S(2)}, u32[]{:S(2)}) collective-permute-start(f32[48,384]{1,0:T(8,128)S(1)} %add.27.refs_0_), channel_id=1, source_target_pairs={{0,2},{1,3},{2,0},{3,1},{4,6},{5,7},{6,4},{7,5},{8,10},{9,11},{10,... | collective-permute-start | bytes 221192 | tf_op jit(solution)/shard_map/ppermute | solution.py:309
  28.2 2.7 %collective-permute-done.6.refs_1_ = f32[48,384]{1,0:T(8,128)S(1)} collective-permute-done((f32[48,384]{1,0:T(8,128)S(1)}, f32[48,384]{1,0:T(8,128)S(1)}, u32[]{:S(2)}, u32[]{:S(2)}) %collective-permute-start.6) | collective-permute-done | bytes 73760 | tf_op jit(solution)/shard_map/ppermute | solution.py:309
  31.6 3.0 %collective-permute-start.12 = (f32[48,768]{1,0:T(8,128)S(1)}, f32[48,768]{1,0:T(8,128)S(1)}, u32[]{:S(2)}, u32[]{:S(2)}) collective-permute-start(f32[48,768]{1,0:T(8,128)S(1)} %get-tuple-element.32), channel_id=1, source_target_pairs={{0,16},{1,17},{2,18},{3,19},{4,20},{5,21},{6,22},{7,23},{8,24},{9,... | collective-permute-start | bytes 442376 | tf_op jit(solution)/shard_map/ppermute | solution.py:309
  34.7 1.6 %collective-permute-start.10 = (f32[48,384]{1,0:T(8,128)S(1)}, f32[48,384]{1,0:T(8,128)S(1)}, u32[]{:S(2)}, u32[]{:S(2)}) collective-permute-start(f32[48,384]{1,0:T(8,128)S(1)} %broadcast_select_fusion.4.refs_1_), channel_id=1, source_target_pairs={{0,4},{1,5},{2,6},{3,7},{4,0},{5,1},{6,2},{7,3},{8,12},{9,13},{10,... | collective-permute-start | bytes 221192 | tf_op jit(solution)/shard_map/ppermute | solution.py:309
  36.9 2.2 %collective-permute-done.10.token_ref.refs_7_ = f32[48,384]{1,0:T(8,128)S(1)} collective-permute-done((f32[48,384]{1,0:T(8,128)S(1)}, f32[48,384]{1,0:T(8,128)S(1)}, u32[]{:S(2)}, u32[]{:S(2)}) %collective-permute-start.10) | collective-permute-done | bytes 73760 | tf_op jit(solution)/shard_map/ppermute | solution.py:309
  39.1 2.0 %shard_map.57 = (bf16[1536,384]{1,0:T(8,128)(2,1)S(1)}, bf16[1536,384]{1,0:T(8,128)(2,1)S(1)}) custom-call(f32[48,384]{1,0:T(8,128)S(1)} %collective-permute-done.10.token_ref.refs_7_, f32[4,384,1536]{2,1,0:T(8,128)} %inverse_ref.7), custom_call_target="tpu_custom_call" | custom-call | tf_op jit(solution)/shard_map/pallas_call | solution.py:58
  41.1 4.3 %collective-permute-done.12.refs_2_ = f32[48,768]{1,0:T(8,128)S(1)} collective-permute-done((f32[48,768]{1,0:T(8,128)S(1)}, f32[48,768]{1,0:T(8,128)S(1)}, u32[]{:S(2)}, u32[]{:S(2)}) %collective-permute-start.12) | collective-permute-done | bytes 147488 | tf_op jit(solution)/shard_map/ppermute | solution.py:309
  48.1 2.5 %collective-permute-start.14 = (f32[48,384]{1,0:T(8,128)S(1)}, f32[48,384]{1,0:T(8,128)S(1)}, u32[]{:S(2)}, u32[]{:S(2)}) collective-permute-start(f32[48,384]{1,0:T(8,128)S(1)} %add.28.refs_0_), channel_id=1, source_target_pairs={{0,2},{1,3},{2,0},{3,1},{4,6},{5,7},{6,4},{7,5},{8,10},{9,11},{10,... | collective-permute-start | bytes 221192 | tf_op jit(solution)/shard_map/ppermute | solution.py:309
  50.6 2.7 %collective-permute-start.17 = (f32[48,768]{1,0:T(8,128)S(1)}, f32[48,768]{1,0:T(8,128)S(1)}, u32[]{:S(2)}, u32[]{:S(2)}) collective-permute-start(f32[48,768]{1,0:T(8,128)S(1)} %get-tuple-element.37), channel_id=1, source_target_pairs={{0,16},{1,17},{2,18},{3,19},{4,20},{5,21},{6,22},{7,23},{8,24},{9,... | collective-permute-start | bytes 442376 | tf_op jit(solution)/shard_map/ppermute | solution.py:309
  53.3 4.8 %shard_map.62.token_ref.refs_1_.refs_2_ = f32[48,1536]{1,0:T(8,128)S(1)} custom-call(s32[1]{0:T(128)} %constant.53.clone.1.own_ref, f32[48,384]{1,0:T(8,128)S(1)} %broadcast_select_fusion.8.refs_0_, f32[48,384]{1,0:T(8,128)S(1)} %broadcast_select_fusion.7.refs_1_, f32[48,384]{1,0:T(8,128)S(1)} %get-tuple-element.42.refs_2_, ...), custom_call_target="tpu_custom_call" | custom-call | tf_op jit(solution)/shard_map/pallas_call | solution.py:58
  58.1 2.0 %shard_map.63 = (bf16[1536,384]{1,0:T(8,128)(2,1)S(1)}, bf16[1536,384]{1,0:T(8,128)(2,1)S(1)}) custom-call(f32[48,1536]{1,0:T(8,128)S(1)} %shard_map.62.token_ref.refs_1_.refs_2_, f32[4,384,1536]{2,1,0:T(8,128)} %inverse_ref.7), custom_call_target="tpu_custom_call" | custom-call | tf_op jit(solution)/shard_map/pallas_call | solution.py:58
  60.1 2.7 %collective-permute-done.17.refs_2_ = f32[48,768]{1,0:T(8,128)S(1)} collective-permute-done((f32[48,768]{1,0:T(8,128)S(1)}, f32[48,768]{1,0:T(8,128)S(1)}, u32[]{:S(2)}, u32[]{:S(2)}) %collective-permute-start.17) | collective-permute-done | bytes 147488 | tf_op jit(solution)/shard_map/ppermute | solution.py:309
  68.1 1.6 %shard_map.65.refs_5_.refs_2_ = f32[4608,128]{1,0:T(8,128)S(1)} custom-call(f32[48,384]{1,0:T(8,128)S(1)} %shard_map.64.token_ref, f32[4,4608,128]{2,1,0:T(8,128)} %bitcast.24), custom_call_target="tpu_custom_call" | custom-call | tf_op jit(solution)/shard_map/pallas_call | solution.py:58
  71.9 2.4 %collective-permute-start.22 = (f32[48,384]{1,0:T(8,128)S(1)}, f32[48,384]{1,0:T(8,128)S(1)}, u32[]{:S(2)}, u32[]{:S(2)}) collective-permute-start(f32[48,384]{1,0:T(8,128)S(1)} %get-tuple-element.46), channel_id=1, source_target_pairs={{0,24},{1,25},{2,26},{3,27},{4,28},{5,29},{6,30},{7,31},{8,16},{9,... | collective-permute-start | bytes 221192 | tf_op jit(solution)/shard_map/ppermute | solution.py:309
  74.3 2.1 %collective-permute-start.24 = (f32[48,384]{1,0:T(8,128)S(1)}, f32[48,384]{1,0:T(8,128)S(1)}, u32[]{:S(2)}, u32[]{:S(2)}) collective-permute-start(f32[48,384]{1,0:T(8,128)S(1)} %get-tuple-element.44), channel_id=1, source_target_pairs={{0,8},{1,9},{2,10},{3,11},{4,12},{5,13},{6,14},{7,15},{8,0},{9,1},... | collective-permute-start | bytes 221192 | tf_op jit(solution)/shard_map/ppermute | solution.py:309
  78.6 1.6 %collective-permute-done.23.refs_2_ = f32[48,384]{1,0:T(8,128)S(1)} collective-permute-done((f32[48,384]{1,0:T(8,128)S(1)}, f32[48,384]{1,0:T(8,128)S(1)}, u32[]{:S(2)}, u32[]{:S(2)}) %collective-permute-start.23) | collective-permute-done | bytes 73760 | tf_op jit(solution)/shard_map/ppermute | solution.py:309
  (61 shorter events, 20.1 us)
Async XLA Ops:
  3.1 1.4 %collective-permute-start = (f32[48,384]{1,0:T(8,128)S(1)}, f32[48,384]{1,0:T(8,128)S(1)}, u32[]{:S(2)}, u32[]{:S(2)}) collective-permute-start(f32[48,384]{1,0:T(8,128)S(1)} %get-tuple-element.21), channel_id=1, source_target_pairs={{0,1},{1,0},{2,3},{3,2},{4,5},{5,4},{6,7},{7,6},{8,9},{9,8},{10,11... | collective-permute-start | bytes 221192 | tf_op jit(solution)/shard_map/ppermute | solution.py:309
  5.2 1.6 %collective-permute-start.1 = (f32[48,1536]{1,0:T(8,128)S(1)}, f32[48,1536]{1,0:T(8,128)S(1)}, u32[]{:S(2)}, u32[]{:S(2)}) collective-permute-start(f32[48,1536]{1,0:T(8,128)S(1)} %shard_map.51), channel_id=1, source_target_pairs={{0,1},{1,0},{2,3},{3,2},{4,5},{5,4},{6,7},{7,6},{8,9},{9,8},{10,11... | collective-permute-start | bytes 884744 | tf_op jit(solution)/shard_map/ppermute | solution.py:309
  6.9 21.1 %collective-permute-start.8 = (f32[4,4608,128]{2,1,0:T(8,128)}, f32[4,4608,128]{2,1,0:T(8,128)}, u32[]{:S(2)}, u32[]{:S(2)}) collective-permute-start(f32[4,4608,128]{2,1,0:T(8,128)} %bitcast.18), channel_id=1, source_target_pairs={{0,1},{1,0},{2,3},{3,2},{4,5},{5,4},{6,7},{7,6},{8,9},{9,8},{10,11... | collective-permute-start | bytes 28311560 | tf_op jit(solution)/shard_map/ppermute | solution.py:309
  7.3 15.8 %collective-permute-start.2 = (f32[48,1536]{1,0:T(8,128)S(1)}, f32[48,1536]{1,0:T(8,128)S(1)}, u32[]{:S(2)}, u32[]{:S(2)}) collective-permute-start(f32[48,1536]{1,0:T(8,128)S(1)} %broadcast_select_fusion.refs_0_), channel_id=1, source_target_pairs={{0,8},{1,25},{2,10},{3,27},{4,12},{5,29},{6,14},{7,31},{8,0},{9,17... | collective-permute-start | bytes 884744 | tf_op jit(solution)/shard_map/ppermute | solution.py:309
  10.0 13.0 %collective-permute-start.3 = (f32[48,768]{1,0:T(8,128)S(1)}, f32[48,768]{1,0:T(8,128)S(1)}, u32[]{:S(2)}, u32[]{:S(2)}) collective-permute-start(f32[48,768]{1,0:T(8,128)S(1)} %constant_dynamic-slice_fusion.4), channel_id=1, source_target_pairs={{0,16},{1,17},{2,18},{3,19},{4,20},{5,21},{6,22},{7,23},{8,24},{9,... | collective-permute-start | bytes 442376 | tf_op jit(solution)/shard_map/ppermute | solution.py:309
  12.7 4.4 %collective-permute-start.4 = (f32[48,384]{1,0:T(8,128)S(1)}, f32[48,384]{1,0:T(8,128)S(1)}, u32[]{:S(2)}, u32[]{:S(2)}) collective-permute-start(f32[48,384]{1,0:T(8,128)S(1)} %broadcast_select_fusion.6.refs_0_), channel_id=1, source_target_pairs={{0,2},{1,3},{2,0},{3,1},{4,6},{5,7},{6,4},{7,5},{8,10},{9,11},{10,... | collective-permute-start | bytes 221192 | tf_op jit(solution)/shard_map/ppermute | solution.py:309
  23.6 2.8 %collective-permute-start.5 = (f32[48,384]{1,0:T(8,128)S(1)}, f32[48,384]{1,0:T(8,128)S(1)}, u32[]{:S(2)}, u32[]{:S(2)}) collective-permute-start(f32[48,384]{1,0:T(8,128)S(1)} %shard_map.53.refs_5_.token_ref), channel_id=1, source_target_pairs={{0,1},{1,0},{2,3},{3,2},{4,5},{5,4},{6,7},{7,6},{8,9},{9,8},{10,11... | collective-permute-start | bytes 221192 | tf_op jit(solution)/shard_map/ppermute | solution.py:309
  25.4 2.7 %collective-permute-start.7 = (f32[48,1536]{1,0:T(8,128)S(1)}, f32[48,1536]{1,0:T(8,128)S(1)}, u32[]{:S(2)}, u32[]{:S(2)}) collective-permute-start(f32[48,1536]{1,0:T(8,128)S(1)} %get-tuple-element.27.refs_1_.refs_2_.refs_3_), channel_id=1, source_target_pairs={{0,1},{1,0},{2,3},{3,2},{4,5},{5,4},{6,7},{7,6},{8,9},{9,8},{10,11... | collective-permute-start | bytes 884744 | tf_op jit(solution)/shard_map/ppermute | solution.py:309
  26.4 4.6 %collective-permute-start.6 = (f32[48,384]{1,0:T(8,128)S(1)}, f32[48,384]{1,0:T(8,128)S(1)}, u32[]{:S(2)}, u32[]{:S(2)}) collective-permute-start(f32[48,384]{1,0:T(8,128)S(1)} %add.27.refs_0_), channel_id=1, source_target_pairs={{0,2},{1,3},{2,0},{3,1},{4,6},{5,7},{6,4},{7,5},{8,10},{9,11},{10,... | collective-permute-start | bytes 221192 | tf_op jit(solution)/shard_map/ppermute | solution.py:309
  31.6 13.8 %collective-permute-start.11 = (f32[48,1536]{1,0:T(8,128)S(1)}, f32[48,1536]{1,0:T(8,128)S(1)}, u32[]{:S(2)}, u32[]{:S(2)}) collective-permute-start(f32[48,1536]{1,0:T(8,128)S(1)} %get-tuple-element.29.refs_6_.refs_0_), channel_id=1, source_target_pairs={{0,8},{1,25},{2,10},{3,27},{4,12},{5,29},{6,14},{7,31},{8,0},{9,17... | collective-permute-start | bytes 884744 | tf_op jit(solution)/shard_map/ppermute | solution.py:309
  31.6 13.7 %collective-permute-start.12 = (f32[48,768]{1,0:T(8,128)S(1)}, f32[48,768]{1,0:T(8,128)S(1)}, u32[]{:S(2)}, u32[]{:S(2)}) collective-permute-start(f32[48,768]{1,0:T(8,128)S(1)} %get-tuple-element.32), channel_id=1, source_target_pairs={{0,16},{1,17},{2,18},{3,19},{4,20},{5,21},{6,22},{7,23},{8,24},{9,... | collective-permute-start | bytes 442376 | tf_op jit(solution)/shard_map/ppermute | solution.py:309
  34.7 4.4 %collective-permute-start.10 = (f32[48,384]{1,0:T(8,128)S(1)}, f32[48,384]{1,0:T(8,128)S(1)}, u32[]{:S(2)}, u32[]{:S(2)}) collective-permute-start(f32[48,384]{1,0:T(8,128)S(1)} %broadcast_select_fusion.4.refs_1_), channel_id=1, source_target_pairs={{0,4},{1,5},{2,6},{3,7},{4,0},{5,1},{6,2},{7,3},{8,12},{9,13},{10,... | collective-permute-start | bytes 221192 | tf_op jit(solution)/shard_map/ppermute | solution.py:309
  36.3 4.8 %collective-permute-start.9 = (f32[48,384]{1,0:T(8,128)S(1)}, f32[48,384]{1,0:T(8,128)S(1)}, u32[]{:S(2)}, u32[]{:S(2)}) collective-permute-start(f32[48,384]{1,0:T(8,128)S(1)} %broadcast_select_fusion.5.refs_0_), channel_id=1, source_target_pairs={{0,4},{1,5},{2,6},{3,7},{4,0},{5,1},{6,2},{7,3},{8,12},{9,13},{10,... | collective-permute-start | bytes 221192 | tf_op jit(solution)/shard_map/ppermute | solution.py:309
  47.8 15.0 %collective-permute-start.16 = (f32[48,1536]{1,0:T(8,128)S(1)}, f32[48,1536]{1,0:T(8,128)S(1)}, u32[]{:S(2)}, u32[]{:S(2)}) collective-permute-start(f32[48,1536]{1,0:T(8,128)S(1)} %get-tuple-element.35.refs_0_), channel_id=1, source_target_pairs={{0,8},{1,25},{2,10},{3,27},{4,12},{5,29},{6,14},{7,31},{8,0},{9,17... | collective-permute-start | bytes 884744 | tf_op jit(solution)/shard_map/ppermute | solution.py:309
  48.1 5.2 %collective-permute-start.14 = (f32[48,384]{1,0:T(8,128)S(1)}, f32[48,384]{1,0:T(8,128)S(1)}, u32[]{:S(2)}, u32[]{:S(2)}) collective-permute-start(f32[48,384]{1,0:T(8,128)S(1)} %add.28.refs_0_), channel_id=1, source_target_pairs={{0,2},{1,3},{2,0},{3,1},{4,6},{5,7},{6,4},{7,5},{8,10},{9,11},{10,... | collective-permute-start | bytes 221192 | tf_op jit(solution)/shard_map/ppermute | solution.py:309
  50.6 12.3 %collective-permute-start.17 = (f32[48,768]{1,0:T(8,128)S(1)}, f32[48,768]{1,0:T(8,128)S(1)}, u32[]{:S(2)}, u32[]{:S(2)}) collective-permute-start(f32[48,768]{1,0:T(8,128)S(1)} %get-tuple-element.37), channel_id=1, source_target_pairs={{0,16},{1,17},{2,18},{3,19},{4,20},{5,21},{6,22},{7,23},{8,24},{9,... | collective-permute-start | bytes 442376 | tf_op jit(solution)/shard_map/ppermute | solution.py:309
  63.4 1.6 %collective-permute-start.18 = (f32[48,384]{1,0:T(8,128)S(1)}, f32[48,384]{1,0:T(8,128)S(1)}, u32[]{:S(2)}, u32[]{:S(2)}) collective-permute-start(f32[48,384]{1,0:T(8,128)S(1)} %shard_map.64.token_ref), channel_id=1, source_target_pairs={{0,1},{1,0},{2,3},{3,2},{4,5},{5,4},{6,7},{7,6},{8,9},{9,8},{10,11... | collective-permute-start | bytes 221192 | tf_op jit(solution)/shard_map/ppermute | solution.py:309
  63.7 4.4 %collective-permute-start.15 = (f32[48,384]{1,0:T(8,128)S(1)}, f32[48,384]{1,0:T(8,128)S(1)}, u32[]{:S(2)}, u32[]{:S(2)}) collective-permute-start(f32[48,384]{1,0:T(8,128)S(1)} %get-tuple-element.43), channel_id=1, source_target_pairs={{0,4},{1,5},{2,6},{3,7},{4,0},{5,1},{6,2},{7,3},{8,12},{9,13},{10,... | collective-permute-start | bytes 221192 | tf_op jit(solution)/shard_map/ppermute | solution.py:309
  65.0 6.2 %collective-permute-start.19 = (f32[48,384]{1,0:T(8,128)S(1)}, f32[48,384]{1,0:T(8,128)S(1)}, u32[]{:S(2)}, u32[]{:S(2)}) collective-permute-start(f32[48,384]{1,0:T(8,128)S(1)} %add.29), channel_id=1, source_target_pairs={{2,0},{3,1},{10,8},{11,9},{18,16},{19,17},{26,24},{27,25}} | collective-permute-start | bytes 221192 | tf_op jit(solution)/shard_map/ppermute | solution.py:309
  66.3 5.0 %collective-permute-start.20 = (f32[48,384]{1,0:T(8,128)S(1)}, f32[48,384]{1,0:T(8,128)S(1)}, u32[]{:S(2)}, u32[]{:S(2)}) collective-permute-start(f32[48,384]{1,0:T(8,128)S(1)} %add.29), channel_id=1, source_target_pairs={{2,6},{3,7},{10,14},{11,15},{18,22},{19,23},{26,30},{27,31}} | collective-permute-start | bytes 221192 | tf_op jit(solution)/shard_map/ppermute | solution.py:309
  67.0 4.3 %collective-permute-start.21 = (f32[48,384]{1,0:T(8,128)S(1)}, f32[48,384]{1,0:T(8,128)S(1)}, u32[]{:S(2)}, u32[]{:S(2)}) collective-permute-start(f32[48,384]{1,0:T(8,128)S(1)} %add.29), channel_id=1, source_target_pairs={{2,4},{3,5},{10,12},{11,13},{18,20},{19,21},{26,28},{27,29}} | collective-permute-start | bytes 221192 | tf_op jit(solution)/shard_map/ppermute | solution.py:309
  71.9 6.7 %collective-permute-start.22 = (f32[48,384]{1,0:T(8,128)S(1)}, f32[48,384]{1,0:T(8,128)S(1)}, u32[]{:S(2)}, u32[]{:S(2)}) collective-permute-start(f32[48,384]{1,0:T(8,128)S(1)} %get-tuple-element.46), channel_id=1, source_target_pairs={{0,24},{1,25},{2,26},{3,27},{4,28},{5,29},{6,30},{7,31},{8,16},{9,... | collective-permute-start | bytes 221192 | tf_op jit(solution)/shard_map/ppermute | solution.py:309
  74.3 6.0 %collective-permute-start.23 = (f32[48,384]{1,0:T(8,128)S(1)}, f32[48,384]{1,0:T(8,128)S(1)}, u32[]{:S(2)}, u32[]{:S(2)}) collective-permute-start(f32[48,384]{1,0:T(8,128)S(1)} %get-tuple-element.45), channel_id=1, source_target_pairs={{0,16},{1,17},{2,18},{3,19},{4,20},{5,21},{6,22},{7,23},{8,24},{9,... | collective-permute-start | bytes 221192 | tf_op jit(solution)/shard_map/ppermute | solution.py:309
  74.3 6.0 %collective-permute-start.24 = (f32[48,384]{1,0:T(8,128)S(1)}, f32[48,384]{1,0:T(8,128)S(1)}, u32[]{:S(2)}, u32[]{:S(2)}) collective-permute-start(f32[48,384]{1,0:T(8,128)S(1)} %get-tuple-element.44), channel_id=1, source_target_pairs={{0,8},{1,9},{2,10},{3,11},{4,12},{5,13},{6,14},{7,15},{8,0},{9,1},... | collective-permute-start | bytes 221192 | tf_op jit(solution)/shard_map/ppermute | solution.py:309
  (1 other events, 1.3 us)

commit v7 on v5

--- a/solution.py
+++ b/solution.py
@@ -395,7 +395,7 @@
     size = length // rows
     chunk = lambda at: lax.dynamic_slice_in_dim(accum, at * size, size, 1)
     parts = [chunk(row)]
-    for offset in range(rows - 1, 0, -1):
+    for offset in list(range(rows // 2, rows)) + list(range(1, rows // 2)):
         parts.append(move(chunk(row ^ offset), lambda z, q: (z ^ offset, q)))
     updated = add_rows(parts).reshape(count, 1, 1, size)
     return jnp.stack([x_0, x_1, x_2, x_3], axis=1), updated

time: 82.4 us -> 81.8 us (level)
  starting transfers between devices: 31.9 us -> 31 us
    ppermute x25, starting transfers between devices: 31.9 us -> 31 us  [move(): return lax.ppermute(value, ('row', 'col'), pairs)]
where the time goes in v7:
time: 81.8 us; the launch traced here: 80.4 us
  starting transfers between devices  31 us (38%)
  waiting for transfers between devices  27.2 us (33%)
  Pallas kernels  20.2 us (25%)
  between operations  0.91 us (1%)
  local copies, waits for them, and re-layouts  0.88 us (1%)
    ppermute x25, starting transfers between devices, move(): return lax.ppermute(value, ('row', 'col'), pairs)  31 us
    ppermute x25, waiting for transfers between devices, move(): return lax.ppermute(value, ('row', 'col'), pairs)  27.2 us
    pallas_call x19, Pallas kernels, call(): pl.pallas_call(kernel, out_shape=outs, in_specs=in_specs, out_specs=[VMEM...  20.2 us
  transfers between devices with their start and end apart: 25, of which 14 were waited for; matrix products, arithmetic and copies ran while one was open for 1% of the time, Pallas kernels for 17%

profile of v7, /device:TPU:0, one launch (start us, length us, event | category | flops | bytes accessed | tf_op | source)
XLA Modules:
  0.0 80.4 jit_solution(13184325984748819843)
XLA Ops:
  0.6 2.5 %shard_map.50 = (f32[48,384]{1,0:T(8,128)S(1)}, f32[48,1536]{1,0:T(8,128)S(1)}, f32[4608,128]{1,0:T(8,128)S(1)}) custom-call(s32[1]{0:T(128)} %bitcast.2.keep_ref, f32[576,128]{1,0:T(8,128)} %bitcast.24, f32[4,384,1536]{2,1,0:T(8,128)} %inverse_ref.7, f32[4,4608,128]{2,1,0:T(8,128)} %bitcast.16), custom_call_target="tpu_custom_call" | custom-call | flops 169869312 | bytes 2727936 | tf_op jit(solution)/shard_map/pallas_call | solution.py:58
  7.3 2.7 %collective-permute-start.2 = (f32[48,1536]{1,0:T(8,128)S(1)}, f32[48,1536]{1,0:T(8,128)S(1)}, u32[]{:S(2)}, u32[]{:S(2)}) collective-permute-start(f32[48,1536]{1,0:T(8,128)S(1)} %broadcast_select_fusion.refs_0_), channel_id=1, source_target_pairs={{0,8},{1,25},{2,10},{3,27},{4,12},{5,29},{6,14},{7,31},{8,0},{9,17... | collective-permute-start | bytes 884744 | tf_op jit(solution)/shard_map/ppermute | solution.py:309
  10.0 2.7 %collective-permute-start.3 = (f32[48,768]{1,0:T(8,128)S(1)}, f32[48,768]{1,0:T(8,128)S(1)}, u32[]{:S(2)}, u32[]{:S(2)}) collective-permute-start(f32[48,768]{1,0:T(8,128)S(1)} %constant_dynamic-slice_fusion.4), channel_id=1, source_target_pairs={{0,16},{1,17},{2,18},{3,19},{4,20},{5,21},{6,22},{7,23},{8,24},{9,... | collective-permute-start | bytes 442376 | tf_op jit(solution)/shard_map/ppermute | solution.py:309
  12.7 1.5 %collective-permute-start.4 = (f32[48,384]{1,0:T(8,128)S(1)}, f32[48,384]{1,0:T(8,128)S(1)}, u32[]{:S(2)}, u32[]{:S(2)}) collective-permute-start(f32[48,384]{1,0:T(8,128)S(1)} %broadcast_select_fusion.5.refs_0_), channel_id=1, source_target_pairs={{0,2},{1,3},{2,0},{3,1},{4,6},{5,7},{6,4},{7,5},{8,10},{9,11},{10,... | collective-permute-start | bytes 221192 | tf_op jit(solution)/shard_map/ppermute | solution.py:309
  14.2 2.9 %collective-permute-done.4.token_ref.refs_5_ = f32[48,384]{1,0:T(8,128)S(1)} collective-permute-done((f32[48,384]{1,0:T(8,128)S(1)}, f32[48,384]{1,0:T(8,128)S(1)}, u32[]{:S(2)}, u32[]{:S(2)}) %collective-permute-start.4) | collective-permute-done | bytes 73760 | tf_op jit(solution)/shard_map/ppermute | solution.py:309
  17.0 2.0 %shard_map.52 = (bf16[1536,384]{1,0:T(8,128)(2,1)S(1)}, bf16[1536,384]{1,0:T(8,128)(2,1)S(1)}) custom-call(f32[48,384]{1,0:T(8,128)S(1)} %collective-permute-done.4.token_ref.refs_5_, f32[4,384,1536]{2,1,0:T(8,128)} %inverse_ref.7), custom_call_target="tpu_custom_call" | custom-call | tf_op jit(solution)/shard_map/pallas_call | solution.py:58
  19.0 4.0 %collective-permute-done.3.refs_2_ = f32[48,768]{1,0:T(8,128)S(1)} collective-permute-done((f32[48,768]{1,0:T(8,128)S(1)}, f32[48,768]{1,0:T(8,128)S(1)}, u32[]{:S(2)}, u32[]{:S(2)}) %collective-permute-start.3) | collective-permute-done | bytes 147488 | tf_op jit(solution)/shard_map/ppermute | solution.py:309
  23.6 1.9 %collective-permute-start.5 = (f32[48,384]{1,0:T(8,128)S(1)}, f32[48,384]{1,0:T(8,128)S(1)}, u32[]{:S(2)}, u32[]{:S(2)}) collective-permute-start(f32[48,384]{1,0:T(8,128)S(1)} %shard_map.53.refs_5_.token_ref), channel_id=1, source_target_pairs={{0,1},{1,0},{2,3},{3,2},{4,5},{5,4},{6,7},{7,6},{8,9},{9,8},{10,11... | collective-permute-start | bytes 221192 | tf_op jit(solution)/shard_map/ppermute | solution.py:309
  26.4 1.6 %collective-permute-start.6 = (f32[48,384]{1,0:T(8,128)S(1)}, f32[48,384]{1,0:T(8,128)S(1)}, u32[]{:S(2)}, u32[]{:S(2)}) collective-permute-start(f32[48,384]{1,0:T(8,128)S(1)} %add.26.refs_0_), channel_id=1, source_target_pairs={{0,2},{1,3},{2,0},{3,1},{4,6},{5,7},{6,4},{7,5},{8,10},{9,11},{10,... | collective-permute-start | bytes 221192 | tf_op jit(solution)/shard_map/ppermute | solution.py:309
  28.2 2.7 %collective-permute-done.6.refs_1_ = f32[48,384]{1,0:T(8,128)S(1)} collective-permute-done((f32[48,384]{1,0:T(8,128)S(1)}, f32[48,384]{1,0:T(8,128)S(1)}, u32[]{:S(2)}, u32[]{:S(2)}) %collective-permute-start.6) | collective-permute-done | bytes 73760 | tf_op jit(solution)/shard_map/ppermute | solution.py:309
  31.6 3.0 %collective-permute-start.12 = (f32[48,768]{1,0:T(8,128)S(1)}, f32[48,768]{1,0:T(8,128)S(1)}, u32[]{:S(2)}, u32[]{:S(2)}) collective-permute-start(f32[48,768]{1,0:T(8,128)S(1)} %get-tuple-element.34), channel_id=1, source_target_pairs={{0,16},{1,17},{2,18},{3,19},{4,20},{5,21},{6,22},{7,23},{8,24},{9,... | collective-permute-start | bytes 442376 | tf_op jit(solution)/shard_map/ppermute | solution.py:309
  34.7 1.6 %collective-permute-start.10 = (f32[48,384]{1,0:T(8,128)S(1)}, f32[48,384]{1,0:T(8,128)S(1)}, u32[]{:S(2)}, u32[]{:S(2)}) collective-permute-start(f32[48,384]{1,0:T(8,128)S(1)} %broadcast_select_fusion.3.refs_1_), channel_id=1, source_target_pairs={{0,4},{1,5},{2,6},{3,7},{4,0},{5,1},{6,2},{7,3},{8,12},{9,13},{10,... | collective-permute-start | bytes 221192 | tf_op jit(solution)/shard_map/ppermute | solution.py:309
  36.9 2.2 %collective-permute-done.10.token_ref.refs_7_ = f32[48,384]{1,0:T(8,128)S(1)} collective-permute-done((f32[48,384]{1,0:T(8,128)S(1)}, f32[48,384]{1,0:T(8,128)S(1)}, u32[]{:S(2)}, u32[]{:S(2)}) %collective-permute-start.10) | collective-permute-done | bytes 73760 | tf_op jit(solution)/shard_map/ppermute | solution.py:309
  39.1 2.0 %shard_map.57 = (bf16[1536,384]{1,0:T(8,128)(2,1)S(1)}, bf16[1536,384]{1,0:T(8,128)(2,1)S(1)}) custom-call(f32[48,384]{1,0:T(8,128)S(1)} %collective-permute-done.10.token_ref.refs_7_, f32[4,384,1536]{2,1,0:T(8,128)} %inverse_ref.7), custom_call_target="tpu_custom_call" | custom-call | tf_op jit(solution)/shard_map/pallas_call | solution.py:58
  41.1 4.3 %collective-permute-done.12.refs_2_ = f32[48,768]{1,0:T(8,128)S(1)} collective-permute-done((f32[48,768]{1,0:T(8,128)S(1)}, f32[48,768]{1,0:T(8,128)S(1)}, u32[]{:S(2)}, u32[]{:S(2)}) %collective-permute-start.12) | collective-permute-done | bytes 147488 | tf_op jit(solution)/shard_map/ppermute | solution.py:309
  48.1 2.7 %collective-permute-start.17 = (f32[48,768]{1,0:T(8,128)S(1)}, f32[48,768]{1,0:T(8,128)S(1)}, u32[]{:S(2)}, u32[]{:S(2)}) collective-permute-start(f32[48,768]{1,0:T(8,128)S(1)} %get-tuple-element.39), channel_id=1, source_target_pairs={{0,16},{1,17},{2,18},{3,19},{4,20},{5,21},{6,22},{7,23},{8,24},{9,... | collective-permute-start | bytes 442376 | tf_op jit(solution)/shard_map/ppermute | solution.py:309
  50.8 2.5 %collective-permute-start.14 = (f32[48,384]{1,0:T(8,128)S(1)}, f32[48,384]{1,0:T(8,128)S(1)}, u32[]{:S(2)}, u32[]{:S(2)}) collective-permute-start(f32[48,384]{1,0:T(8,128)S(1)} %add.27.refs_0_), channel_id=1, source_target_pairs={{0,2},{1,3},{2,0},{3,1},{4,6},{5,7},{6,4},{7,5},{8,10},{9,11},{10,... | collective-permute-start | bytes 221192 | tf_op jit(solution)/shard_map/ppermute | solution.py:309
  53.3 3.7 %shard_map.62.token_ref.refs_1_ = f32[48,1536]{1,0:T(8,128)S(1)} custom-call(s32[1]{0:T(128)} %constant.44.clone.1.own_ref, f32[48,384]{1,0:T(8,128)S(1)} %broadcast_select_fusion.7.refs_0_, f32[48,384]{1,0:T(8,128)S(1)} %broadcast_select_fusion.6.refs_1_, f32[48,1536]{1,0:T(8,128)S(1)} %get-tuple-element.29.refs_1_.refs_2_, ...), custom_call_target="tpu_custom_call" | custom-call | tf_op jit(solution)/shard_map/pallas_call | solution.py:58
  57.0 2.0 %shard_map.63 = (bf16[1536,384]{1,0:T(8,128)(2,1)S(1)}, bf16[1536,384]{1,0:T(8,128)(2,1)S(1)}) custom-call(f32[48,1536]{1,0:T(8,128)S(1)} %shard_map.62.token_ref.refs_1_, f32[4,384,1536]{2,1,0:T(8,128)} %inverse_ref.7), custom_call_target="tpu_custom_call" | custom-call | tf_op jit(solution)/shard_map/pallas_call | solution.py:58
  59.0 3.2 %collective-permute-done.17.refs_2_ = f32[48,768]{1,0:T(8,128)S(1)} collective-permute-done((f32[48,768]{1,0:T(8,128)S(1)}, f32[48,768]{1,0:T(8,128)S(1)}, u32[]{:S(2)}, u32[]{:S(2)}) %collective-permute-start.17) | collective-permute-done | bytes 147488 | tf_op jit(solution)/shard_map/ppermute | solution.py:309
  63.4 1.6 %collective-permute-start.15 = (f32[48,384]{1,0:T(8,128)S(1)}, f32[48,384]{1,0:T(8,128)S(1)}, u32[]{:S(2)}, u32[]{:S(2)}) collective-permute-start(f32[48,384]{1,0:T(8,128)S(1)} %broadcast_select_fusion.2), channel_id=1, source_target_pairs={{0,4},{1,5},{2,6},{3,7},{4,0},{5,1},{6,2},{7,3},{8,12},{9,13},{10,... | collective-permute-start | bytes 221192 | tf_op jit(solution)/shard_map/ppermute | solution.py:309
  67.8 2.4 %shard_map.65 = (f32[4608,128]{1,0:T(8,128)S(1)}, f32[4608,128]{1,0:T(8,128)S(1)}) custom-call(f32[48,384]{1,0:T(8,128)S(1)} %shard_map.64.token_ref, f32[4,4608,128]{2,1,0:T(8,128)} %bitcast.23), custom_call_target="tpu_custom_call" | custom-call | tf_op jit(solution)/shard_map/pallas_call | solution.py:58
  73.4 2.1 %collective-permute-start.24 = (f32[48,384]{1,0:T(8,128)S(1)}, f32[48,384]{1,0:T(8,128)S(1)}, u32[]{:S(2)}, u32[]{:S(2)}) collective-permute-start(f32[48,384]{1,0:T(8,128)S(1)} %get-tuple-element.46), channel_id=1, source_target_pairs={{0,8},{1,9},{2,10},{3,11},{4,12},{5,13},{6,14},{7,15},{8,0},{9,1},... | collective-permute-start | bytes 221192 | tf_op jit(solution)/shard_map/ppermute | solution.py:309
  76.3 2.6 %collective-permute-done.22.refs_1_ = f32[48,384]{1,0:T(8,128)S(1)} collective-permute-done((f32[48,384]{1,0:T(8,128)S(1)}, f32[48,384]{1,0:T(8,128)S(1)}, u32[]{:S(2)}, u32[]{:S(2)}) %collective-permute-start.22) | collective-permute-done | bytes 73760 | tf_op jit(solution)/shard_map/ppermute | solution.py:309
  (61 shorter events, 19.3 us)
Async XLA Ops:
  3.1 1.4 %collective-permute-start = (f32[48,384]{1,0:T(8,128)S(1)}, f32[48,384]{1,0:T(8,128)S(1)}, u32[]{:S(2)}, u32[]{:S(2)}) collective-permute-start(f32[48,384]{1,0:T(8,128)S(1)} %get-tuple-element.23), channel_id=1, source_target_pairs={{0,1},{1,0},{2,3},{3,2},{4,5},{5,4},{6,7},{7,6},{8,9},{9,8},{10,11... | collective-permute-start | bytes 221192 | tf_op jit(solution)/shard_map/ppermute | solution.py:309
  5.2 1.6 %collective-permute-start.1 = (f32[48,1536]{1,0:T(8,128)S(1)}, f32[48,1536]{1,0:T(8,128)S(1)}, u32[]{:S(2)}, u32[]{:S(2)}) collective-permute-start(f32[48,1536]{1,0:T(8,128)S(1)} %shard_map.51), channel_id=1, source_target_pairs={{0,1},{1,0},{2,3},{3,2},{4,5},{5,4},{6,7},{7,6},{8,9},{9,8},{10,11... | collective-permute-start | bytes 884744 | tf_op jit(solution)/shard_map/ppermute | solution.py:309
  6.9 21.1 %collective-permute-start.8 = (f32[4,4608,128]{2,1,0:T(8,128)}, f32[4,4608,128]{2,1,0:T(8,128)}, u32[]{:S(2)}, u32[]{:S(2)}) collective-permute-start(f32[4,4608,128]{2,1,0:T(8,128)} %bitcast.17), channel_id=1, source_target_pairs={{0,1},{1,0},{2,3},{3,2},{4,5},{5,4},{6,7},{7,6},{8,9},{9,8},{10,11... | collective-permute-start | bytes 28311560 | tf_op jit(solution)/shard_map/ppermute | solution.py:309
  7.3 15.8 %collective-permute-start.2 = (f32[48,1536]{1,0:T(8,128)S(1)}, f32[48,1536]{1,0:T(8,128)S(1)}, u32[]{:S(2)}, u32[]{:S(2)}) collective-permute-start(f32[48,1536]{1,0:T(8,128)S(1)} %broadcast_select_fusion.refs_0_), channel_id=1, source_target_pairs={{0,8},{1,25},{2,10},{3,27},{4,12},{5,29},{6,14},{7,31},{8,0},{9,17... | collective-permute-start | bytes 884744 | tf_op jit(solution)/shard_map/ppermute | solution.py:309
  10.0 13.0 %collective-permute-start.3 = (f32[48,768]{1,0:T(8,128)S(1)}, f32[48,768]{1,0:T(8,128)S(1)}, u32[]{:S(2)}, u32[]{:S(2)}) collective-permute-start(f32[48,768]{1,0:T(8,128)S(1)} %constant_dynamic-slice_fusion.4), channel_id=1, source_target_pairs={{0,16},{1,17},{2,18},{3,19},{4,20},{5,21},{6,22},{7,23},{8,24},{9,... | collective-permute-start | bytes 442376 | tf_op jit(solution)/shard_map/ppermute | solution.py:309
  12.7 4.4 %collective-permute-start.4 = (f32[48,384]{1,0:T(8,128)S(1)}, f32[48,384]{1,0:T(8,128)S(1)}, u32[]{:S(2)}, u32[]{:S(2)}) collective-permute-start(f32[48,384]{1,0:T(8,128)S(1)} %broadcast_select_fusion.5.refs_0_), channel_id=1, source_target_pairs={{0,2},{1,3},{2,0},{3,1},{4,6},{5,7},{6,4},{7,5},{8,10},{9,11},{10,... | collective-permute-start | bytes 221192 | tf_op jit(solution)/shard_map/ppermute | solution.py:309
  23.6 2.8 %collective-permute-start.5 = (f32[48,384]{1,0:T(8,128)S(1)}, f32[48,384]{1,0:T(8,128)S(1)}, u32[]{:S(2)}, u32[]{:S(2)}) collective-permute-start(f32[48,384]{1,0:T(8,128)S(1)} %shard_map.53.refs_5_.token_ref), channel_id=1, source_target_pairs={{0,1},{1,0},{2,3},{3,2},{4,5},{5,4},{6,7},{7,6},{8,9},{9,8},{10,11... | collective-permute-start | bytes 221192 | tf_op jit(solution)/shard_map/ppermute | solution.py:309
  25.4 2.7 %collective-permute-start.7 = (f32[48,1536]{1,0:T(8,128)S(1)}, f32[48,1536]{1,0:T(8,128)S(1)}, u32[]{:S(2)}, u32[]{:S(2)}) collective-permute-start(f32[48,1536]{1,0:T(8,128)S(1)} %get-tuple-element.29.refs_1_.refs_2_), channel_id=1, source_target_pairs={{0,1},{1,0},{2,3},{3,2},{4,5},{5,4},{6,7},{7,6},{8,9},{9,8},{10,11... | collective-permute-start | bytes 884744 | tf_op jit(solution)/shard_map/ppermute | solution.py:309
  26.4 4.6 %collective-permute-start.6 = (f32[48,384]{1,0:T(8,128)S(1)}, f32[48,384]{1,0:T(8,128)S(1)}, u32[]{:S(2)}, u32[]{:S(2)}) collective-permute-start(f32[48,384]{1,0:T(8,128)S(1)} %add.26.refs_0_), channel_id=1, source_target_pairs={{0,2},{1,3},{2,0},{3,1},{4,6},{5,7},{6,4},{7,5},{8,10},{9,11},{10,... | collective-permute-start | bytes 221192 | tf_op jit(solution)/shard_map/ppermute | solution.py:309
  31.5 13.8 %collective-permute-start.11 = (f32[48,1536]{1,0:T(8,128)S(1)}, f32[48,1536]{1,0:T(8,128)S(1)}, u32[]{:S(2)}, u32[]{:S(2)}) collective-permute-start(f32[48,1536]{1,0:T(8,128)S(1)} %get-tuple-element.31.refs_6_.refs_0_), channel_id=1, source_target_pairs={{0,8},{1,25},{2,10},{3,27},{4,12},{5,29},{6,14},{7,31},{8,0},{9,17... | collective-permute-start | bytes 884744 | tf_op jit(solution)/shard_map/ppermute | solution.py:309
  31.6 13.8 %collective-permute-start.12 = (f32[48,768]{1,0:T(8,128)S(1)}, f32[48,768]{1,0:T(8,128)S(1)}, u32[]{:S(2)}, u32[]{:S(2)}) collective-permute-start(f32[48,768]{1,0:T(8,128)S(1)} %get-tuple-element.34), channel_id=1, source_target_pairs={{0,16},{1,17},{2,18},{3,19},{4,20},{5,21},{6,22},{7,23},{8,24},{9,... | collective-permute-start | bytes 442376 | tf_op jit(solution)/shard_map/ppermute | solution.py:309
  34.7 4.4 %collective-permute-start.10 = (f32[48,384]{1,0:T(8,128)S(1)}, f32[48,384]{1,0:T(8,128)S(1)}, u32[]{:S(2)}, u32[]{:S(2)}) collective-permute-start(f32[48,384]{1,0:T(8,128)S(1)} %broadcast_select_fusion.3.refs_1_), channel_id=1, source_target_pairs={{0,4},{1,5},{2,6},{3,7},{4,0},{5,1},{6,2},{7,3},{8,12},{9,13},{10,... | collective-permute-start | bytes 221192 | tf_op jit(solution)/shard_map/ppermute | solution.py:309
  36.3 4.8 %collective-permute-start.9 = (f32[48,384]{1,0:T(8,128)S(1)}, f32[48,384]{1,0:T(8,128)S(1)}, u32[]{:S(2)}, u32[]{:S(2)}) collective-permute-start(f32[48,384]{1,0:T(8,128)S(1)} %broadcast_select_fusion.4.refs_0_), channel_id=1, source_target_pairs={{0,4},{1,5},{2,6},{3,7},{4,0},{5,1},{6,2},{7,3},{8,12},{9,13},{10,... | collective-permute-start | bytes 221192 | tf_op jit(solution)/shard_map/ppermute | solution.py:309
  47.8 14.3 %collective-permute-start.16 = (f32[48,1536]{1,0:T(8,128)S(1)}, f32[48,1536]{1,0:T(8,128)S(1)}, u32[]{:S(2)}, u32[]{:S(2)}) collective-permute-start(f32[48,1536]{1,0:T(8,128)S(1)} %get-tuple-element.37.refs_6_.refs_0_), channel_id=1, source_target_pairs={{0,8},{1,25},{2,10},{3,27},{4,12},{5,29},{6,14},{7,31},{8,0},{9,17... | collective-permute-start | bytes 884744 | tf_op jit(solution)/shard_map/ppermute | solution.py:309
  48.1 14.0 %collective-permute-start.17 = (f32[48,768]{1,0:T(8,128)S(1)}, f32[48,768]{1,0:T(8,128)S(1)}, u32[]{:S(2)}, u32[]{:S(2)}) collective-permute-start(f32[48,768]{1,0:T(8,128)S(1)} %get-tuple-element.39), channel_id=1, source_target_pairs={{0,16},{1,17},{2,18},{3,19},{4,20},{5,21},{6,22},{7,23},{8,24},{9,... | collective-permute-start | bytes 442376 | tf_op jit(solution)/shard_map/ppermute | solution.py:309
  50.8 8.1 %collective-permute-start.14 = (f32[48,384]{1,0:T(8,128)S(1)}, f32[48,384]{1,0:T(8,128)S(1)}, u32[]{:S(2)}, u32[]{:S(2)}) collective-permute-start(f32[48,384]{1,0:T(8,128)S(1)} %add.27.refs_0_), channel_id=1, source_target_pairs={{0,2},{1,3},{2,0},{3,1},{4,6},{5,7},{6,4},{7,5},{8,10},{9,11},{10,... | collective-permute-start | bytes 221192 | tf_op jit(solution)/shard_map/ppermute | solution.py:309
  62.7 2.3 %collective-permute-start.18 = (f32[48,384]{1,0:T(8,128)S(1)}, f32[48,384]{1,0:T(8,128)S(1)}, u32[]{:S(2)}, u32[]{:S(2)}) collective-permute-start(f32[48,384]{1,0:T(8,128)S(1)} %shard_map.64.token_ref), channel_id=1, source_target_pairs={{0,1},{1,0},{2,3},{3,2},{4,5},{5,4},{6,7},{7,6},{8,9},{9,8},{10,11... | collective-permute-start | bytes 221192 | tf_op jit(solution)/shard_map/ppermute | solution.py:309
  63.4 4.4 %collective-permute-start.15 = (f32[48,384]{1,0:T(8,128)S(1)}, f32[48,384]{1,0:T(8,128)S(1)}, u32[]{:S(2)}, u32[]{:S(2)}) collective-permute-start(f32[48,384]{1,0:T(8,128)S(1)} %broadcast_select_fusion.2), channel_id=1, source_target_pairs={{0,4},{1,5},{2,6},{3,7},{4,0},{5,1},{6,2},{7,3},{8,12},{9,13},{10,... | collective-permute-start | bytes 221192 | tf_op jit(solution)/shard_map/ppermute | solution.py:309
  65.0 6.2 %collective-permute-start.19 = (f32[48,384]{1,0:T(8,128)S(1)}, f32[48,384]{1,0:T(8,128)S(1)}, u32[]{:S(2)}, u32[]{:S(2)}) collective-permute-start(f32[48,384]{1,0:T(8,128)S(1)} %add.28), channel_id=1, source_target_pairs={{2,0},{3,1},{10,8},{11,9},{18,16},{19,17},{26,24},{27,25}} | collective-permute-start | bytes 221192 | tf_op jit(solution)/shard_map/ppermute | solution.py:309
  66.3 5.0 %collective-permute-start.20 = (f32[48,384]{1,0:T(8,128)S(1)}, f32[48,384]{1,0:T(8,128)S(1)}, u32[]{:S(2)}, u32[]{:S(2)}) collective-permute-start(f32[48,384]{1,0:T(8,128)S(1)} %add.28), channel_id=1, source_target_pairs={{2,6},{3,7},{10,14},{11,15},{18,22},{19,23},{26,30},{27,31}} | collective-permute-start | bytes 221192 | tf_op jit(solution)/shard_map/ppermute | solution.py:309
  66.9 4.3 %collective-permute-start.21 = (f32[48,384]{1,0:T(8,128)S(1)}, f32[48,384]{1,0:T(8,128)S(1)}, u32[]{:S(2)}, u32[]{:S(2)}) collective-permute-start(f32[48,384]{1,0:T(8,128)S(1)} %add.28), channel_id=1, source_target_pairs={{2,4},{3,5},{10,12},{11,13},{18,20},{19,21},{26,28},{27,29}} | collective-permute-start | bytes 221192 | tf_op jit(solution)/shard_map/ppermute | solution.py:309
  71.9 7.0 %collective-permute-start.22 = (f32[48,384]{1,0:T(8,128)S(1)}, f32[48,384]{1,0:T(8,128)S(1)}, u32[]{:S(2)}, u32[]{:S(2)}) collective-permute-start(f32[48,384]{1,0:T(8,128)S(1)} %get-tuple-element.48), channel_id=1, source_target_pairs={{0,16},{1,17},{2,18},{3,19},{4,20},{5,21},{6,22},{7,23},{8,24},{9,... | collective-permute-start | bytes 221192 | tf_op jit(solution)/shard_map/ppermute | solution.py:309
  72.0 7.0 %collective-permute-start.23 = (f32[48,384]{1,0:T(8,128)S(1)}, f32[48,384]{1,0:T(8,128)S(1)}, u32[]{:S(2)}, u32[]{:S(2)}) collective-permute-start(f32[48,384]{1,0:T(8,128)S(1)} %get-tuple-element.47), channel_id=1, source_target_pairs={{0,24},{1,25},{2,26},{3,27},{4,28},{5,29},{6,30},{7,31},{8,16},{9,... | collective-permute-start | bytes 221192 | tf_op jit(solution)/shard_map/ppermute | solution.py:309
  73.4 6.4 %collective-permute-start.24 = (f32[48,384]{1,0:T(8,128)S(1)}, f32[48,384]{1,0:T(8,128)S(1)}, u32[]{:S(2)}, u32[]{:S(2)}) collective-permute-start(f32[48,384]{1,0:T(8,128)S(1)} %get-tuple-element.46), channel_id=1, source_target_pairs={{0,8},{1,9},{2,10},{3,11},{4,12},{5,13},{6,14},{7,15},{8,0},{9,1},... | collective-permute-start | bytes 221192 | tf_op jit(solution)/shard_map/ppermute | solution.py:309
  (1 other events, 1.3 us)
